TPU v7x, 32 devices: a whole 2x2x4 slice. The times are simulated.
32 devices in a mesh: row: 8 (over z, x), col: 4 (over y, core).
Axes of the slice: x: 2, y: 2, z: 4, core: 2. Of those that a mesh axis runs over, the one named last changes fastest.
Arguments:
- tokens: float32 [2560, 2048], P('row'), may hold values from -8 to 8
- cotangent: float32 [2560, 2048], P('row'), may hold values from -8 to 8
- w_query: float32 [2048, 2048], P('row', 'col'), may hold values from -0.125 to 0.125
- w_key: float32 [2048, 2048], P('row', 'col'), may hold values from -0.125 to 0.125
- w_value: float32 [2048, 2048], P('row', 'col'), may hold values from -0.125 to 0.125
- w_output: float32 [2048, 2048], P('row', 'col'), may hold values from -0.125 to 0.125
- gain_attn: float32 [2048], P('row'), may hold values from 0.1 to 1.9
- lambda_query_first: float32 [128], P('row'), may hold values from -1.75 to 1.75
- lambda_key_first: float32 [128], P('row'), may hold values from -1.75 to 1.75
- lambda_query_second: float32 [128], P('row'), may hold values from -1.75 to 1.75
- lambda_key_second: float32 [128], P('row'), may hold values from -1.75 to 1.75
- gain_head: float32 [256], P('row'), may hold values from 0.1 to 1.9
- w_gate: float32 [2048, 5632], P('row', 'col'), may hold values from -0.125 to 0.125
- w_up: float32 [2048, 5632], P('row', 'col'), may hold values from -0.125 to 0.125
- w_down: float32 [2048, 5632], P('row', 'col'), may hold values from -0.078125 to 0.078125
- gain_ffn: float32 [2048], P('row'), may hold values from 0.1 to 1.9
- tau: float32 [1], replicated, may hold values from 1.5 to 3
- parent_slot: int32 [40], replicated, may hold values from 0 to 39, as said below
- depth: int32 [2560], P('row'), may hold values from 0 to 639, as said below
Outputs:
- output: float32 [2560, 2048], P('row')
- grad_tokens: float32 [2560, 2048], P('row')
- grad_query: float32 [2048, 2048], P('row', 'col')
- grad_key: float32 [2048, 2048], P('row', 'col')
- grad_value: float32 [2048, 2048], P('row', 'col')
- grad_output: float32 [2048, 2048], P('row', 'col')
- grad_gain_attn: float32 [2048], P('row')
- grad_mix: float32 [1], replicated
- grad_gain_head: float32 [256], P('row')
- grad_gate: float32 [2048, 5632], P('row', 'col')
- grad_up: float32 [2048, 5632], P('row', 'col')
- grad_down: float32 [2048, 5632], P('row', 'col')
- grad_gain_ffn: float32 [2048], P('row')
- maxima: float32 [16], replicated
- clipped_query: float32 [2048, 2048], P('row', 'col')
- clipped_key: float32 [2048, 2048], P('row', 'col')
Inputs may be any that keep to these rules, and one draw needn't show every extreme that they name: `parent_slot`: every tree has 8 trunk segments in a chain, 4 branch segments whose parent is the last trunk segment and 2 leaf segments on each branch; a tree's first trunk segment is its own parent; the slots of all trees are spread over the devices of row, 5 slots on each. depth[t] = 64 times the number of strict ancestors of t's slot plus t's offset within its slot.
All inputs are finite; a program needn't handle non-finite values.
Results may differ from a plain program's by a relative error of at most 0.0003.
Values sent between devices are 32-bit elements; how exact they have to be, the bound alone decides.
No kernel may reach another device: no remote copies, remote signals or barrier semaphores. Data moves between devices by JAX's collectives and lax.ppermute only.
A program may use at most 256 MiB of HBM per device.

v0:
```python
import math

import jax
import jax.numpy as jnp
from jax import lax
from jax.sharding import PartitionSpec as P

HEADS = 8
HD = 128
VD = 256
SEG = 64
SEGS_DEV = 5
TRUNK_SEGS = 8


epsilon = 1e-05
lambda_init = 0.2
rope_log_base = 9.210340371976184
highest = lax.Precision.HIGHEST


def rms_scale(values, gain_vec):
    return (
        values * lax.rsqrt(jnp.mean(values * values, axis=-1, keepdims=True) + epsilon) * gain_vec
    )


def rotate(values, positions):
    half_dim = values.shape[-1] // 2
    frequency = jnp.exp(-rope_log_base * jnp.arange(half_dim, dtype=jnp.float32) / half_dim)
    angles = positions.astype(jnp.float32)[:, None] * frequency[None, :]
    cosine_part = jnp.cos(angles)[:, None, None, :]
    sine_part = jnp.sin(angles)[:, None, None, :]
    lead_half = values[..., :half_dim]
    tail_half = values[..., half_dim:]
    return jnp.concatenate(
        [
            lead_half * cosine_part - tail_half * sine_part,
            tail_half * cosine_part + lead_half * sine_part,
        ],
        axis=-1,
    )


def shards(
    tokens,
    cotangent,
    w_query,
    w_key,
    w_value,
    w_output,
    gain_attn,
    lambda_query_first,
    lambda_key_first,
    lambda_query_second,
    lambda_key_second,
    gain_head,
    w_gate,
    w_up,
    w_down,
    gain_ffn,
    tau,
    parent_slot,
    depth,
):
    row_index = lax.axis_index("row")
    col_index = lax.axis_index("col")
    local_rows = tokens.shape[0]
    (
        query_full,
        key_full,
        value_full,
        output_full,
        attn_gain,
        query_first,
        key_first,
        query_second,
        key_second,
        head_gain,
    ) = (
        lax.all_gather(w_query, "row", axis=0, tiled=True),
        lax.all_gather(w_key, "row", axis=0, tiled=True),
        lax.all_gather(w_value, "row", axis=0, tiled=True),
        lax.all_gather(w_output, "row", axis=0, tiled=True),
        lax.all_gather(gain_attn, "row", axis=0, tiled=True),
        lax.all_gather(lambda_query_first, "row", axis=0, tiled=True),
        lax.all_gather(lambda_key_first, "row", axis=0, tiled=True),
        lax.all_gather(lambda_query_second, "row", axis=0, tiled=True),
        lax.all_gather(lambda_key_second, "row", axis=0, tiled=True),
        lax.all_gather(gain_head, "row", axis=0, tiled=True),
    )
    local_heads = query_full.shape[1] // (2 * HD)
    mix_value = (
        jnp.exp(jnp.sum(query_first * key_first))
        - jnp.exp(jnp.sum(query_second * key_second))
        + lambda_init
    )
    mix_vec = jnp.reshape(mix_value, (1,))
    slot_total = parent_slot.shape[0]
    slot_ids = jnp.arange(slot_total, dtype=jnp.int32)
    own_slots = row_index * SEGS_DEV + jnp.arange(SEGS_DEV, dtype=jnp.int32)

    def climb(climb_step, state_now):
        current, marked = state_now
        picked = current[:, None] == slot_ids[None, :]
        current = jnp.sum(jnp.where(picked, parent_slot[None, :], 0), axis=1)
        marked = marked | (current[:, None] == slot_ids[None, :])
        return (current, marked)

    current, marked = lax.fori_loop(
        0, TRUNK_SEGS + 2, climb, (own_slots, jnp.zeros((SEGS_DEV, slot_total), dtype=bool))
    )
    strict = (marked & (own_slots[:, None] != slot_ids[None, :])).astype(jnp.float32)
    local_slot = jnp.arange(local_rows, dtype=jnp.int32) // SEG
    row_onehot = (local_slot[:, None] == jnp.arange(SEGS_DEV, dtype=jnp.int32)[None, :]).astype(
        jnp.float32
    )
    path_rows = jnp.dot(row_onehot, strict, precision=highest)
    row_global = row_index * local_rows + jnp.arange(local_rows, dtype=jnp.int32)
    row_slot_global = row_global // SEG

    def allowed_block(key_start, key_count):
        key_ids = key_start + jnp.arange(key_count, dtype=jnp.int32)
        key_slot = key_ids // SEG
        key_onehot = (key_slot[:, None] == slot_ids[None, :]).astype(jnp.float32)
        from_path = jnp.dot(path_rows, key_onehot.T, precision=highest) > 0.5
        same_slot = (row_slot_global[:, None] == key_slot[None, :]) & (
            key_ids[None, :] <= row_global[:, None]
        )
        return (from_path | same_slot)[None, None]

    normed_attn, attn_norm_back = jax.vjp(rms_scale, tokens, attn_gain)

    def project(normed, query_mat, key_mat, value_mat):
        queries = jnp.dot(normed, query_mat, precision=highest).reshape(
            local_rows, local_heads, 2, HD
        )
        key_rows = jnp.dot(normed, key_mat, precision=highest).reshape(
            local_rows, local_heads, 2, HD
        )
        key_flat = rotate(key_rows, depth).reshape(local_rows, local_heads * 2 * HD)
        value_flat = jnp.dot(normed, value_mat, precision=highest)
        return (rotate(queries, depth), key_flat, value_flat)

    (queries, key_flat, value_flat), project_back = jax.vjp(
        project, normed_attn, query_full, key_full, value_full
    )
    key_all, value_all = (
        lax.all_gather(key_flat, "row", axis=0, tiled=True),
        lax.all_gather(value_flat, "row", axis=0, tiled=True),
    )
    key_total = key_all.shape[0]
    key_block = math.gcd(key_total, 512)
    block_count = key_total // key_block
    logit_scale = 1.0 / math.sqrt(HD)
    block_ids = jnp.arange(block_count, dtype=jnp.int32)

    def forward_step(state_now, inputs):
        key_blk, value_blk, blk_index = inputs
        allowed = allowed_block(blk_index * key_block, key_block)

        def forward_visit(state_in):
            peak_logit, row_total, weighted = state_in
            scores = (
                jnp.einsum("thjd,khjd->jhtk", queries, key_blk, precision=highest) * logit_scale
            )
            masked = jnp.where(allowed, scores, -1e30)
            new_peak = jnp.maximum(peak_logit, jnp.max(masked, axis=-1))
            rescale = jnp.exp(peak_logit - new_peak)
            weights = jnp.where(allowed, jnp.exp(masked - new_peak[..., None]), 0.0)
            row_total = row_total * rescale + jnp.sum(weights, axis=-1)
            weighted = weighted * rescale[..., None] + jnp.einsum(
                "jhtk,khv->jhtv", weights, value_blk, precision=highest
            )
            return (new_peak, row_total, weighted)

        def forward_skip(state_in):
            return state_in

        return (lax.cond(jnp.any(allowed), forward_visit, forward_skip, state_now), None)

    init_state = (
        jnp.full((2, local_heads, local_rows), -1e30, jnp.float32),
        jnp.zeros((2, local_heads, local_rows), jnp.float32),
        jnp.zeros((2, local_heads, local_rows, VD), jnp.float32),
    )
    (peak_logit, row_total, weighted), unused_out = lax.scan(
        forward_step,
        init_state,
        (
            key_all.reshape(block_count, key_block, local_heads, 2, HD),
            value_all.reshape(block_count, key_block, local_heads, VD),
            block_ids,
        ),
    )
    mixed = weighted / row_total[..., None]
    log_total = peak_logit + jnp.log(row_total)
    local_peaks = jnp.max(peak_logit, axis=-1).T.reshape(2 * local_heads)
    peak_table = lax.dynamic_update_slice(
        jnp.full((2 * HEADS,), -1e30, jnp.float32), local_peaks, (col_index * 2 * local_heads,)
    )
    maxima = lax.pmax(peak_table, ("row", "col"))

    def heads_out(mixed_in, mix_in, gain_vec, output_mat):
        contrast = mixed_in[0] - mix_in[0] * mixed_in[1]
        headed = rms_scale(contrast, gain_vec) * (1.0 - lambda_init)
        joined = jnp.transpose(headed, (1, 0, 2)).reshape(local_rows, local_heads * VD)
        return jnp.dot(joined, output_mat.T, precision=highest)

    branch_part, heads_back = jax.vjp(heads_out, mixed, mix_vec, head_gain, output_full)
    residual = tokens + lax.psum(branch_part, "col")
    gate_full, up_full, down_full, ffn_gain = (
        lax.all_gather(w_gate, "row", axis=0, tiled=True),
        lax.all_gather(w_up, "row", axis=0, tiled=True),
        lax.all_gather(w_down, "row", axis=0, tiled=True),
        lax.all_gather(gain_ffn, "row", axis=0, tiled=True),
    )
    normed_ffn, ffn_norm_back = jax.vjp(rms_scale, residual, ffn_gain)

    def feed(normed, gate_mat, up_mat, down_mat):
        gating = jnp.dot(normed, gate_mat, precision=highest)
        up_proj = jnp.dot(normed, up_mat, precision=highest)
        return jnp.dot(jax.nn.silu(gating) * up_proj, down_mat.T, precision=highest)

    ffn_part, feed_back = jax.vjp(feed, normed_ffn, gate_full, up_full, down_full)
    output = residual + lax.psum(ffn_part, "col")
    grad_normed_part, grad_gate, grad_up, grad_down = feed_back(cotangent)
    grad_normed = lax.psum(grad_normed_part, "col")
    grad_from_norm, grad_ffn_gain = ffn_norm_back(grad_normed)
    grad_residual = cotangent + grad_from_norm
    grad_gate, grad_up, grad_down, grad_ffn_gain = (
        lax.psum_scatter(grad_gate, "row", scatter_dimension=0, tiled=True),
        lax.psum_scatter(grad_up, "row", scatter_dimension=0, tiled=True),
        lax.psum_scatter(grad_down, "row", scatter_dimension=0, tiled=True),
        lax.psum_scatter(grad_ffn_gain, "row", scatter_dimension=0, tiled=True),
    )
    grad_mixed, grad_mix_part, grad_head_gain, grad_output = heads_back(grad_residual)
    key_back, value_back = (key_all, value_all)
    row_inner = jnp.sum(grad_mixed * mixed, axis=-1)

    def backward_step(grad_queries, inputs):
        key_blk, value_blk, blk_index = inputs
        allowed = allowed_block(blk_index * key_block, key_block)

        def backward_visit(grad_in):
            scores = (
                jnp.einsum("thjd,khjd->jhtk", queries, key_blk, precision=highest) * logit_scale
            )
            weights = jnp.where(
                allowed, jnp.exp(jnp.where(allowed, scores, -1e30) - log_total[..., None]), 0.0
            )
            grad_weights = jnp.einsum("jhtv,khv->jhtk", grad_mixed, value_blk, precision=highest)
            grad_scores = weights * (grad_weights - row_inner[..., None])
            grad_out = (
                grad_in
                + jnp.einsum("jhtk,khjd->thjd", grad_scores, key_blk, precision=highest)
                * logit_scale
            )
            grad_key_blk = (
                jnp.einsum("jhtk,thjd->khjd", grad_scores, queries, precision=highest) * logit_scale
            )
            grad_value_blk = jnp.einsum("jhtk,jhtv->khv", weights, grad_mixed, precision=highest)
            return (grad_out, (grad_key_blk, grad_value_blk))

        def backward_skip(grad_in):
            return (grad_in, (jnp.zeros_like(key_blk), jnp.zeros_like(value_blk)))

        return lax.cond(jnp.any(allowed), backward_visit, backward_skip, grad_queries)

    grad_queries, (grad_key_blocks, grad_value_blocks) = lax.scan(
        backward_step,
        jnp.zeros_like(queries),
        (
            key_back.reshape(block_count, key_block, local_heads, 2, HD),
            value_back.reshape(block_count, key_block, local_heads, VD),
            block_ids,
        ),
    )
    grad_keys, grad_values = (
        lax.psum_scatter(
            grad_key_blocks.reshape(key_total, local_heads * 2 * HD),
            "row",
            scatter_dimension=0,
            tiled=True,
        ),
        lax.psum_scatter(
            grad_value_blocks.reshape(key_total, local_heads * VD),
            "row",
            scatter_dimension=0,
            tiled=True,
        ),
    )
    grad_attn_part, grad_query, grad_key, grad_value = project_back(
        (grad_queries, grad_keys, grad_values)
    )
    grad_attn_normed, grad_mix_heads, grad_head_gain = lax.psum(
        (grad_attn_part, grad_mix_part, grad_head_gain), "col"
    )
    grad_mix = lax.psum(grad_mix_heads, "row")
    grad_tok_norm, grad_attn_gain = attn_norm_back(grad_attn_normed)
    grad_tokens = grad_residual + grad_tok_norm
    grad_query, grad_key, grad_value, grad_output, grad_attn_gain, grad_head_gain = (
        lax.psum_scatter(grad_query, "row", scatter_dimension=0, tiled=True),
        lax.psum_scatter(grad_key, "row", scatter_dimension=0, tiled=True),
        lax.psum_scatter(grad_value, "row", scatter_dimension=0, tiled=True),
        lax.psum_scatter(grad_output, "row", scatter_dimension=0, tiled=True),
        lax.psum_scatter(grad_attn_gain, "row", scatter_dimension=0, tiled=True),
        lax.psum_scatter(grad_head_gain, "row", scatter_dimension=0, tiled=True),
    )
    factor = tau[0] / jnp.maximum(maxima, tau[0])
    local_factor = lax.dynamic_slice_in_dim(factor, col_index * 2 * local_heads, 2 * local_heads)
    root_factor = jnp.sqrt(local_factor).reshape(1, local_heads, 2, 1)
    weight_rows = w_query.shape[0]
    clipped_query = (w_query.reshape(weight_rows, local_heads, 2, HD) * root_factor).reshape(
        w_query.shape
    )
    clipped_key = (w_key.reshape(weight_rows, local_heads, 2, HD) * root_factor).reshape(
        w_key.shape
    )
    return (
        output,
        grad_tokens,
        grad_query,
        grad_key,
        grad_value,
        grad_output,
        grad_attn_gain,
        grad_mix,
        grad_head_gain,
        grad_gate,
        grad_up,
        grad_down,
        grad_ffn_gain,
        maxima,
        clipped_query,
        clipped_key,
    )


def solution(mesh):
    placed = (
        P("row", None),
        P("row", None),
        P("row", "col"),
        P("row", "col"),
        P("row", "col"),
        P("row", "col"),
        P("row"),
        P("row"),
        P("row"),
        P("row"),
        P("row"),
        P("row"),
        P("row", "col"),
        P("row", "col"),
        P("row", "col"),
        P("row"),
        P(),
        P(),
        P("row"),
    )
    return jax.shard_map(
        shards,
        mesh=mesh,
        in_specs=placed,
        out_specs=(
            P("row", None),
            P("row", None),
            P("row", "col"),
            P("row", "col"),
            P("row", "col"),
            P("row", "col"),
            P("row"),
            P(),
            P("row"),
            P("row", "col"),
            P("row", "col"),
            P("row", "col"),
            P("row"),
            P(),
            P("row", "col"),
            P("row", "col"),
        ),
        check_vma=False,
    )
```

profile of v0, /device:TPU:0, one launch (start us, length us, event | category | flops | bytes accessed | tf_op | source)
XLA Modules:
  0.0 2634.1 jit_solution(5221771867914664438)
XLA Ops:
  9.5 22.6 all-gather
  34.7 51.6 %all-gather.18.cloned.1.call-done = f32[2048,512]{1,0:T(8,128)} async-done(((f32[256,512]{1,0:T(8,128)}), f32[2048,512]{1,0:T(8,128)}) %all-gather.18.cloned.1.call-update) | async-done | bytes 4194320 | tf_op jit(solution)/shard_map/all_gather | solution.py:83
  95.6 64.5 %all-gather.16.cloned.1.call-done = f32[2048,512]{1,0:T(8,128)} async-done(((f32[256,512]{1,0:T(8,128)}), f32[2048,512]{1,0:T(8,128)}) %all-gather.16.cloned.1.call-update) | async-done | bytes 4194320 | tf_op jit(solution)/shard_map/all_gather | solution.py:81
  169.3 64.6 %all-gather.12.cloned.1.call-done = f32[2048,512]{1,0:T(8,128)} async-done(((f32[256,512]{1,0:T(8,128)}), f32[2048,512]{1,0:T(8,128)}) %all-gather.12.cloned.1.call-update) | async-done | bytes 4194320 | tf_op jit(solution)/shard_map/all_gather | solution.py:82
  281.1 40.2 %all-gather.20.cloned.1.call-done = f32[2560,512]{1,0:T(8,128)} async-done(((f32[320,512]{1,0:T(8,128)}), f32[2560,512]{1,0:T(8,128)}) %all-gather.20.cloned.1.call-update) | async-done | bytes 5242896 | tf_op jit(solution)/shard_map/all_gather | solution.py:150
  334.5 73.9 %all-gather.14.cloned.1.call-done = f32[2560,512]{1,0:T(8,128)} async-done(((f32[320,512]{1,0:T(8,128)}), f32[2560,512]{1,0:T(8,128)}) %all-gather.14.cloned.1.call-update) | async-done | bytes 5242896 | tf_op jit(solution)/shard_map/all_gather | solution.py:149
  422.8 71.3 %while.54 = (s32[]{:T(128)}, f32[2,2,320]{2,1,0:T(2,128)S(1)}, f32[2,2,320]{2,1,0:T(2,128)S(1)}, f32[2,2,320,256]{3,2,0,1:T(8,128)}, s32[5]{0:T(128)S(1)}, /*ind...) while((s32[]{:T(128)}, f32[2,2,320]{2,1,0:T(2,128)S(1)}, ...), condition=%wide.region_10.11_spmd.clone.clone, body=%wide.region_4.10_spmd.clone.clone.sunk | while | flops 3105459712 | bytes 16504091 | solution.py:187
  525.2 38.6 %all-reduce.21.cloned.1.call-done = f32[320,2048]{1,0:T(8,128)} async-done(((f32[320,2048]{1,0:T(8,128)}), f32[320,2048]{1,0:T(8,128)}) %all-reduce.21.cloned.1.call-update) | async-done | bytes 2621456 | tf_op jit(solution)/shard_map/psum | solution.py:211
  567.4 162.4 %all-gather.24.cloned.1.call-done = f32[2048,1408]{1,0:T(8,128)} async-done(((f32[256,1408]{1,0:T(8,128)}), f32[2048,1408]{1,0:T(8,128)}) %all-gather.24.cloned.1.call-update) | async-done | bytes 11534352 | tf_op jit(solution)/shard_map/all_gather | solution.py:213
  747.7 146.2 %all-gather.26.cloned.1.call-done = f32[2048,1408]{1,0:T(8,128)} async-done(((f32[256,1408]{1,0:T(8,128)}), f32[2048,1408]{1,0:T(8,128)}) %all-gather.26.cloned.1.call-update) | async-done | bytes 11534352 | tf_op jit(solution)/shard_map/all_gather | solution.py:214
  911.6 146.2 %all-gather.28.cloned.1.call-done = f32[2048,1408]{1,0:T(8,128)} async-done(((f32[256,1408]{1,0:T(8,128)}), f32[2048,1408]{1,0:T(8,128)}) %all-gather.28.cloned.1.call-update) | async-done | bytes 11534352 | tf_op jit(solution)/shard_map/all_gather | solution.py:215
  1108.2 56.8 %all-reduce.23.cloned.1.call-done = f32[320,2048]{1,0:T(8,128)} async-done(((f32[320,2048]{1,0:T(8,128)}), f32[320,2048]{1,0:T(8,128)}) %all-reduce.23.cloned.1.call-update) | async-done | bytes 2621456 | tf_op jit(solution)/shard_map/psum | solution.py:228
  1181.4 150.6 %while.55 = (s32[]{:T(128)}, f32[320,2,2,128]{3,0,2,1:T(8,128)}, f32[5,512,2,2,128]{4,3,2,1,0:T(2,128)}, f32[5,512,2,256]{3,2,1,0:T(2,128)}, s32[5]{0:T(128)S(1)...) while((s32[]{:T(128)}, f32[320,2,2,128]{3,0,2,1:T(8,128)}, ...), condition=%wide.region_25.26_spmd.clone.clone, body=%wide.region_21.25_spmd.clone.clone.sunk | while | flops 7133234176 | bytes 41468784 | solution.py:270
  1185.9 22.3 conditional.9
  1215.9 22.3 conditional.9
  1245.9 22.3 conditional.9
  1275.9 22.3 conditional.9
  1305.9 22.3 conditional.9
  1365.6 77.2 %reduce-scatter.12.cloned.1.call-done = f32[320,512]{1,0:T(8,128)} async-done(((f32[2560,512]{1,0:T(8,128)}), f32[320,512]{1,0:T(8,128)}) %reduce-scatter.12.cloned.1.call-update) | async-done | bytes 655376 | tf_op jit(solution)/shard_map/reduce_scatter | solution.py:280
  1454.7 94.1 %reduce-scatter.10.cloned.1.call-done = f32[320,512]{1,0:T(8,128)} async-done(((f32[2560,512]{1,0:T(8,128)}), f32[320,512]{1,0:T(8,128)}) %reduce-scatter.10.cloned.1.call-update) | async-done | bytes 655376 | tf_op jit(solution)/shard_map/reduce_scatter | solution.py:286
  1566.5 24.1 convolution_bitcast_fusion
  1630.2 25.3 fusion.97
  1655.5 25.2 fusion.96
  1683.1 43.3 %pmax.7 = f32[16]{0:T(128)S(1)} all-reduce(f32[16]{0:T(128)S(1)} %dynamic_update_slice.17), channel_id=1, replica_groups=mesh['row'=8,'col'=4] {'row','col'}, use_global_device_ids=true, to_apply=%region_48.49 | all-reduce | flops 16 | bytes 128 | tf_op jit(solution)/shard_map/pmax | solution.py:202
  1741.1 41.3 %all-reduce.14 = (f32[2048]{0:T(1024)S(1)}, f32[1]{0:T(128)}, f32[256]{0:T(256)S(1)}, f32[2048]{0:T(1024)S(1)}) all-reduce(f32[2048]{0:T(1024)S(1)} %get-tuple-element.845, f32[1]{0:T(128)} %psum.53, f32[256]{0:T(256)S(1)} %get-tuple-element.847, f32[2048]{0:T(1024)S(1)} %get-tuple-element.843), channel_id=8, replica_groups=mesh['row'=8,'col'=4] {'row'}, use_global_device_ids=true, to_apply=%region_35.36.clone | all-reduce | flops 4353 | bytes 34824
  1794.9 72.0 %reduce-scatter.26.cloned.1.call-done = f32[256,1408]{0,1:T(8,128)} async-done(((f32[2048,1408]{0,1:T(8,128)}), f32[256,1408]{0,1:T(8,128)}) %reduce-scatter.26.cloned.1.call-update) | async-done | bytes 1441808 | tf_op jit(solution)/shard_map/reduce_scatter | solution.py:234
  1869.8 88.2 %reduce-scatter.20.cloned.1.call-done = f32[256,512]{1,0:T(8,128)} async-done(((f32[2048,512]{1,0:T(8,128)}), f32[256,512]{1,0:T(8,128)}) %reduce-scatter.20.cloned.1.call-update) | async-done | bytes 524304 | tf_op jit(solution)/shard_map/reduce_scatter | solution.py:306
  1958.0 92.2 %reduce-scatter.18.cloned.1.call-done = f32[256,512]{1,0:T(8,128)} async-done(((f32[2048,512]{1,0:T(8,128)}), f32[256,512]{1,0:T(8,128)}) %reduce-scatter.18.cloned.1.call-update) | async-done | bytes 524304 | tf_op jit(solution)/shard_map/reduce_scatter | solution.py:305
  2050.2 91.8 %reduce-scatter.14.cloned.1.call-done = f32[256,512]{1,0:T(8,128)} async-done(((f32[2048,512]{1,0:T(8,128)}), f32[256,512]{1,0:T(8,128)}) %reduce-scatter.14.cloned.1.call-update) | async-done | bytes 524304 | tf_op jit(solution)/shard_map/reduce_scatter | solution.py:303
  2142.0 92.3 %reduce-scatter.16.cloned.1.call-done = f32[256,512]{1,0:T(8,128)} async-done(((f32[2048,512]{1,0:T(8,128)}), f32[256,512]{1,0:T(8,128)}) %reduce-scatter.16.cloned.1.call-update) | async-done | bytes 524304 | tf_op jit(solution)/shard_map/reduce_scatter | solution.py:304
  2234.3 196.5 %reduce-scatter.22.cloned.1.call-done = f32[256,1408]{1,0:T(8,128)} async-done(((f32[2048,1408]{1,0:T(8,128)}), f32[256,1408]{1,0:T(8,128)}) %reduce-scatter.22.cloned.1.call-update) | async-done | bytes 1441808 | tf_op jit(solution)/shard_map/reduce_scatter | solution.py:232
  2430.8 196.0 %reduce-scatter.24.cloned.1.call-done = f32[256,1408]{1,0:T(8,128)} async-done(((f32[2048,1408]{1,0:T(8,128)}), f32[256,1408]{1,0:T(8,128)}) %reduce-scatter.24.cloned.1.call-update) | async-done | bytes 1441808 | tf_op jit(solution)/shard_map/reduce_scatter | solution.py:233
  (420 shorter events, 625.1 us)
Async XLA Ops:
  7.2 79.1 %copy-start = (f32[320,2048]{1,0:T(8,128)S(1)}, f32[320,2048]{1,0:T(8,128)}, u32[]{:S(2)}) copy-start(f32[320,2048]{1,0:T(8,128)} %param.29) | copy-start | bytes 7864324
  7.2 79.1 %all-gather.18.cloned.1.call-start = ((), (), s32[]{:S(2)}) async-start(), calls=%async_computation.12 | async-start | bytes 4718592 | tf_op jit(solution)/shard_map/all_gather | solution.py:83
  7.9 152.2 %all-gather.16.cloned.1.call-start = ((), (), s32[]{:S(2)}) async-start(), calls=%async_computation.11 | async-start | bytes 4718592 | tf_op jit(solution)/shard_map/all_gather | solution.py:81
  8.7 225.3 %all-gather.12.cloned.1.call-start = ((), (), s32[]{:S(2)}) async-start(), calls=%async_computation.9 | async-start | bytes 4718592 | tf_op jit(solution)/shard_map/all_gather | solution.py:82
  9.4 311.9 %all-gather.20.cloned.1.call-start = ((), (), s32[]{:S(2)}) async-start(), calls=%async_computation.13 | async-start | bytes 5898240 | tf_op jit(solution)/shard_map/all_gather | solution.py:150
  32.1 201.9 %copy-start.30 = (f32[8,1,256]{2,1,0:T(1,128)}, f32[8,1,256]{2,1,0:T(1,128)S(1)}, u32[]{:S(2)}) copy-start(f32[8,1,256]{2,1,0:T(1,128)S(1)} %all-gather) | copy-start | bytes 24580
  34.7 199.2 %copy-start.32 = (f32[320]{0:T(512)}, f32[320]{0:T(512)S(1)}, u32[]{:S(2)}) copy-start(f32[320]{0:T(512)S(1)} %fusion.128) | copy-start | bytes 3844
  94.0 314.4 %all-gather.14.cloned.1.call-start = ((), (), s32[]{:S(2)}) async-start(), calls=%async_computation.10 | async-start | bytes 5898240 | tf_op jit(solution)/shard_map/all_gather | solution.py:149
  95.6 148.4 %copy-start.28 = (f32[320,64]{1,0:T(8,128)}, f32[320,64]{1,0:T(8,128)S(1)}, u32[]{:S(2)}) copy-start(f32[320,64]{1,0:T(8,128)S(1)} %get-tuple-element.954) | copy-start | bytes 245764
  247.7 26.8 %copy-start.44 = (s32[40]{0:T(128)S(1)}, s32[40]{0:T(128)}, u32[]{:S(2)}) copy-start(s32[40]{0:T(128)} %param.46) | copy-start | bytes 484
  249.9 247.3 %all-gather.22.cloned.1.call-start = ((), (), s32[]{:S(2)}) async-start(), calls=%async_computation.14 | async-start | bytes 4718592 | tf_op jit(solution)/shard_map/all_gather | solution.py:84
  250.5 313.4 %all-reduce.21.cloned.1.call-start = ((), (), s32[]{:S(2)}) async-start(), calls=%async_computation.15 | async-start | bytes 5242880 | tf_op jit(solution)/shard_map/psum | solution.py:211
  505.6 224.2 %all-gather.24.cloned.1.call-start = ((), (), s32[]{:S(2)}) async-start(), calls=%async_computation.16 | async-start | bytes 12976128 | tf_op jit(solution)/shard_map/all_gather | solution.py:213
  506.3 387.5 %all-gather.26.cloned.1.call-start = ((), (), s32[]{:S(2)}) async-start(), calls=%async_computation.17 | async-start | bytes 12976128 | tf_op jit(solution)/shard_map/all_gather | solution.py:214
  507.0 550.7 %all-gather.28.cloned.1.call-start = ((), (), s32[]{:S(2)}) async-start(), calls=%async_computation.18 | async-start | bytes 12976128 | tf_op jit(solution)/shard_map/all_gather | solution.py:215
  507.6 657.4 %all-reduce.23.cloned.1.call-start = ((), (), s32[]{:S(2)}) async-start(), calls=%async_computation.19 | async-start | bytes 5242880 | tf_op jit(solution)/shard_map/psum | solution.py:228
  1057.7 34.0 %slice-start = ((s8[11534336]{0:T(1024)(128)(4,1)}), s8[4194304]{0:T(1024)(128)(4,1)S(1)}, s32[]{:S(2)}) async-start(s8[11534336]{0:T(1024)(128)(4,1)} %bitcast.181), calls=%async_computation.30 | async-start | bytes 8388608
  1057.8 34.0 %slice-start.1 = ((s8[11534336]{0:T(1024)(128)(4,1)}), s8[4194304]{0:T(1024)(128)(4,1)S(1)}, s32[]{:S(2)}) async-start(s8[11534336]{0:T(1024)(128)(4,1)} %bitcast.181), calls=%async_computation.31 | async-start | bytes 8388608
  1106.7 336.1 %reduce-scatter.12.cloned.1.call-start = ((), (), s32[]{:S(2)}) async-start(), calls=%async_computation.21 | async-start | bytes 5898240 | tf_op jit(solution)/shard_map/reduce_scatter | solution.py:280
  1340.0 208.7 %reduce-scatter.10.cloned.1.call-start = ((), (), s32[]{:S(2)}) async-start(), calls=%async_computation.20 | async-start | bytes 5898240 | tf_op jit(solution)/shard_map/reduce_scatter | solution.py:286
  1345.4 390.1 %all-reduce.25.cloned.1.call-start = ((), (), s32[]{:S(2)}) async-start(), calls=%async_computation.29 | async-start | bytes 10485760 | tf_op jit(solution)/shard_map/psum | solution.py:226
  1364.3 80.0 %copy-start.29 = (f32[320,64]{1,0:T(8,128)S(1)}, f32[320,64]{1,0:T(8,128)}, u32[]{:S(2)}) copy-start(f32[320,64]{1,0:T(8,128)} %copy-done.28) | copy-start | bytes 245764
  1454.7 100.9 %copy-start.21 = (f32[320,512]{1,0:T(8,128)}, f32[320,512]{1,0:T(8,128)S(1)}, u32[]{:S(2)}) copy-start(f32[320,512]{1,0:T(8,128)S(1)} %reshape.321) | copy-start | bytes 1966084
  1566.4 300.5 %reduce-scatter.26.cloned.1.call-start = ((), (), s32[]{:S(2)}) async-start(), calls=%async_computation.28 | async-start | bytes 12976128 | tf_op jit(solution)/shard_map/reduce_scatter | solution.py:234
  1590.6 367.4 %reduce-scatter.20.cloned.1.call-start = ((), (), s32[]{:S(2)}) async-start(), calls=%async_computation.25 | async-start | bytes 4718592 | tf_op jit(solution)/shard_map/reduce_scatter | solution.py:306
  1601.4 448.8 %reduce-scatter.18.cloned.1.call-start = ((), (), s32[]{:S(2)}) async-start(), calls=%async_computation.24 | async-start | bytes 4718592 | tf_op jit(solution)/shard_map/reduce_scatter | solution.py:305
  1610.9 531.0 %reduce-scatter.14.cloned.1.call-start = ((), (), s32[]{:S(2)}) async-start(), calls=%async_computation.22 | async-start | bytes 4718592 | tf_op jit(solution)/shard_map/reduce_scatter | solution.py:303
  1620.4 613.9 %reduce-scatter.16.cloned.1.call-start = ((), (), s32[]{:S(2)}) async-start(), calls=%async_computation.23 | async-start | bytes 4718592 | tf_op jit(solution)/shard_map/reduce_scatter | solution.py:304
  1630.1 800.7 %reduce-scatter.22.cloned.1.call-start = ((), (), s32[]{:S(2)}) async-start(), calls=%async_computation.26 | async-start | bytes 12976128 | tf_op jit(solution)/shard_map/reduce_scatter | solution.py:232
  1655.5 971.3 %reduce-scatter.24.cloned.1.call-start = ((), (), s32[]{:S(2)}) async-start(), calls=%async_computation.27 | async-start | bytes 12976128 | tf_op jit(solution)/shard_map/reduce_scatter | solution.py:233
  1680.7 46.0 %copy-start.27 = (f32[256,512]{1,0:T(8,128)S(1)}, f32[256,512]{1,0:T(8,128)}, u32[]{:S(2)}) copy-start(f32[256,512]{1,0:T(8,128)} %param.31) | copy-start | bytes 1572868
  1740.3 49.7 %copy-start.35 = (f32[320]{0:T(512)S(1)}, f32[320]{0:T(512)}, u32[]{:S(2)}) copy-start(f32[320]{0:T(512)} %copy-done.34) | copy-start | bytes 3844
  (50 other events, 270.9 us)
Sparse Core Ops, SparseCore 0:
  10.2 76.1 all-gather.17
  88.4 71.6 all-gather.15
  162.3 71.6 all-gather.11
  236.6 84.7 all-gather.19
  323.9 84.4 all-gather.13
  410.4 71.5 all-gather.21
  505.7 58.1 all-reduce.20
  566.0 163.7 all-gather.23
  732.0 161.8 all-gather.25
  895.9 161.8 all-gather.27
  1106.9 58.1 all-reduce.22
  1340.1 102.6 reduce-scatter.11
  1446.4 102.3 reduce-scatter.9
  1566.5 102.4 all-reduce.24
  1672.5 194.3 reduce-scatter.25
  1871.0 86.9 reduce-scatter.19
  1962.5 87.6 reduce-scatter.17
  2054.3 87.6 reduce-scatter.13
  2146.6 87.6 reduce-scatter.15
  2238.3 192.4 reduce-scatter.21
  2435.0 191.7 reduce-scatter.23
where the time goes:
time: 2640 us; the launch traced here: 2630 us
  waiting for transfers between devices  1850 us (70%)
  matrix products  445 us (17%)
  blocking collectives  157 us (6%)
  local copies, waits for them, and re-layouts  92.5 us (4%)
  other arithmetic  53.9 us (2%)
    reduce_scatter x1, waiting for transfers between devices, shards(): lax.psum_scatter(grad_gate, 'row', scatter_dimension=0, tiled=True)  196 us
    reduce_scatter x1, waiting for transfers between devices, shards(): lax.psum_scatter(grad_up, 'row', scatter_dimension=0, tiled=True)  196 us
    all_gather x1, waiting for transfers between devices, shards(): lax.all_gather(w_gate, 'row', axis=0, tiled=True)  162 us
    all_gather x1, waiting for transfers between devices, shards(): lax.all_gather(w_up, 'row', axis=0, tiled=True)  146 us
    all_gather x1, waiting for transfers between devices, shards(): lax.all_gather(w_down, 'row', axis=0, tiled=True)  146 us
    reduce_scatter x1, waiting for transfers between devices, shards(): lax.psum_scatter(grad_value_blocks.reshape(key_total, local_heads * VD),...  94.1 us
    reduce_scatter x1, waiting for transfers between devices, shards(): lax.psum_scatter(grad_key, 'row', scatter_dimension=0, tiled=True)  92.3 us
    reduce_scatter x1, waiting for transfers between devices, shards(): lax.psum_scatter(grad_value, 'row', scatter_dimension=0, tiled=True)  92.2 us
  transfers between devices with their start and end apart: 21, of which 19 were waited for; matrix products, arithmetic and copies ran while one was open for 13% of the time, Pallas kernels for 0%

commit v1 on v0

v1 whole, which is shorter than its diff:
```python
import math

import jax
import jax.numpy as jnp
from jax import lax
from jax.experimental import pallas as pl
from jax.experimental.pallas import tpu as pltpu
from jax.sharding import Mesh
from jax.sharding import PartitionSpec as P

HEADS = 8
HD = 128
VD = 256
SEG = 64
ZN = 4
KN = 2
BLOCKS = ZN
TRUNK_SEGS = 8

epsilon = 1e-05
lambda_init = 0.2
rope_log_base = 9.210340371976184
high = lax.Precision.HIGH
highest = lax.Precision.HIGHEST
f32 = jnp.float32
bf16 = jnp.bfloat16
VMEM_BYTES = 60 * 1024 * 1024


def dot(a, b, contract_a=1, contract_b=0):
    return lax.dot_general(
        a, b, (((contract_a,), (contract_b,)), ((), ())), precision=high, preferred_element_type=f32
    )


def fine(a, b, contract_a=1, contract_b=0):
    return lax.dot_general(
        a, b, (((contract_a,), (contract_b,)), ((), ())), precision=highest, preferred_element_type=f32
    )


def thirds(v):
    top = v.astype(bf16)
    rest = v - top.astype(f32)
    low = rest.astype(bf16)
    return top, low, (rest - low.astype(f32)).astype(bf16)


def six(a, b):
    (a1, a2, a3), (b1, b2, b3) = a, b
    return mm(a1, b1) + (mm(a1, b2) + mm(a2, b1)) + (mm(a2, b2) + mm(a1, b3) + mm(a3, b1))


def halves(v):
    top = v.astype(bf16)
    return top, (v - top.astype(f32)).astype(bf16)


def mm(a, b):
    return jnp.dot(a, b, preferred_element_type=f32)


def after(v, *others):
    return lax.optimization_barrier((v,) + others)[0]


def shifted(v, axis, n, shift):
    return lax.ppermute(v, axis, [(i, (i + shift) % n) for i in range(n)])


def at(v, index, dim):
    return lax.dynamic_index_in_dim(v, index, dim, keepdims=False)


def part(v, index, rows):
    return lax.dynamic_slice_in_dim(v, index * rows, rows)


def exchanged(v, axis, n):
    i = lax.axis_index(axis)
    rows = v.shape[0] // n
    return [part(v, i, rows)] + [
        shifted(part(v, (i + s) % n, rows), axis, n, s) for s in range(1, n)
    ]


def in_order(pieces, axis, n, dim=0):
    i = lax.axis_index(axis)

    def source(j):
        shift = (i + n - j) % n
        out = pieces[0]
        for s in range(1, n):
            out = jnp.where(shift == s, pieces[s], out)
        return out

    return jnp.concatenate([source(j) for j in range(n)], axis=dim)


def small_gather(v, axis, n):
    return in_order([v[None]] + [shifted(v[None], axis, n, s) for s in range(1, n)], axis, n)


def small_fold(v, axis, n, fold):
    out = v
    for s in range(1, n):
        out = fold(out, shifted(v, axis, n, s))
    return out


def direct(v, xn, yn):
    out = {}
    for s in range(xn):
        for t in range(yn):
            pairs = [
                (a * yn + b, (a + s) % xn * yn + (b + t) % yn) for a in range(xn) for b in range(yn)
            ]
            out[s, t] = lax.ppermute(v, ("x", "y"), pairs) if s or t else v
    return out


def square_out(v, first, sizes):
    n = sizes[first]
    return [v] + [shifted(v, first, n, s) for s in range(1, n)]


def side_out(v, first, sizes):
    second = "y" if first == "x" else "x"
    n = sizes[second]
    return [shifted(v, second, n, t) for t in range(1, n)]


def square_on(came, first, sizes, side=None):
    second = "y" if first == "x" else "x"
    n = sizes[second]
    out = {}
    for s, v in enumerate(came):
        out[s, 0] = v
        for t in range(1, n):
            out[s, t] = side[t - 1] if side and s == 0 else shifted(v, second, n, t)
    return out if first == "x" else {(s, t): v for (t, s), v in out.items()}


def along_first(pieces, first):
    return pieces if first == "x" else {(t, s): v for (s, t), v in pieces.items()}


def square_back(pieces, first, sizes):
    m, n = sizes[first], sizes["y" if first == "x" else "x"]
    v = along_first(pieces, first)
    return [shifted(v[s, t], first, m, -s) for t in reversed(range(n)) for s in range(1, m)]


def square_added(pieces, came, first, sizes):
    m, n = sizes[first], sizes["y" if first == "x" else "x"]
    v = along_first(pieces, first)
    out = [v[0, t] for t in range(n)]
    order = [t for t in reversed(range(n)) for s in range(1, m)]
    for t, what in zip(order, came):
        out[t] = out[t] + what
    return out


def square_back_on(sums, second, sizes):
    n = sizes[second]
    return [shifted(sums[t], second, n, -t) for t in range(1, n)]


def logits_chunk(keys_wide, queries, rows, j):
    first, last = keys_wide[0, j, rows, :], keys_wide[1, j, rows, :]
    top, low, rest = queries[j]
    return mm(first, top) + (mm(first, low) + mm(last, rest))


def split_keys(keys, keys_wide, rows):
    for j in range(2):
        top, low, rest = thirds(keys[:, j * HD : (j + 1) * HD])
        keys_wide[0, j, rows, :HD] = top
        keys_wide[0, j, rows, HD:] = low
        keys_wide[1, j, rows, :HD] = top
        keys_wide[1, j, rows, HD:] = rest


def split_queries(q):
    out = []
    for j in range(2):
        top, low, rest = thirds(q[:, j * HD : (j + 1) * HD].T)
        out.append([jnp.concatenate(p, axis=0) for p in ((top, top), (low, low), (rest, top))])
    return out


def chunk_rows(c, size):
    return pl.ds(pl.multiple_of(c * size, size), size)


def brought(run, start_ref, first, count, source, target):
    def move(i, carry):
        target[chunk_rows(i, run), :] = source[chunk_rows(start_ref[first + i], run), :]
        return carry

    lax.fori_loop(0, count, move, 0)


def taken_back(run, start_ref, first, count, source, target):
    def move(i, carry):
        target[chunk_rows(start_ref[first + i], run), :] = source[chunk_rows(i, run), :]
        return carry

    lax.fori_loop(0, count, move, 0)


def forward_kernel(
    run, mix_ref, seen_ref, count_ref, key_ref, own_ref, q_ref, k_ref, v_ref, bias_ref,
    o_ref, stat_ref, keys_wide, vt, held, sorted_rows, sorted_q,
):
    total = k_ref.shape[0]
    chunk = vt.shape[3]
    count = total // chunk
    tile = pl.program_id(0)

    @pl.when(tile == 0)
    def _():
        brought(run, own_ref, 0, q_ref.shape[0] // run, q_ref, sorted_q)
        brought(run, key_ref, 0, total // run, k_ref, sorted_rows)

        def split(c, carry):
            rows = chunk_rows(c, chunk)
            split_keys(sorted_rows[rows, :], keys_wide, rows)
            return carry

        lax.fori_loop(0, count, split, 0)
        brought(run, key_ref, 0, total // run, v_ref, sorted_rows)

        def turn(c, carry):
            for i, p in enumerate(thirds(sorted_rows[chunk_rows(c, chunk), :].T)):
                vt[i, c] = p
            return carry

        lax.fori_loop(0, count, turn, 0)

    split = split_queries(sorted_q[chunk_rows(tile, TILE), :])
    visits = count_ref[tile]

    def score(i, peaks):
        rows = chunk_rows(seen_ref[tile * count + i], chunk)
        out = []
        for j in range(2):
            s = logits_chunk(keys_wide, split, rows, j) + bias_ref[rows, :]
            held[j, rows, :] = s
            out.append(jnp.maximum(peaks[j], jnp.max(s, axis=0, keepdims=True)))
        return tuple(out)

    peaks = lax.fori_loop(0, visits, score, (jnp.full((1, TILE), -1e30, f32),) * 2)

    def weigh(i, sums):
        rows = chunk_rows(seen_ref[tile * count + i], chunk)
        out = []
        for j in range(2):
            w = jnp.exp(held[j, rows, :] - peaks[j])
            held[j, rows, :] = w
            out.append(sums[j] + jnp.sum(w, axis=0, keepdims=True))
        return tuple(out)

    sums = lax.fori_loop(0, visits, weigh, (jnp.zeros((1, TILE), f32),) * 2)
    first, second = 1.0 / sums[0], mix_ref[0] / sums[1]

    def collect(i, acc):
        c = seen_ref[tile * count + i]
        rows = chunk_rows(c, chunk)
        both = thirds(held[0, rows, :] * first - held[1, rows, :] * second)
        return acc + six([vt[i, c] for i in range(3)], both)

    out = lax.fori_loop(0, visits, collect, jnp.zeros((VD, TILE), f32)).T
    for i in range(TILE // run):
        o_ref[chunk_rows(own_ref[tile * (TILE // run) + i], run), :] = out[i * run : (i + 1) * run, :]
    for j in range(2):
        stat_ref[j : j + 1, :] = peaks[j] + jnp.log(sums[j])
        stat_ref[2 + j : 3 + j, :] = peaks[j]
    stat_ref[4:8, :] = jnp.zeros((4, TILE), f32)


def backward_kernel(
    run, mix_ref, seen_ref, count_ref, key_ref, own_ref, q_ref, dc_ref, stat_ref, k_ref, v_ref, bias_ref,
    dq_ref, dk_ref, dv_ref, inner_ref, keys_wide, kt, held, cross, sorted_v, sorted_q, sorted_dc,
):
    total = k_ref.shape[0]
    chunk = kt.shape[3]
    count = total // chunk
    mix = mix_ref[0]
    tile = pl.program_id(0)

    @pl.when(tile == 0)
    def _():
        brought(run, own_ref, 0, q_ref.shape[0] // run, q_ref, sorted_q)
        brought(run, own_ref, 0, q_ref.shape[0] // run, dc_ref, sorted_dc)
        brought(run, key_ref, 0, total // run, k_ref, sorted_v)

        def prepare(c, carry):
            rows = chunk_rows(c, chunk)
            keys = sorted_v[rows, :]
            split_keys(keys, keys_wide, rows)
            for i, p in enumerate(halves(keys.T)):
                kt[i, c] = p
            dk_ref[rows, :] = jnp.zeros(keys.shape, f32)
            dv_ref[rows, :] = jnp.zeros(keys.shape, f32)
            return carry

        lax.fori_loop(0, count, prepare, 0)
        brought(run, key_ref, 0, total // run, v_ref, sorted_v)

    queries, cotangents = sorted_q[chunk_rows(tile, TILE), :], sorted_dc[chunk_rows(tile, TILE), :]
    split = split_queries(queries)
    dct = thirds(cotangents.T)
    dc_top, dc_low = halves(cotangents)
    dc_wide = jnp.concatenate([dc_top, dc_top], axis=0)
    q_top, q_low = halves(queries)
    q_wide = jnp.concatenate([q_top, q_top], axis=0)
    norms = [stat_ref[j : j + 1, :] for j in range(2)]
    visits = count_ref[tile]

    def first(i, inner):
        rows = chunk_rows(seen_ref[tile * count + i], chunk)
        bias = bias_ref[rows, :]
        both = six(thirds(sorted_v[rows, :]), dct)
        cross[rows, :] = both
        out, probs = [], []
        for j in range(2):
            p = jnp.exp(logits_chunk(keys_wide, split, rows, j) + bias - norms[j])
            held[j, rows, :] = p
            probs.append(p)
            out.append(inner[j] + jnp.sum(p * both, axis=0, keepdims=True))
        top, low = halves(probs[0] - mix * probs[1])
        dv_ref[rows, :] += mm(jnp.concatenate([top, low], axis=1), dc_wide) + mm(top, dc_low)
        return tuple(out)

    inner = lax.fori_loop(0, visits, first, (jnp.zeros((1, TILE), f32),) * 2)

    def second(i, acc):
        c = seen_ref[tile * count + i]
        rows = chunk_rows(c, chunk)
        both = cross[rows, :]
        out = []
        for j in range(2):
            d = held[j, rows, :] * (both - inner[j])
            if j == 1:
                d = d * (-mix)
            top, low = halves(d)
            cols = slice(j * HD, (j + 1) * HD)
            dk_ref[rows, cols] += mm(jnp.concatenate([top, low], axis=1), q_wide[:, cols]) + mm(
                top, q_low[:, cols]
            )
            kt_top, kt_low = kt[0, c, cols, :], kt[1, c, cols, :]
            out.append(acc[j] + (mm(kt_top, top) + (mm(kt_top, low) + mm(kt_low, top))))
        return tuple(out)

    dq = lax.fori_loop(0, visits, second, (jnp.zeros((HD, TILE), f32),) * 2)
    dq = jnp.concatenate(dq, axis=0).T
    for i in range(TILE // run):
        dq_ref[chunk_rows(own_ref[tile * (TILE // run) + i], run), :] = dq[i * run : (i + 1) * run, :]
    for j in range(2):
        inner_ref[j : j + 1, :] = inner[j]
    inner_ref[2:8, :] = jnp.zeros((6, TILE), f32)

    @pl.when(tile == pl.num_programs(0) - 1)
    def _():
        for ref in (dk_ref, dv_ref):

            def keep(c, carry):
                rows = chunk_rows(c, chunk)
                sorted_v[rows, :] = ref[rows, :]
                return carry

            lax.fori_loop(0, count, keep, 0)
            taken_back(run, key_ref, 0, total // run, sorted_v, ref)


TILE = 128
CHUNK = 256


def whole():
    return pl.BlockSpec(memory_space=pltpu.VMEM)


def table():
    return pl.BlockSpec(memory_space=pltpu.SMEM)


def attend(run, mix, tables, queries, keys, values, bias):
    total, count = keys.shape[0], queries.shape[0]
    chunk = math.gcd(total, CHUNK)
    lanes = lambda rows: pl.BlockSpec((rows, TILE), lambda i: (0, i))
    return pl.pallas_call(
        lambda *refs: forward_kernel(run, *refs),
        grid=(count // TILE,),
        in_specs=[table()] * 5 + [whole()] * 3 + [lanes(total)],
        out_specs=[whole(), lanes(8)],
        out_shape=[
            jax.ShapeDtypeStruct((count, VD), f32), jax.ShapeDtypeStruct((8, count), f32),
        ],
        scratch_shapes=[
            pltpu.VMEM((2, 2, total, 2 * HD), bf16),
            pltpu.VMEM((3, total // chunk, VD, chunk), bf16),
            pltpu.VMEM((2, total, TILE), f32),
            pltpu.VMEM((total, 2 * HD), f32),
            pltpu.VMEM((count, 2 * HD), f32),
        ],
        compiler_params=pltpu.CompilerParams(vmem_limit_bytes=VMEM_BYTES),
        cost_estimate=pl.CostEstimate(flops=4 * 10**10, bytes_accessed=0, transcendentals=0),
        name="attend",
    )(mix, *tables, queries, keys, values, bias)


def attend_back(run, mix, tables, queries, contrast, stat, keys, values, bias):
    total, count = keys.shape[0], queries.shape[0]
    chunk = math.gcd(total, CHUNK)
    lanes = lambda rows: pl.BlockSpec((rows, TILE), lambda i: (0, i))
    return pl.pallas_call(
        lambda *refs: backward_kernel(run, *refs),
        grid=(count // TILE,),
        in_specs=[table()] * 5 + [whole()] * 2 + [lanes(8)] + [whole()] * 2 + [lanes(total)],
        out_specs=[whole(), whole(), whole(), lanes(8)],
        out_shape=[
            jax.ShapeDtypeStruct((count, 2 * HD), f32),
            jax.ShapeDtypeStruct((total, 2 * HD), f32),
            jax.ShapeDtypeStruct((total, VD), f32),
            jax.ShapeDtypeStruct((8, count), f32),
        ],
        scratch_shapes=[
            pltpu.VMEM((2, 2, total, 2 * HD), bf16),
            pltpu.VMEM((2, total // chunk, 2 * HD, chunk), bf16),
            pltpu.VMEM((2, total, TILE), f32),
            pltpu.VMEM((total, TILE), f32),
            pltpu.VMEM((total, VD), f32),
            pltpu.VMEM((count, 2 * HD), f32),
            pltpu.VMEM((count, VD), f32),
        ],
        compiler_params=pltpu.CompilerParams(vmem_limit_bytes=VMEM_BYTES),
        cost_estimate=pl.CostEstimate(flops=4 * 10**10, bytes_accessed=0, transcendentals=0),
        name="attend_back",
    )(mix, *tables, queries, contrast, stat, keys, values, bias)


def layer(xn, yn):
    sizes = {"x": xn, "y": yn}
    places = [(s, t) for s in range(xn) for t in range(yn)]

    def shards(
        tokens, cotangent, w_query, w_key, w_value, w_output, gain_attn, lambda_query_first,
        lambda_key_first, lambda_query_second, lambda_key_second, gain_head, w_gate, w_up, w_down,
        gain_ffn, tau, parent_slot, depth,
    ):
        z, x, y, k = (lax.axis_index(a) for a in "zxyk")
        home_rows, width = tokens.shape
        segs = home_rows // SEG
        run = SEG // (yn * KN)
        piece_rows = segs * run
        group = ZN * KN * piece_rows
        sub = BLOCKS // yn
        held_rows = w_query.shape[0]
        part_rows = held_rows // yn
        square_rows = ZN * part_rows
        total = ZN * xn * home_rows
        slot_total = parent_slot.shape[0]
        hidden_cols = w_gate.shape[1] // sub

        def block(v, i):
            return v[:, i * part_rows : (i + 1) * part_rows]

        def by_index(i, n, order):
            out = order(0)
            for j in range(1, n):
                out = jnp.where(i == j, order(j), out)
            return out

        def to_distance_x(v):
            return by_index(x, xn, lambda j: jnp.concatenate(
                [block(v, (c * xn + (j + xn - s) % xn) * yn + t)
                 for s in range(xn) for c in range(ZN) for t in range(yn)], axis=1))

        def from_distance_x(v):
            return by_index(x, xn, lambda j: jnp.concatenate(
                [block(v, ((j + xn - a) % xn * ZN + c) * yn + t)
                 for c in range(ZN) for a in range(xn) for t in range(yn)], axis=1))

        def to_distance_y(v):
            return by_index(y, yn, lambda j: jnp.concatenate(
                [block(v, (s * ZN + c) * yn + (j + yn - t) % yn)
                 for s in range(xn) for t in range(yn) for c in range(ZN)], axis=1))

        def from_distance_y(v):
            return by_index(y, yn, lambda j: jnp.concatenate(
                [block(v, (s * yn + (j + yn - t) % yn) * ZN + c)
                 for s in range(xn) for c in range(ZN) for t in range(yn)], axis=1))

        def piece(v):
            v = v.reshape(segs, yn * KN, run, width)
            return to_distance_x(at(v, y * KN + k, 1).reshape(piece_rows, width))

        def home_along(v, axis, n):
            return [v] + [shifted(v, axis, n, s) for s in range(1, n)]

        def homed(v):
            v = v.reshape(KN, yn, segs, run, width)
            return jnp.transpose(v, (2, 1, 0, 3, 4)).reshape(home_rows, width)

        def group_gather(v):
            return lax.all_gather(v, ("z", "k"), axis=0, tiled=True)

        def group_sum(v):
            return lax.psum_scatter(v, ("z", "k"), scatter_dimension=0, tiled=True)

        def packed(mats, blocks):
            rows = mats[0].shape[1] // blocks
            mats = [m.T for m in mats]
            return jnp.concatenate([m[s * rows : (s + 1) * rows] for s in range(blocks) for m in mats])

        def lanes(v, index, size):
            return lax.dynamic_slice_in_dim(v, index * size, size, 1)

        def along_y(v):
            mine = lanes(v, y, part_rows)
            return [mine] + [shifted(lanes(v, (y + s) % yn, part_rows), "y", yn, s) for s in range(1, yn)]

        def back_along_z(mats):
            v = jnp.concatenate(mats)
            size = v.shape[1] // ZN
            mine = lanes(v, z, size)
            return [mine] + [shifted(lanes(v, (z + s) % ZN, size), "z", ZN, s) for s in range(1, ZN)]

        def unpacked(v, mats, blocks):
            cols = v.shape[0] // (blocks * mats)
            part = lambda s, m: v[(s * mats + m) * cols : (s * mats + m + 1) * cols]
            return [jnp.concatenate([part(s, m) for s in range(blocks)]).T for m in range(mats)]

        def joined_up(pieces):
            return jnp.concatenate([pieces[p] for p in places], axis=1)

        def cut(g):
            return {p: g[:, i * square_rows : (i + 1) * square_rows] for i, p in enumerate(places)}

        def tiled_up(pieces):
            return jnp.concatenate(
                [jnp.concatenate([pieces[s, t] for s in range(xn)], axis=1) for t in range(yn)]
            )

        def tiles(g):
            r, c = g.shape[0] // yn, g.shape[1] // xn
            return {(s, t): g[t * r : (t + 1) * r, s * c : (s + 1) * c] for s, t in places}

        def halved(v):
            mid = v.shape[0] // 2
            return v[:mid], v[mid:]

        def rowsum(w, g):
            return jnp.sum(w * g, axis=1)

        last = []

        def now(*v):
            out = lax.optimization_barrier(tuple(v) + tuple(last))[: len(v)]
            return out[0] if len(v) == 1 else out

        def then(*v):
            last[:] = v
            return v[0] if len(v) == 1 else v

        def take(*v):
            out = now(*v)
            return then(*(out if len(v) > 1 else (out,)))

        def take_all(pieces):
            out = lax.optimization_barrier(tuple(pieces) + tuple(last))[: len(pieces)]
            then(*out)
            return list(out)

        attn_gain, ffn_gain = gain_attn[:, None], gain_ffn[:, None]
        sent = along_y(packed([w_query, w_key, w_value], sub))
        small = jnp.concatenate(
            [gain_head, lambda_query_first, lambda_key_first, lambda_query_second, lambda_key_second]
        )
        small_sent = home_along(small[None], "x", xn)
        mine = piece(tokens)
        scale = lax.rsqrt(jnp.mean(mine * mine, axis=1, keepdims=True) + epsilon)
        plain_mine = then(to_distance_y(mine) * scale)
        small = in_order(take_all(small_sent), "x", xn).reshape(1, -1)
        small_sent = home_along(small, "z", ZN)
        down_sent = w_down.T
        then(down_sent)
        small = in_order(take_all(small_sent), "z", ZN)
        attn_y = in_order(take_all(sent), "y", yn)
        y_gain = part(gain_attn, y, part_rows)[None, :]
        sent = exchanged(attn_y * y_gain, "z", ZN)
        output_sent = along_y(after(packed([w_output], sub), attn_y))
        small = small.reshape(ZN * xn, -1)
        n_gain, n_lambda = gain_head.shape[0], lambda_key_first.shape[0]
        head_gain = small[:, :n_gain].reshape(1, -1)
        query_first, key_first, query_second, key_second = (
            small[:, n_gain + i * n_lambda : n_gain + (i + 1) * n_lambda] for i in range(4)
        )
        mix = (
            jnp.exp(jnp.sum(query_first * key_first))
            - jnp.exp(jnp.sum(query_second * key_second))
            + lambda_init
        ).reshape(1)

        slot_ids = jnp.arange(slot_total, dtype=jnp.int32)
        same = slot_ids[:, None] == slot_ids[None, :]
        reach = (same | (parent_slot[:, None] == slot_ids[None, :])).astype(f32)
        for _ in range(4):
            reach = (jnp.dot(reach, reach) > 0.5).astype(f32)
        strict = jnp.where(same, 0.0, reach)
        depth_of = jnp.sum(strict, axis=1)

        ids = slot_ids.astype(f32)
        root = jnp.sum(reach * jnp.where(depth_of == 0, ids, 0.0)[None, :], axis=1)
        branch_slot = jnp.sum(reach * jnp.where(depth_of == TRUNK_SEGS, ids + 1.0, 0.0)[None, :], axis=1)
        leaf = jnp.where(depth_of > TRUNK_SEGS, ids + 1.0, 0.0)
        place = jnp.where(
            depth_of < TRUNK_SEGS, depth_of, TRUNK_SEGS + branch_slot * (slot_total + 1) + leaf
        )
        ordinal = (root * (TRUNK_SEGS + (slot_total + 1) ** 2 + 1) + place).astype(jnp.int32)
        before = (ordinal[None, :] < ordinal[:, None]) | (
            (ordinal[None, :] == ordinal[:, None]) & (slot_ids[None, :] < slot_ids[:, None])
        )
        rank = jnp.sum(before, axis=1)
        mine_too = slot_ids // segs % xn == x
        own_rank = jnp.sum(before & mine_too[None, :], axis=1)
        own_slots = ZN * segs
        key_order = jnp.sum(jnp.where(rank[:, None] == slot_ids[None, :], slot_ids[:, None], 0), axis=0)
        own_order = jnp.sum(
            jnp.where(
                (own_rank[:, None] == jnp.arange(own_slots)[None, :]) & mine_too[:, None],
                slot_ids[:, None], 0,
            ),
            axis=0,
        )

        def run_at(slot, k_of):
            return ((slot // (xn * segs)) * KN + k_of) * segs + slot % segs

        ks = jnp.arange(KN, dtype=jnp.int32)
        own_runs = run_at(own_order[:, None], ks[None, :]).reshape(-1)
        ys = jnp.arange(yn, dtype=jnp.int32)[None, :, None]
        slot = key_order[:, None, None]
        piece_of = ((x + xn - slot // segs % xn) % xn) * yn + (y + yn - ys) % yn
        key_runs = (piece_of * (group // run) + run_at(slot, ks[None, None, :])).reshape(-1)

        padded = -(-group // TILE) * TILE
        extra = padded - group
        own_slot = jnp.repeat(own_order, group // own_slots)
        own_offset = y * KN * run + jnp.arange(group, dtype=jnp.int32) % (KN * run)
        key_slot, key_offset = jnp.repeat(key_order, SEG), jnp.arange(total, dtype=jnp.int32) % SEG
        own_hot = (own_slot[:, None] == slot_ids[None, :]).astype(f32)
        key_hot = (key_slot[:, None] == slot_ids[None, :]).astype(f32)
        own_path = jnp.dot(own_hot, strict)
        seen = jnp.dot(key_hot, own_path.T) > 0.5
        seen = seen | (
            (key_slot[:, None] == own_slot[None, :]) & (key_offset[:, None] <= own_offset[None, :])
        )
        seen = jnp.pad(seen, ((0, 0), (0, extra)))
        own_runs = jnp.concatenate([own_runs, jnp.arange(group // run, padded // run, dtype=own_runs.dtype)])
        bias = jnp.where(seen, 0.0, -1e30).astype(f32)
        chunk = math.gcd(total, CHUNK)
        chunks = total // chunk
        slot_seen = (own_path + own_hot > 0.5).astype(f32)
        slot_seen = jnp.pad(slot_seen, ((0, extra), (0, 0))).reshape(padded // TILE, TILE, slot_total)
        slot_seen = jnp.max(slot_seen, axis=1)
        in_chunk = (rank[:, None] * SEG // chunk == jnp.arange(chunks)[None, :]).astype(f32)
        visited = jnp.dot(slot_seen, in_chunk) > 0.5
        visits = jnp.sum(visited, axis=1).astype(jnp.int32)
        turn = jnp.cumsum(visited, axis=1) - 1
        listed = (turn[:, :, None] == jnp.arange(chunks)[None, None, :]) & visited[:, :, None]
        listed = jnp.sum(jnp.where(listed, jnp.arange(chunks)[None, :, None], 0), axis=1)
        tables = tuple(
            v.reshape(-1).astype(jnp.int32) for v in (listed, visits, key_runs, own_runs)
        )

        def padded_rows(v):
            return jnp.pad(v, ((0, extra), (0, 0)))

        shape = (ZN, KN, segs, run)
        zs, ks, gs, rs = (lax.broadcasted_iota(jnp.int32, shape, d) for d in range(4))
        lying_slot = ((zs * xn + x) * segs + gs).reshape(group)
        own_hot = (lying_slot[:, None] == slot_ids[None, :]).astype(f32)
        own_offset = ((y * KN + ks) * run + rs).reshape(group)
        position = jnp.dot(own_hot, depth_of[:, None], precision=lax.Precision.HIGHEST) * SEG
        position = position + own_offset[:, None].astype(f32)
        half_dim = HD // 2
        frequency = jnp.exp(-rope_log_base * jnp.arange(half_dim, dtype=f32) / half_dim)
        angles = position * frequency[None, :]
        cosine, sine = jnp.cos(angles), jnp.sin(angles)
        cosine = jnp.concatenate([cosine] * 4, axis=1)
        sine = jnp.concatenate([-sine, sine] * 2, axis=1)

        def rotate(v, sign):
            parts = [v[:, i * half_dim : (i + 1) * half_dim] for i in (1, 0, 3, 2)]
            return v * cosine + jnp.concatenate(parts, axis=1) * (sign * sine)

        gate_up_sent = packed([w_up * ffn_gain, w_gate * ffn_gain], 1)
        cot_mine = piece(cotangent)
        then(gate_up_sent, cot_mine, bias, cosine, sine, mix, *tables)
        output_y = in_order(take_all(output_sent), "y", yn)
        attn_z = in_order(take_all(sent), "z", ZN, 1)
        upper, lower = halved(attn_z)
        upper_out, lower_out = square_out(upper, "x", sizes), square_out(lower, "y", sizes)
        upper_side, lower_side = side_out(upper, "x", sizes), side_out(lower, "y", sizes)
        plain_sent = group_gather(after(plain_mine, attn_z))
        upper_on = square_on(take_all(upper_out), "x", sizes, upper_side)
        lower_on = square_on(take_all(lower_out), "y", sizes, lower_side)

        plain = take(plain_sent)
        up_sent, gate_sent = halved(gate_up_sent)
        down_sent = exchanged(after(down_sent, plain), "z", ZN)
        output_sent = exchanged(after(output_y, plain), "z", ZN)
        upper = joined_up(dict(zip(places, take_all([upper_on[p] for p in places]), strict=True)))
        lower = joined_up(dict(zip(places, take_all([lower_on[p] for p in places]), strict=True)))
        wqkv = jnp.concatenate([upper, lower])
        wqk, wv = wqkv[: 4 * HD], wqkv[4 * HD :]
        then(wqkv)
        logit_scale = 1.0 / math.sqrt(HD)
        key_own = then(rotate(fine(now(plain), wqk[2 * HD :], 1, 1), 1.0))
        key_sent = square_out(key_own, "x", sizes)
        value_own = then(fine(now(plain), wv, 1, 1))
        value_sent = square_out(value_own, "y", sizes)
        queries = rotate(fine(now(plain), wqk[: 2 * HD], 1, 1), 1.0)
        queries = then(padded_rows(queries * logit_scale))
        key_sent = square_on(take_all(key_sent), "x", sizes)
        value_sent = square_on(take_all(value_sent), "y", sizes)
        down_z = in_order(take_all(down_sent), "z", ZN, 1)
        up_sent = exchanged(after(up_sent, queries), "z", ZN)
        gate_sent = exchanged(after(gate_sent, down_z), "z", ZN)
        output_z = in_order(take_all(output_sent), "z", ZN, 1)
        key_list = take_all([key_sent[p] for p in places])
        value_list = take_all([value_sent[p] for p in places])
        up_w = in_order(take_all(up_sent), "z", ZN, 1)
        output_sent = direct(after(output_z, *value_list), xn, yn)
        down_z = after(down_z, *value_list)
        down_out, down_side = square_out(down_z, "x", sizes), side_out(down_z, "x", sizes)
        keys, values = jnp.concatenate(key_list), jnp.concatenate(value_list)
        contrast, stat = attend(run, mix, tables, now(queries), keys, values, bias)
        then(contrast)
        gate_w = in_order(take_all(gate_sent), "z", ZN, 1)
        output_sent = dict(zip(places, take_all([output_sent[p] for p in places]), strict=True))
        wo = joined_up(output_sent)
        contrast = now(contrast)[:group]
        head_scale = lax.rsqrt(jnp.mean(contrast * contrast, axis=1, keepdims=True) + epsilon)
        head_plain = contrast * head_scale
        joined = head_plain * head_gain * (1.0 - lambda_init)
        branch_part = then(fine(joined, wo))
        branch_sent = group_sum(branch_part)

        down_out, down_side = take_all(down_out), take_all(down_side)
        down_on = square_on(down_out, "x", sizes, down_side)
        up_w = after(up_w, *down_out)
        up_out, up_side = square_out(up_w, "y", sizes), side_out(up_w, "y", sizes)
        down_pieces = dict(zip(places, take_all([down_on[p] for p in places]), strict=True))
        up_side = take_all(up_side)
        gate_top, gate_low = halved(after(gate_w, *up_side))
        top_out, low_out = square_out(gate_top, "x", sizes), square_out(gate_low, "y", sizes)
        top_side, low_side = side_out(gate_top, "x", sizes), side_out(gate_low, "y", sizes)
        branch = take(branch_sent)
        residual = mine + from_distance_y(branch)
        ffn_scale = lax.rsqrt(jnp.mean(residual * residual, axis=1, keepdims=True) + epsilon)
        ffn_mine = then(residual * ffn_scale)
        ffn_sent = group_gather(ffn_mine)
        wd = then(tiled_up(down_pieces))
        top_out, low_side = take_all(top_out), take_all(low_side)
        up_on = square_on(take_all(up_out), "y", sizes, up_side)
        top_on = square_on(top_out, "x", sizes, top_side)
        low_on = square_on(take_all(low_out), "y", sizes, low_side)
        up_pieces = dict(zip(places, take_all([up_on[p] for p in places]), strict=True))
        ffn_plain = take(ffn_sent)
        cot_sent = group_gather(after(cot_mine, ffn_plain))
        wu = tiled_up(up_pieces)
        up_proj = then(fine(wu, ffn_plain, 1, 1))
        top_list = take_all([top_on[p] for p in places])
        low_list = take_all([low_on[p] for p in places])
        wg = tiled_up({p: jnp.concatenate(v) for p, *v in zip(places, top_list, low_list, strict=True)})

        gating = then(fine(wg, ffn_plain, 1, 1))
        gate = lax.logistic(gating)
        active = gating * gate
        hidden = active * up_proj
        cot = take(cot_sent)
        grad_hidden = fine(wd, cot, 1, 1)
        grad_up_proj = grad_hidden * active
        grad_gating = grad_hidden * up_proj * gate * (1.0 + gating * (1.0 - gate))
        grad_ffn_part = then(fine(grad_gating, wg, 0, 0) + fine(grad_up_proj, wu, 0, 0))
        grad_ffn_sent = group_sum(grad_ffn_part)
        down_grad = then(dot(now(hidden), cot))
        down_first = tiles(down_grad)
        down_sent = square_back(down_first, "x", sizes)
        up_grad = then(dot(now(grad_up_proj), ffn_plain))
        up_first = tiles(up_grad)
        up_sent = square_back(up_first, "y", sizes)
        gate_grad = then(dot(now(grad_gating), ffn_plain))
        gate_tiles = {p: halved(v) for p, v in tiles(gate_grad).items()}
        top_first = {p: v[0] for p, v in gate_tiles.items()}
        low_first = {p: v[1] for p, v in gate_tiles.items()}
        out_part = then(dot(now(hidden), wd, 0, 0))
        early = (xn - 1) * (yn - 1)
        down_sent[:early], up_sent[:early] = take_all(down_sent[:early]), take_all(up_sent[:early])
        down_first = square_added(down_first, down_sent[:early], "x", sizes)
        down_sent_on = square_back_on(down_first, "y", sizes)
        up_first = square_added(up_first, up_sent[:early], "y", sizes)
        up_sent_on = square_back_on(up_first, "x", sizes)
        then(*down_first[1:], *up_first[1:])
        scaled = take(grad_ffn_sent)
        grad_residual = cot_mine + ffn_scale * (
            scaled - ffn_mine * jnp.mean(scaled * ffn_mine, axis=1, keepdims=True)
        )
        grad_residual_attn = then(to_distance_y(grad_residual))
        grad_branch_sent = group_gather(grad_residual_attn)
        down_grad = sum(take_all(down_sent[early:]), down_first[0])
        up_grad = sum(take_all(up_sent[early:]), up_first[0])
        then(down_grad, up_grad)
        grad_branch = take(grad_branch_sent)

        out_sent = group_sum(after(out_part, grad_branch))
        grad_joined = fine(grad_branch, wo, 1, 1) * (1.0 - lambda_init)
        grad_head_gain = jnp.sum(grad_joined * head_plain, axis=0)
        scaled = grad_joined * head_gain
        grad_contrast = padded_rows(
            head_scale * (scaled - head_plain * jnp.mean(scaled * head_plain, axis=1, keepdims=True))
        )
        grad_contrast = then(grad_contrast)
        down_grad = sum(take_all(down_sent_on), down_grad)
        down_back = back_along_z([down_grad])
        up_grad = sum(take_all(up_sent_on), up_grad)
        up_back = back_along_z([up_grad])
        then(down_grad, up_grad)
        top_sent = square_back({p: after(v, down_grad) for p, v in top_first.items()}, "x", sizes)
        low_sent = square_back({p: after(v, up_grad) for p, v in low_first.items()}, "y", sizes)
        grad_contrast = now(grad_contrast)
        grad_queries, grad_keys, grad_values, inner = attend_back(
            run, mix, tables, queries, grad_contrast, stat, keys, values, bias
        )
        then(grad_queries, grad_keys, grad_values)
        rows_cut = lambda g: {p: g[i * group : (i + 1) * group] for i, p in enumerate(places)}
        key_first, value_first = rows_cut(grad_keys), rows_cut(grad_values)
        key_sent = square_back(key_first, "x", sizes)
        value_sent = square_back(value_first, "y", sizes)
        def reduced(v):
            return jnp.concatenate([jnp.max(v[:, :2], axis=0), jnp.sum(v[:, 2:], axis=0)])[None]

        peak = jnp.max(stat[2:4, :group], axis=1)
        every = jnp.concatenate([peak, grad_head_gain, -jnp.sum(inner[1:2, :group], axis=1)])[None]
        every_sent = home_along(every, "x", xn)
        top_first = square_added(top_first, take_all(top_sent), "x", sizes)
        low_first = square_added(low_first, take_all(low_sent), "y", sizes)
        then(*top_first, *low_first)
        key_first = square_added(key_first, take_all(key_sent), "x", sizes)
        key_sent = square_back_on(key_first, "y", sizes)
        value_first = square_added(value_first, take_all(value_sent), "y", sizes)
        value_sent = square_back_on(value_first, "x", sizes)
        then(*key_first, *value_first)
        every_sent = home_along(reduced(in_order(take_all(every_sent), "x", xn)), "y", yn)
        top_sent = square_back_on([after(v, *key_first) for v in top_first], "y", sizes)
        low_sent = square_back_on([after(v, *value_first) for v in low_first], "x", sizes)
        grad_q = rotate(grad_queries[:group] * logit_scale, -1.0)
        query_grad = dot(grad_q, plain, 0, 0)
        output_grad = dot(joined, grad_branch, 0, 0)
        then(query_grad, output_grad)
        down_back = in_order(take_all(down_back), "z", ZN)
        grad_k = rotate(sum(take_all(key_sent), key_first[0]), -1.0)
        grad_value_own = sum(take_all(value_sent), value_first[0])
        every = reduced(in_order(take_all(every_sent), "y", yn))
        every_sent = home_along(every, "k", KN)
        query_first, output_first = (
            cut(after(g, grad_k, grad_value_own)) for g in (query_grad, output_grad)
        )
        query_sent = square_back(query_first, "x", sizes)
        output_sent = square_back(output_first, "y", sizes)
        key_grad = then(dot(grad_k, plain, 0, 0))
        key_first = cut(key_grad)
        key_sent = square_back(key_first, "x", sizes)
        value_grad = then(dot(grad_value_own, plain, 0, 0))
        value_first = cut(value_grad)
        value_sent = square_back(value_first, "y", sizes)
        grad_qk = now(jnp.concatenate([grad_q, grad_k], axis=1))
        grad_part = then(dot(grad_qk, wqk) + dot(grad_value_own, wv))
        grad_attn_sent = group_sum(grad_part)

        every = in_order(take_all(every_sent), "k", KN)
        every = jnp.concatenate([every[:, :2].reshape(1, -1), jnp.sum(every[:, 2:], axis=0, keepdims=True)], axis=1)
        every_sent = home_along(every, "z", ZN)
        top_grad = sum(take_all(top_sent), top_first[0])
        low_grad = sum(take_all(low_sent), low_first[0])
        gate_back = back_along_z([jnp.concatenate([top_grad, low_grad])])
        query_first = square_added(query_first, take_all(query_sent), "x", sizes)
        query_sent = square_back_on(query_first, "y", sizes)
        output_first = square_added(output_first, take_all(output_sent), "y", sizes)
        output_sent = square_back_on(output_first, "x", sizes)
        then(*query_first, *output_first)
        key_first = square_added(key_first, take_all(key_sent), "x", sizes)
        key_sent = square_back_on(key_first, "y", sizes)
        value_first = square_added(value_first, take_all(value_sent), "y", sizes)
        value_sent = square_back_on(value_first, "x", sizes)
        then(*key_first, *value_first)
        every = in_order(take_all(every_sent), "z", ZN)
        up_back = in_order(take_all(up_back), "z", ZN)
        out_sum = take(out_sent)
        output = residual + out_sum
        out_sent = home_along(from_distance_x(output), "y", yn)
        query_grad = sum(take_all(query_sent), query_first[0])
        output_grad = sum(take_all(output_sent), output_first[0])
        early_sent = back_along_z([query_grad, output_grad])
        grad_down, grad_up = (v.T for v in now(down_back, up_back))
        then(grad_down, grad_up)
        key_grad = sum(take_all(key_sent), key_first[0])
        value_grad = sum(take_all(value_sent), value_first[0])
        late_sent = back_along_z([key_grad, value_grad])
        grad_gate = then(in_order(take_all(gate_back), "z", ZN).T)
        out_sent = home_along(in_order(take_all(out_sent), "y", yn), "k", KN)
        ffn_gain_part = then(rowsum(w_gate, grad_gate) + rowsum(w_up, grad_up))
        scaled = take(grad_attn_sent)
        grad_mine = grad_residual_attn + scale * (
            scaled - plain_mine * jnp.mean(scaled * plain_mine, axis=1, keepdims=True)
        )
        grad_mine = then(from_distance_x(from_distance_y(grad_mine)))
        tokens_sent = home_along(grad_mine, "y", yn)
        output = then(homed(in_order(take_all(out_sent), "k", KN)))
        early = in_order(take_all(early_sent), "z", ZN)
        early_sent = exchanged(early, "y", yn)
        tokens_sent = home_along(in_order(take_all(tokens_sent), "y", yn), "k", KN)
        late = in_order(take_all(late_sent), "z", ZN)
        late_sent = exchanged(late, "y", yn)
        grad_tokens = then(homed(in_order(take_all(tokens_sent), "k", KN)))
        by_block = lambda v, mats: v.reshape(BLOCKS, mats, 2 * HD, part_rows)
        held_w, held_early, held_late = by_block(attn_y, 3), by_block(early, 2), by_block(late, 2)
        attn_gain_part = (
            jnp.sum(held_w[:, 0] * held_early[:, 0], axis=(0, 1))
            + jnp.sum(held_w[:, 1] * held_late[:, 0], axis=(0, 1))
            + jnp.sum(held_w[:, 2] * held_late[:, 1], axis=(0, 1))
        )
        gains = then(jnp.concatenate([attn_gain_part, ffn_gain_part]))[None]
        gains_sent = home_along(gains, "k", KN)
        early = in_order(take_all(early_sent), "y", yn, 1)
        grad_query, grad_output = unpacked(early, 2, sub)
        then(grad_query, grad_output)
        gains = jnp.sum(in_order(take_all(gains_sent), "k", KN), axis=0, keepdims=True)
        gains_sent = home_along(gains, "y", yn)
        sums = jnp.sum(every[:, 2 * KN :], axis=0)
        size = gain_head.shape[0]
        grad_head_gain = lax.dynamic_slice_in_dim(sums[:VD], (z * xn + x) * size, size)
        grad_mix = sums[VD:]
        peak = every[:, : 2 * KN].reshape(yn, sub, KN, 2)
        maxima = jnp.transpose(peak, (0, 2, 1, 3)).reshape(2 * HEADS)
        late = in_order(take_all(late_sent), "y", yn, 1)
        grad_key, grad_value = unpacked(late, 2, sub)
        gains = in_order(take_all(gains_sent), "y", yn)
        grad_attn_gain = gains[:, :part_rows].reshape(-1)
        grad_ffn_gain = jnp.sum(gains[:, part_rows:], axis=0)
        factor = jnp.sqrt(tau[0] / jnp.maximum(maxima, tau[0]))
        mine_factor = lax.dynamic_slice_in_dim(factor, (y * KN + k) * 2 * sub, 2 * sub)
        wide_factor = jnp.repeat(mine_factor, HD)[None, :]
        return (
            output, grad_tokens, grad_query * attn_gain, grad_key * attn_gain, grad_value * attn_gain,
            grad_output, grad_attn_gain, grad_mix, grad_head_gain, grad_gate * ffn_gain,
            grad_up * ffn_gain, grad_down, grad_ffn_gain, maxima,
            w_query * wide_factor, w_key * wide_factor,
        )

    return shards


def solution(mesh):
    xn, yn = mesh.shape["row"] // ZN, mesh.shape["col"] // KN
    split = Mesh(mesh.devices.reshape(ZN, xn, yn, KN), ("z", "x", "y", "k"))
    row, col = ("z", "x"), ("y", "k")
    rows, both, vector = P(row, None), P(row, col), P(row)
    return jax.shard_map(
        layer(xn, yn),
        mesh=split,
        in_specs=(rows, rows, both, both, both, both, vector, vector, vector, vector, vector, vector,
                  both, both, both, vector, P(), P(), vector),
        out_specs=(rows, rows, both, both, both, both, vector, P(), vector, both, both, both, vector,
                   P(), both, both),
        check_vma=False,
    )
```

time: 2640 us -> 1070 us (0.41)
  waiting for transfers between devices: 1850 us -> 399 us
  matrix products: 445 us -> 195 us
  starting transfers between devices: 1.24 us -> 183 us
  blocking collectives: 157 us -> 0 us
  Pallas kernels: 0 us -> 62.4 us
  other arithmetic: 53.9 us -> 100 us
    reduce_scatter x9 -> x4, waiting for transfers between devices: 1000 us -> 17.8 us  [group_sum(): return lax.psum_scatter(v, ('z', 'k'), scatter_dimension=0, tiled=True)]
    all_gather x9 -> x4, waiting for transfers between devices: 750 us -> 52.1 us  [group_gather(): return lax.all_gather(v, ('z', 'k'), axis=0, tiled=True)]
    ppermute x0 -> x107, waiting for transfers between devices: none -> 329 us  [the longest x104 329 us: shifted(): return lax.ppermute(v, axis, [(i, (i + shift) % n) for i in range(n)])]
    dot_general x67 -> x26, matrix products: 445 us -> 195 us  [the longest x10 124 us: fine(): lax.dot_general(a, b, (((contract_a,), (contract_b,)), ((), ())), precisi...]
    ppermute x0 -> x107, starting transfers between devices: none -> 182 us  [the longest x104 180 us: shifted(): return lax.ppermute(v, axis, [(i, (i + shift) % n) for i in range(n)])]
    psum x3 -> x0, waiting for transfers between devices: 95.4 us -> none  [the longest x1 56.8 us: shards(): grad_normed = lax.psum(grad_normed_part, 'col')]
    pallas_call x0 -> x2, Pallas kernels: none -> 62.4 us  [the longest x1 36.9 us: attend_back(): pl.pallas_call(lambda *refs: backward_kernel(run, *refs), grid=(count //...]
    unnamed x2 -> x0, blocking collectives: 60.2 us -> none
  transfers between devices with their start and end apart: 21 -> 115, of which waited for: 19 -> 44; matrix products, arithmetic and copies ran while one was open for 13% -> 25% of each run, Pallas kernels for 0% -> 6%
where the time goes in v1:
time: 1070 us; the launch traced here: 1060 us
  waiting for transfers between devices  399 us (37%)
  matrix products  195 us (18%)
  starting transfers between devices  183 us (17%)
  local copies, waits for them, and re-layouts  103 us (10%)
  other arithmetic  100 us (9%)
  Pallas kernels  62.4 us (6%)
  between operations  19.9 us (2%)
    ppermute x104, waiting for transfers between devices, shifted(): return lax.ppermute(v, axis, [(i, (i + shift) % n) for i in range(n)])  329 us
    ppermute x104, starting transfers between devices, shifted(): return lax.ppermute(v, axis, [(i, (i + shift) % n) for i in range(n)])  180 us
    dot_general x10, matrix products, fine(): lax.dot_general(a, b, (((contract_a,), (contract_b,)), ((), ())), precisi...  124 us
    dot_general x10, matrix products, dot(): lax.dot_general(a, b, (((contract_a,), (contract_b,)), ((), ())), precisi...  63.7 us
    unnamed x399, local copies, waits for them, and re-layouts  62.6 us
    all_gather x4, waiting for transfers between devices, group_gather(): return lax.all_gather(v, ('z', 'k'), axis=0, tiled=True)  52.1 us
    pallas_call x1, Pallas kernels, attend_back(): pl.pallas_call(lambda *refs: backward_kernel(run, *refs), grid=(count //...  36.9 us
    pallas_call x1, Pallas kernels, attend(): pl.pallas_call(lambda *refs: forward_kernel(run, *refs), grid=(count // T...  25.5 us
  transfers between devices with their start and end apart: 115, of which 44 were waited for; matrix products, arithmetic and copies ran while one was open for 25% of the time, Pallas kernels for 6%

profile of v1, /device:TPU:0, one launch (start us, length us, event | category | flops | bytes accessed | tf_op | source)
XLA Modules:
  0.0 1062.1 jit_solution(3542233672656784766)
XLA Ops:
  66.3 14.1 %collective-permute-done.6 = f32[768,128]{1,0:T(8,128)S(1)} collective-permute-done((f32[768,128]{1,0:T(8,128)S(1)}, f32[768,128]{1,0:T(8,128)S(1)}, u32[]{:S(2)}, u32[]{:S(2)}) %collective-permute-start.6) | collective-permute-done | bytes 393248 | tf_op jit(solution)/shard_map/ppermute | solution.py:68
  94.7 12.8 %collective-permute-done.10 = f32[384,512]{1,0:T(8,128)} collective-permute-done((f32[384,512]{1,0:T(8,128)}, f32[384,512]{1,0:T(8,128)}, u32[]{:S(2)}, u32[]{:S(2)}) %collective-permute-start.10) | collective-permute-done | bytes 786464 | tf_op jit(solution)/shard_map/ppermute | solution.py:68
  115.3 27.9 %all-gather.5.cloned.1.call-done = f32[640,2048]{1,0:T(8,128)} async-done(((f32[80,2048]{1,0:T(8,128)}), f32[640,2048]{1,0:T(8,128)}) %all-gather.5.cloned.1.call-update) | async-done | bytes 5242896 | tf_op jit(solution)/shard_map/all_gather | solution.py:508
  202.3 13.9 %collective-permute-start.15 = (f32[352,256]{1,0:T(8,128)S(1)}, f32[352,256]{1,0:T(8,128)S(1)}, u32[]{:S(2)}, u32[]{:S(2)}) collective-permute-start(f32[352,256]{1,0:T(8,128)S(1)} %get-tuple-element.626), channel_id=1, source_target_pairs={{0,8},{8,16},{16,24},{24,0},{1,9},{9,17},{17,25},{25,1},{2,10},{10... | collective-permute-start | bytes 1081352 | tf_op jit(solution)/shard_map/ppermute | solution.py:68
  226.6 14.0 %collective-permute-start.17 = (f32[352,256]{1,0:T(8,128)S(1)}, f32[352,256]{1,0:T(8,128)S(1)}, u32[]{:S(2)}, u32[]{:S(2)}) collective-permute-start(f32[352,256]{1,0:T(8,128)S(1)} %get-tuple-element.624), channel_id=1, source_target_pairs={{0,24},{8,0},{16,8},{24,16},{1,25},{9,1},{17,9},{25,17},{2,26},{10... | collective-permute-start | bytes 1081352 | tf_op jit(solution)/shard_map/ppermute | solution.py:68
  260.3 25.5 %attend.1 = (f32[640,256]{1,0:T(8,128)}, f32[8,640]{1,0:T(8,128)}) custom-call(f32[1]{0:T(128)} %bitcast.4.refs_0_, s32[50]{0:T(128)} %reshape.597.refs_1_, s32[5]{0:T(128)} %convert_reduce_fusion.2.refs_2_, s32[160]{0:T(256)} %add.906.refs_3_, s32[40]{0:T(128)} %add.913.refs_4_, f32[640,256]{1,0:T(8,128)} %fusion.20.refs_5_, f32[2560,256]{1,0:T(8,128)} %copy-done.93, ...), custom_call_target="tpu_custom_call" | custom-call | flops 40000000000 | tf_op jit(solution)/shard_map/attend/pallas_call | solution.py:393
  301.6 25.2 %collective-permute-done.36 = f32[352,1024]{1,0:T(8,128)S(1)} collective-permute-done((f32[352,1024]{1,0:T(8,128)}, f32[352,1024]{1,0:T(8,128)S(1)}, u32[]{:S(2)}, u32[]{:S(2)}) %collective-permute-start.36) | collective-permute-done | bytes 1441824 | tf_op jit(solution)/shard_map/ppermute | solution.py:68
  331.9 19.8 %collective-permute-done.39 = f32[352,1024]{1,0:T(8,128)S(1)} collective-permute-done((f32[352,1024]{1,0:T(8,128)S(1)}, f32[352,1024]{1,0:T(8,128)S(1)}, u32[]{:S(2)}, u32[]{:S(2)}) %collective-permute-start.39) | collective-permute-done | bytes 1441824 | tf_op jit(solution)/shard_map/ppermute | solution.py:68
  352.9 17.8 %reduce-scatter.5.cloned.1.call-done = f32[80,2048]{1,0:T(8,128)} async-done(((f32[640,2048]{1,0:T(8,128)}), f32[80,2048]{1,0:T(8,128)}) %reduce-scatter.5.cloned.1.call-update) | async-done | bytes 655376 | tf_op jit(solution)/shard_map/reduce_scatter | solution.py:511
  390.8 17.0 %collective-permute-done.40 = f32[176,1024]{1,0:T(8,128)S(1)} collective-permute-done((f32[176,1024]{1,0:T(8,128)S(1)}, f32[176,1024]{1,0:T(8,128)S(1)}, u32[]{:S(2)}, u32[]{:S(2)}) %collective-permute-start.40) | collective-permute-done | bytes 720928 | tf_op jit(solution)/shard_map/ppermute | solution.py:68
  407.9 12.5 %collective-permute-done.44 = f32[176,1024]{1,0:T(8,128)S(1)} collective-permute-done((f32[176,1024]{1,0:T(8,128)S(1)}, f32[176,1024]{1,0:T(8,128)S(1)}, u32[]{:S(2)}, u32[]{:S(2)}) %collective-permute-start.44) | collective-permute-done | bytes 720928 | tf_op jit(solution)/shard_map/ppermute | solution.py:68
  422.5 13.1 %collective-permute-done.46 = f32[176,1024]{1,0:T(8,128)S(1)} collective-permute-done((f32[176,1024]{1,0:T(8,128)S(1)}, f32[176,1024]{1,0:T(8,128)S(1)}, u32[]{:S(2)}, u32[]{:S(2)}) %collective-permute-start.46) | collective-permute-done | bytes 720928 | tf_op jit(solution)/shard_map/ppermute | solution.py:68
  436.5 14.2 %collective-permute-done.45 = f32[352,1024]{1,0:T(8,128)} collective-permute-done((f32[352,1024]{1,0:T(8,128)S(1)}, f32[352,1024]{1,0:T(8,128)}, u32[]{:S(2)}, u32[]{:S(2)}) %collective-permute-start.45) | collective-permute-done | bytes 1441824 | tf_op jit(solution)/shard_map/ppermute | solution.py:68
  454.4 19.0 %fusion.7 = f32[704,640]{1,0:T(8,128)} fusion(f32[640,2048]{1,0:T(8,128)} %all-gather.7.cloned.1.call-done, f32[352,1024]{1,0:T(8,128)} %collective-permute-done.45, f32[352,1024]{1,0:T(8,128)} %copy-done.116, f32[352,1024]{1,0:T(8,128)} %collective-permute-done.37, f32[352,1024]{1,0:T(8,128)} %copy-done.62), kind=kOutput, calls=%fused_computation.13 | convolution fusion | flops 11077287936 | bytes 12812288 | tf_op jit(solution)/shard_map/dot_general | solution.py:37
  481.9 15.6 %fusion.24 = f32[704,640]{1,0:T(8,128)} fusion(f32[640,2048]{1,0:T(8,128)S(1)} %copy-done.7, f32[176,1024]{1,0:T(8,128)S(1)} %collective-permute-done.47, f32[176,1024]{1,0:T(8,128)S(1)} %collective-permute-done.42, f32[176,1024]{1,0:T(8,128)S(1)} %copy-done.125, f32[176,1024]{1,0:T(8,128)S(1)} %collective-permute-done.41, ...), kind=kOutput, calls=%fused_computation.132 | convolution fusion | flops 11083055104 | bytes 12812288 | tf_op jit(solution)/shard_map/dot_general | solution.py:37
  497.5 11.6 %all-gather.9.cloned.1.call-done = f32[640,2048]{1,0:T(8,128)} async-done(((f32[80,2048]{1,0:T(8,128)}), f32[640,2048]{1,0:T(8,128)}) %all-gather.9.cloned.1.call-update) | async-done | bytes 5242896 | tf_op jit(solution)/shard_map/all_gather | solution.py:508
  509.0 26.3 %fusion.48 = (f32[704,640]{1,0:T(8,128)S(1)}, f32[704,640]{1,0:T(8,128)S(1)}, f32[704,640]{1,0:T(8,128)}) fusion(f32[704,640]{1,0:T(8,128)} %fusion.24, f32[704,640]{1,0:T(8,128)} %fusion.7, f32[640,2048]{1,0:T(8,128)} %all-gather.9.cloned.1.call-done, f32[352,1024]{1,0:T(8,128)} %copy-done.114, f32[352,1024]{1,0:T(8,128)} %copy-done.112, ...), kind=kOutput, calls=%fused_computation.433 | convolution fusion | flops 11082694656 | bytes 20021248 | tf_op jit(solution)/shard_map/dot_general | solution.py:37
  535.4 16.6 %fusion.6 = f32[640,2048]{1,0:T(8,128)} fusion(f32[704,640]{1,0:T(8,128)S(1)} %get-tuple-element.331, f32[352,1024]{1,0:T(8,128)} %collective-permute-done.45, f32[352,1024]{1,0:T(8,128)S(1)} %copy-done.117, f32[352,1024]{1,0:T(8,128)} %collective-permute-done.37, f32[352,1024]{1,0:T(8,128)S(1)} %copy-done.63), kind=kOutput, calls=%fused_computation.12 | convolution fusion | flops 11077287936 | bytes 12812288 | tf_op jit(solution)/shard_map/dot_general | solution.py:37
  552.0 19.6 %convolution_add_fusion = f32[640,2048]{1,0:T(8,128)} fusion(f32[640,2048]{1,0:T(8,128)} %fusion.6, f32[704,640]{1,0:T(8,128)S(1)} %get-tuple-element.332, f32[176,1024]{1,0:T(8,128)} %copy-done.128, f32[176,1024]{1,0:T(8,128)} %copy-done.127, f32[176,1024]{1,0:T(8,128)} %copy-done.124, f32[176,1024]{1,0:T(8,128)} %copy-done.126, ...), kind=kOutput, calls=%fused_computation.14 | convolution fusion | flops 11084365824 | bytes 18055168 | tf_op jit(solution)/shard_map/dot_general | solution.py:37
  571.7 9.9 fusion.137
  598.6 9.1 fusion.139
  607.7 10.7 %fusion.117 = f32[640,2048]{1,0:T(8,128)} fusion(f32[704,640]{1,0:T(8,128)S(1)} %copy-done.44, f32[352,1024]{1,0:T(8,128)S(1)} %copy-done.115, f32[352,1024]{1,0:T(8,128)S(1)} %copy-done.113, f32[352,1024]{1,0:T(8,128)S(1)} %copy-done.111, f32[352,1024]{1,0:T(8,128)S(1)} %copy-done.61), kind=kOutput, calls=%fused_computation.690 | convolution fusion | flops 5540806656 | bytes 12812288 | tf_op jit(solution)/shard_map/dot_general | solution.py:31
  619.1 11.8 %collective-permute-done.49 = f32[352,1024]{1,0:T(8,128)} collective-permute-done((f32[352,1024]{1,0:T(8,128)}, f32[352,1024]{1,0:T(8,128)}, u32[]{:S(2)}, u32[]{:S(2)}) %collective-permute-start.49) | collective-permute-done | bytes 1441824 | tf_op jit(solution)/shard_map/ppermute | solution.py:68
  650.4 25.8 %collective-permute-done.50 = f32[352,1024]{1,0:T(8,128)} collective-permute-done((f32[352,1024]{1,0:T(8,128)}, f32[352,1024]{1,0:T(8,128)}, u32[]{:S(2)}, u32[]{:S(2)}) %collective-permute-start.50) | collective-permute-done | bytes 1441824 | tf_op jit(solution)/shard_map/ppermute | solution.py:68
  682.7 12.7 %all-gather.11.cloned.1.call-done = f32[640,2048]{1,0:T(8,128)} async-done(((f32[80,2048]{1,0:T(8,128)}), f32[640,2048]{1,0:T(8,128)}) %all-gather.11.cloned.1.call-update) | async-done | bytes 5242896 | tf_op jit(solution)/shard_map/all_gather | solution.py:508
  711.2 36.9 %attend_back.1 = (f32[640,256]{1,0:T(8,128)}, f32[2560,256]{1,0:T(8,128)}, f32[2560,256]{1,0:T(8,128)}, f32[8,640]{1,0:T(8,128)}) custom-call(f32[1]{0:T(128)} %bitcast.4.refs_0_, s32[50]{0:T(128)} %reshape.597.refs_1_, s32[5]{0:T(128)} %convert_reduce_fusion.2.refs_2_, s32[160]{0:T(256)} %add.906.refs_3_, s32[40]{0:T(128)} %add.913.refs_4_, ...), custom_call_target="tpu_custom_call" | custom-call | flops 40000000000 | tf_op jit(solution)/shard_map/attend_back/pallas_call | solution.py:418
  769.8 9.8 collective-permute-done.61
  781.1 11.0 %collective-permute-done.63 = f32[176,1024]{1,0:T(8,128)} collective-permute-done((f32[176,1024]{1,0:T(8,128)}, f32[176,1024]{1,0:T(8,128)}, u32[]{:S(2)}, u32[]{:S(2)}) %collective-permute-start.63) | collective-permute-done | bytes 720928 | tf_op jit(solution)/shard_map/ppermute | solution.py:68
  809.8 10.2 collective-permute-done.65
  874.9 26.5 %collective-permute-done.80 = f32[176,1024]{1,0:T(8,128)S(1)} collective-permute-done((f32[176,1024]{1,0:T(8,128)}, f32[176,1024]{1,0:T(8,128)S(1)}, u32[]{:S(2)}, u32[]{:S(2)}) %collective-permute-start.80) | collective-permute-done | bytes 720928 | tf_op jit(solution)/shard_map/ppermute | solution.py:68
  974.9 10.3 collective-permute-start.96
  1012.4 14.1 %collective-permute-done.95 = f32[80,2048]{1,0:T(8,128)S(1)} collective-permute-done((f32[80,2048]{1,0:T(8,128)S(1)}, f32[80,2048]{1,0:T(8,128)S(1)}, u32[]{:S(2)}, u32[]{:S(2)}) %collective-permute-start.95) | collective-permute-done | bytes 655392 | tf_op jit(solution)/shard_map/ppermute | solution.py:68
  (864 shorter events, 507.0 us)
Async XLA Ops:
  7.2 136.0 %all-gather.5.cloned.1.call-start = ((), (), s32[]{:S(2)}) async-start(), calls=%async_computation.4 | async-start | bytes 5898240 | tf_op jit(solution)/shard_map/all_gather | solution.py:508
  12.2 36.1 %collective-permute-start.4 = (f32[1536,128]{1,0:T(8,128)}, f32[1536,128]{1,0:T(8,128)}, u32[]{:S(2)}, u32[]{:S(2)}) collective-permute-start(f32[1536,128]{1,0:T(8,128)} %get-tuple-element.584), channel_id=1, source_target_pairs={{0,2},{2,0},{1,3},{3,1},{4,6},{6,4},{5,7},{7,5},{8,10},{10,8},{9,1... | collective-permute-start | bytes 2359304 | tf_op jit(solution)/shard_map/ppermute | solution.py:68
  81.9 288.8 %reduce-scatter.5.cloned.1.call-start = ((), (), s32[]{:S(2)}) async-start(), calls=%async_computation.5 | async-start | bytes 5898240 | tf_op jit(solution)/shard_map/reduce_scatter | solution.py:511
  94.1 49.0 %collective-permute-start.11 = (f32[384,512]{1,0:T(8,128)}, f32[384,512]{1,0:T(8,128)}, u32[]{:S(2)}, u32[]{:S(2)}) collective-permute-start(f32[384,512]{1,0:T(8,128)} %get-tuple-element.245), channel_id=1, source_target_pairs={{0,2},{2,0},{1,3},{3,1},{4,6},{6,4},{5,7},{7,5},{8,10},{10,8},{9,1... | collective-permute-start | bytes 2359304 | tf_op jit(solution)/shard_map/ppermute | solution.py:68
  107.4 35.7 %collective-permute-start.12 = (f32[384,512]{1,0:T(8,128)}, f32[384,512]{1,0:T(8,128)}, u32[]{:S(2)}, u32[]{:S(2)}) collective-permute-start(f32[384,512]{1,0:T(8,128)} %collective-permute-done.10), channel_id=1, source_target_pairs={{0,2},{2,0},{1,3},{3,1},{4,6},{6,4},{5,7},{7,5},{8,10},{10,8},{9,1... | collective-permute-start | bytes 2359304 | tf_op jit(solution)/shard_map/ppermute | solution.py:68
  110.3 37.7 %collective-permute-start.13 = (f32[384,512]{1,0:T(8,128)}, f32[384,512]{1,0:T(8,128)}, u32[]{:S(2)}, u32[]{:S(2)}) collective-permute-start(f32[384,512]{1,0:T(8,128)} %get-tuple-element.249), channel_id=1, source_target_pairs={{0,4},{4,0},{1,5},{5,1},{2,6},{6,2},{3,7},{7,3},{8,12},{12,8},{9,1... | collective-permute-start | bytes 2359304 | tf_op jit(solution)/shard_map/ppermute | solution.py:68
  111.9 36.1 %collective-permute-start.14 = (f32[384,512]{1,0:T(8,128)S(1)}, f32[384,512]{1,0:T(8,128)}, u32[]{:S(2)}, u32[]{:S(2)}) collective-permute-start(f32[384,512]{1,0:T(8,128)S(1)} %collective-permute-done.9), channel_id=1, source_target_pairs={{0,4},{4,0},{1,5},{5,1},{2,6},{6,2},{3,7},{7,3},{8,12},{12,8},{9,1... | collective-permute-start | bytes 2359304 | tf_op jit(solution)/shard_map/ppermute | solution.py:68
  202.3 40.5 %collective-permute-start.15 = (f32[352,256]{1,0:T(8,128)S(1)}, f32[352,256]{1,0:T(8,128)S(1)}, u32[]{:S(2)}, u32[]{:S(2)}) collective-permute-start(f32[352,256]{1,0:T(8,128)S(1)} %get-tuple-element.626), channel_id=1, source_target_pairs={{0,8},{8,16},{16,24},{24,0},{1,9},{9,17},{17,25},{25,1},{2,10},{10... | collective-permute-start | bytes 1081352 | tf_op jit(solution)/shard_map/ppermute | solution.py:68
  241.2 44.6 %collective-permute-start.34 = (f32[352,256]{1,0:T(8,128)}, f32[352,256]{1,0:T(8,128)S(1)}, u32[]{:S(2)}, u32[]{:S(2)}) collective-permute-start(f32[352,256]{1,0:T(8,128)} %get-tuple-element.629), channel_id=1, source_target_pairs={{0,16},{8,24},{16,0},{24,8},{1,17},{9,25},{17,1},{25,9},{2,18},{10... | collective-permute-start | bytes 1081352 | tf_op jit(solution)/shard_map/ppermute | solution.py:68
  242.8 43.1 %collective-permute-start.35 = (f32[352,256]{1,0:T(8,128)}, f32[352,256]{1,0:T(8,128)S(1)}, u32[]{:S(2)}, u32[]{:S(2)}) collective-permute-start(f32[352,256]{1,0:T(8,128)} %get-tuple-element.628), channel_id=1, source_target_pairs={{0,24},{8,0},{16,8},{24,16},{1,25},{9,1},{17,9},{25,17},{2,26},{10... | collective-permute-start | bytes 1081352 | tf_op jit(solution)/shard_map/ppermute | solution.py:68
  248.2 38.5 %collective-permute-start.30 = (f32[256,512]{0,1:T(8,128)S(1)}, f32[256,512]{0,1:T(8,128)S(1)}, u32[]{:S(2)}, u32[]{:S(2)}) collective-permute-start(f32[256,512]{0,1:T(8,128)S(1)} %pad_maximum_fusion.18), channel_id=1, source_target_pairs={{0,2},{2,0},{4,6},{6,4},{1,3},{3,1},{5,7},{7,5},{8,10},{10,8},{12,... | collective-permute-start | bytes 1572872 | tf_op jit(solution)/shard_map/ppermute | solution.py:118
  295.4 155.3 %all-gather.7.cloned.1.call-start = ((), (), s32[]{:S(2)}) async-start(), calls=%async_computation.6 | async-start | bytes 5898240 | tf_op jit(solution)/shard_map/all_gather | solution.py:508
  385.7 123.3 %all-gather.9.cloned.1.call-start = ((), (), s32[]{:S(2)}) async-start(), calls=%async_computation.7 | async-start | bytes 5898240 | tf_op jit(solution)/shard_map/all_gather | solution.py:508
  385.7 34.7 %collective-permute-start.43 = (f32[352,1024]{1,0:T(8,128)}, f32[352,1024]{1,0:T(8,128)S(1)}, u32[]{:S(2)}, u32[]{:S(2)}) collective-permute-start(f32[352,1024]{1,0:T(8,128)} %copy-done.62), channel_id=1, source_target_pairs={{0,2},{2,0},{1,3},{3,1},{4,6},{6,4},{5,7},{7,5},{8,10},{10,8},{9,1... | collective-permute-start | bytes 4325384 | tf_op jit(solution)/shard_map/ppermute | solution.py:68
  450.7 186.7 %reduce-scatter.7.cloned.1.call-start = ((), (), s32[]{:S(2)}) async-start(), calls=%async_computation.8 | async-start | bytes 5898240 | tf_op jit(solution)/shard_map/reduce_scatter | solution.py:511
  571.6 123.7 %all-gather.11.cloned.1.call-start = ((), (), s32[]{:S(2)}) async-start(), calls=%async_computation.9 | async-start | bytes 5898240 | tf_op jit(solution)/shard_map/all_gather | solution.py:508
  641.3 313.7 %reduce-scatter.9.cloned.1.call-start = ((), (), s32[]{:S(2)}) async-start(), calls=%async_computation.10 | async-start | bytes 5898240 | tf_op jit(solution)/shard_map/reduce_scatter | solution.py:511
  641.3 34.9 %collective-permute-start.50 = (f32[352,1024]{1,0:T(8,128)}, f32[352,1024]{1,0:T(8,128)}, u32[]{:S(2)}, u32[]{:S(2)}) collective-permute-start(f32[352,1024]{1,0:T(8,128)} %get-tuple-element.541), channel_id=1, source_target_pairs={{0,4},{4,0},{1,5},{5,1},{2,6},{6,2},{3,7},{7,3},{8,12},{12,8},{9,1... | collective-permute-start | bytes 4325384 | tf_op jit(solution)/shard_map/ppermute | solution.py:68
  642.0 37.5 %collective-permute-start.51 = (f32[352,1024]{1,0:T(8,128)}, f32[352,1024]{1,0:T(8,128)}, u32[]{:S(2)}, u32[]{:S(2)}) collective-permute-start(f32[352,1024]{1,0:T(8,128)} %get-tuple-element.539), channel_id=1, source_target_pairs={{0,2},{2,0},{1,3},{3,1},{4,6},{6,4},{5,7},{7,5},{8,10},{10,8},{9,1... | collective-permute-start | bytes 4325384 | tf_op jit(solution)/shard_map/ppermute | solution.py:68
  648.7 58.4 %collective-permute-start.52 = (f32[352,1024]{1,0:T(8,128)}, f32[352,1024]{1,0:T(8,128)}, u32[]{:S(2)}, u32[]{:S(2)}) collective-permute-start(f32[352,1024]{1,0:T(8,128)} %slice_add_fusion.2), channel_id=1, source_target_pairs={{0,4},{4,0},{1,5},{5,1},{2,6},{6,2},{3,7},{7,3},{8,12},{12,8},{9,1... | collective-permute-start | bytes 4325384 | tf_op jit(solution)/shard_map/ppermute | solution.py:68
  650.1 55.4 %collective-permute-start.53 = (f32[352,1024]{1,0:T(8,128)}, f32[352,1024]{1,0:T(8,128)}, u32[]{:S(2)}, u32[]{:S(2)}) collective-permute-start(f32[352,1024]{1,0:T(8,128)} %slice_add_fusion.3), channel_id=1, source_target_pairs={{0,2},{2,0},{1,3},{3,1},{4,6},{6,4},{5,7},{7,5},{8,10},{10,8},{9,1... | collective-permute-start | bytes 4325384 | tf_op jit(solution)/shard_map/ppermute | solution.py:68
  695.4 302.1 %reduce-scatter.11.cloned.1.call-start = ((), (), s32[]{:S(2)}) async-start(), calls=%async_computation.11 | async-start | bytes 5898240 | tf_op jit(solution)/shard_map/reduce_scatter | solution.py:511
  709.8 56.9 %collective-permute-start.60 = (f32[176,1024]{1,0:T(8,128)}, f32[176,1024]{1,0:T(8,128)}, u32[]{:S(2)}, u32[]{:S(2)}) collective-permute-start(f32[176,1024]{1,0:T(8,128)} %get-tuple-element.347), channel_id=1, source_target_pairs={{0,4},{4,0},{1,5},{5,1},{2,6},{6,2},{3,7},{7,3},{8,12},{12,8},{9,1... | collective-permute-start | bytes 2162696 | tf_op jit(solution)/shard_map/ppermute | solution.py:68
  764.4 34.3 %collective-permute-start.58 = (f32[640,256]{1,0:T(8,128)}, f32[640,256]{1,0:T(8,128)}, u32[]{:S(2)}, u32[]{:S(2)}) collective-permute-start(f32[640,256]{1,0:T(8,128)} %get-tuple-element.553), channel_id=1, source_target_pairs={{0,4},{4,0},{1,5},{5,1},{2,6},{6,2},{3,7},{7,3},{8,12},{12,8},{9,1... | collective-permute-start | bytes 1966088 | tf_op jit(solution)/shard_map/ppermute | solution.py:68
  766.6 39.0 %collective-permute-start.59 = (f32[640,256]{1,0:T(8,128)}, f32[640,256]{1,0:T(8,128)}, u32[]{:S(2)}, u32[]{:S(2)}) collective-permute-start(f32[640,256]{1,0:T(8,128)} %get-tuple-element.552), channel_id=1, source_target_pairs={{0,4},{4,0},{1,5},{5,1},{2,6},{6,2},{3,7},{7,3},{8,12},{12,8},{9,1... | collective-permute-start | bytes 1966088 | tf_op jit(solution)/shard_map/ppermute | solution.py:68
  779.6 48.7 %collective-permute-start.69 = (f32[352,256]{1,0:T(8,128)}, f32[352,256]{1,0:T(8,128)S(1)}, u32[]{:S(2)}, u32[]{:S(2)}) collective-permute-start(f32[352,256]{1,0:T(8,128)} %get-tuple-element.608), channel_id=1, source_target_pairs={{0,8},{8,16},{16,24},{24,0},{1,9},{9,17},{17,25},{25,1},{2,10},{10... | collective-permute-start | bytes 1081352 | tf_op jit(solution)/shard_map/ppermute | solution.py:68
  862.7 38.7 %collective-permute-start.78 = (f32[256,512]{1,0:T(8,128)}, f32[256,512]{1,0:T(8,128)S(1)}, u32[]{:S(2)}, u32[]{:S(2)}) collective-permute-start(f32[256,512]{1,0:T(8,128)} %get-tuple-element.567), channel_id=1, source_target_pairs={{0,4},{4,0},{1,5},{5,1},{2,6},{6,2},{3,7},{7,3},{8,12},{12,8},{9,1... | collective-permute-start | bytes 1572872 | tf_op jit(solution)/shard_map/ppermute | solution.py:68
  863.2 38.7 %collective-permute-start.79 = (f32[256,512]{1,0:T(8,128)}, f32[256,512]{1,0:T(8,128)S(1)}, u32[]{:S(2)}, u32[]{:S(2)}) collective-permute-start(f32[256,512]{1,0:T(8,128)} %get-tuple-element.566), channel_id=1, source_target_pairs={{0,4},{4,0},{1,5},{5,1},{2,6},{6,2},{3,7},{7,3},{8,12},{12,8},{9,1... | collective-permute-start | bytes 1572872 | tf_op jit(solution)/shard_map/ppermute | solution.py:68
  864.7 36.6 %collective-permute-start.80 = (f32[176,1024]{1,0:T(8,128)}, f32[176,1024]{1,0:T(8,128)S(1)}, u32[]{:S(2)}, u32[]{:S(2)}) collective-permute-start(f32[176,1024]{1,0:T(8,128)} %get-tuple-element.375), channel_id=1, source_target_pairs={{0,4},{4,0},{1,5},{5,1},{2,6},{6,2},{3,7},{7,3},{8,12},{12,8},{9,1... | collective-permute-start | bytes 2162696 | tf_op jit(solution)/shard_map/ppermute | solution.py:68
  866.6 36.8 %collective-permute-start.82 = (f32[256,512]{1,0:T(8,128)}, f32[256,512]{1,0:T(8,128)}, u32[]{:S(2)}, u32[]{:S(2)}) collective-permute-start(f32[256,512]{1,0:T(8,128)} %get-tuple-element.563), channel_id=1, source_target_pairs={{0,2},{2,0},{1,3},{3,1},{4,6},{6,4},{5,7},{7,5},{8,10},{10,8},{9,1... | collective-permute-start | bytes 1572872 | tf_op jit(solution)/shard_map/ppermute | solution.py:68
  935.6 36.0 %collective-permute-start.90 = (f32[256,512]{1,0:T(8,128)}, f32[256,512]{1,0:T(8,128)}, u32[]{:S(2)}, u32[]{:S(2)}) collective-permute-start(f32[256,512]{1,0:T(8,128)} %get-tuple-element.554), channel_id=1, source_target_pairs={{0,4},{4,0},{1,5},{5,1},{2,6},{6,2},{3,7},{7,3},{8,12},{12,8},{9,1... | collective-permute-start | bytes 1572872 | tf_op jit(solution)/shard_map/ppermute | solution.py:68
  988.7 38.0 %collective-permute-start.100 = (f32[512,128]{1,0:T(8,128)}, f32[512,128]{1,0:T(8,128)}, u32[]{:S(2)}, u32[]{:S(2)}) collective-permute-start(f32[512,128]{1,0:T(8,128)} %get-tuple-element.668), channel_id=1, source_target_pairs={{0,8},{8,16},{16,24},{24,0},{1,9},{9,17},{17,25},{25,1},{2,10},{10... | collective-permute-start | bytes 786440 | tf_op jit(solution)/shard_map/ppermute | solution.py:68
  (220 other events, 3221.8 us)
Sparse Core Ops, SparseCore 0:
  82.0 61.0 all-gather.4
  295.5 75.1 reduce-scatter.4
  385.8 54.3 all-gather.6
  450.9 58.1 all-gather.8
  571.8 58.6 reduce-scatter.6
  641.4 53.8 all-gather.10
  697.6 58.6 reduce-scatter.8
  850.8 66.4 reduce-scatter.10

commit v2 on v1

--- a/solution.py
+++ b/solution.py
@@ -166,6 +166,113 @@
     return [shifted(sums[t], second, n, -t) for t in range(1, n)]
 
 
+def table_kernel(sizes, shape, parent_ref, at_ref, seen_ref, count_ref, key_ref, own_ref, code_ref, depth_ref, order, rank, own):
+    xn, yn, segs, run, pieces_run = sizes
+    slots, own_slots, padded_slots, tiles, chunks = shape
+    x, y = at_ref[0], at_ref[1]
+    per_chunk, per_tile = slots // chunks, padded_slots // tiles
+
+    def climb(s, carry):
+        def step(i, now):
+            above = parent_ref[now[0]]
+            return above, now[1] + (above != now[0]).astype(jnp.int32)
+
+        root, depth = lax.fori_loop(0, TRUNK_SEGS + 2, step, (s, jnp.int32(0)))
+        depth_ref[s] = depth
+        branch = jnp.where(depth == TRUNK_SEGS, s, parent_ref[s])
+        past = (branch + 1) * (slots + 1) + jnp.where(depth > TRUNK_SEGS, s + 1, 0)
+        place = jnp.where(depth < TRUNK_SEGS, depth, TRUNK_SEGS + past)
+        order[s] = (root * (TRUNK_SEGS + (slots + 1) * (slots + 2)) + place) * slots + s
+        return carry
+
+    lax.fori_loop(0, slots, climb, 0)
+
+    def place_slot(s, carry):
+        here, mine = jnp.int32(0), jnp.int32(0)
+        for t in range(slots):
+            less = (order[t] < order[s]).astype(jnp.int32)
+            here = here + less
+            mine = mine + less * (t // segs % xn == x).astype(jnp.int32)
+        rank[s] = here
+        own[s] = mine
+        zs = lax.div(s, xn * segs)
+        xs = lax.rem(lax.div(s, segs), xn)
+        for k in range(KN):
+            row = (zs * KN + k) * segs + lax.rem(s, segs)
+            for t in range(yn):
+                piece = lax.rem(x + xn - xs, xn) * yn + lax.rem(y + yn - t, yn)
+                key_ref[(here * yn + t) * KN + k] = piece * pieces_run + row
+
+            @pl.when(xs == x)
+            def _():
+                own_ref[mine * KN + k] = row
+
+        return carry
+
+    lax.fori_loop(0, slots, place_slot, 0)
+    for r in range(own_slots * KN, padded_slots * KN):
+        own_ref[r] = jnp.int32(r)
+
+    def clear(i, carry):
+        for j in range(padded_slots):
+            code_ref[i * padded_slots + j] = jnp.int32(0 if j < own_slots else 1)
+        return carry
+
+    lax.fori_loop(0, slots, clear, 0)
+
+    def mark(s, carry):
+        @pl.when(lax.rem(lax.div(s, segs), xn) == x)
+        def _():
+            def step(i, now):
+                code_ref[rank[now] * padded_slots + own[s]] = jnp.int32(1)
+                return parent_ref[now]
+
+            lax.fori_loop(0, TRUNK_SEGS + 2, step, parent_ref[s])
+            code_ref[rank[s] * padded_slots + own[s]] = jnp.int32(2)
+
+        return carry
+
+    lax.fori_loop(0, slots, mark, 0)
+
+    def visit(tile, carry):
+        def look(c, count):
+            some = jnp.int32(0)
+            for i in range(per_chunk):
+                for j in range(per_tile):
+                    at = tile * per_tile + j
+                    code = code_ref[(c * per_chunk + i) * padded_slots + at]
+                    some = some | jnp.where(at < own_slots, code, 0)
+
+            @pl.when(some > 0)
+            def _():
+                seen_ref[tile * chunks + count] = c
+
+            return count + (some > 0).astype(jnp.int32)
+
+        count_ref[tile] = lax.fori_loop(0, chunks, look, jnp.int32(0))
+        return carry
+
+    lax.fori_loop(0, tiles, visit, 0)
+
+
+def mask(code_ref, y, run, tile, c, chunk, padded_slots):
+    wide = KN * run
+    per_tile = TILE // wide
+    lane = lax.broadcasted_iota(jnp.int32, (1, TILE), 1)
+    row = lax.broadcasted_iota(jnp.int32, (SEG, TILE), 0)
+    which = lax.div(lane, wide)
+    offset = y * wide + lax.rem(lane, wide)
+    blocks = []
+    for i in range(chunk // SEG):
+        code = jnp.zeros((1, TILE), jnp.int32)
+        for j in range(per_tile):
+            one = code_ref[(c * (chunk // SEG) + i) * padded_slots + tile * per_tile + j]
+            code = jnp.where(which == j, one, code)
+        last = jnp.where(code == 0, -1, jnp.where(code == 1, SEG, offset))
+        blocks.append(jnp.where(row <= last, 0.0, -1e30).astype(f32))
+    return jnp.concatenate(blocks, axis=0)
+
+
 def logits_chunk(keys_wide, queries, rows, j):
     first, last = keys_wide[0, j, rows, :], keys_wide[1, j, rows, :]
     top, low, rest = queries[j]
@@ -210,7 +317,7 @@
 
 
 def forward_kernel(
-    run, mix_ref, seen_ref, count_ref, key_ref, own_ref, q_ref, k_ref, v_ref, bias_ref,
+    run, mix_ref, at_ref, seen_ref, count_ref, key_ref, own_ref, code_ref, q_ref, k_ref, v_ref,
     o_ref, stat_ref, keys_wide, vt, held, sorted_rows, sorted_q,
 ):
     total = k_ref.shape[0]
@@ -241,11 +348,15 @@
     split = split_queries(sorted_q[chunk_rows(tile, TILE), :])
     visits = count_ref[tile]
 
+    padded_slots = q_ref.shape[0] // (KN * run)
+
     def score(i, peaks):
-        rows = chunk_rows(seen_ref[tile * count + i], chunk)
+        c = seen_ref[tile * count + i]
+        rows = chunk_rows(c, chunk)
+        bias = mask(code_ref, at_ref[1], run, tile, c, chunk, padded_slots)
         out = []
         for j in range(2):
-            s = logits_chunk(keys_wide, split, rows, j) + bias_ref[rows, :]
+            s = logits_chunk(keys_wide, split, rows, j) + bias
             held[j, rows, :] = s
             out.append(jnp.maximum(peaks[j], jnp.max(s, axis=0, keepdims=True)))
         return tuple(out)
@@ -280,7 +391,7 @@
 
 
 def backward_kernel(
-    run, mix_ref, seen_ref, count_ref, key_ref, own_ref, q_ref, dc_ref, stat_ref, k_ref, v_ref, bias_ref,
+    run, mix_ref, at_ref, seen_ref, count_ref, key_ref, own_ref, code_ref, q_ref, dc_ref, stat_ref, k_ref, v_ref,
     dq_ref, dk_ref, dv_ref, inner_ref, keys_wide, kt, held, cross, sorted_v, sorted_q, sorted_dc,
 ):
     total = k_ref.shape[0]
@@ -318,9 +429,12 @@
     norms = [stat_ref[j : j + 1, :] for j in range(2)]
     visits = count_ref[tile]
 
+    padded_slots = q_ref.shape[0] // (KN * run)
+
     def first(i, inner):
-        rows = chunk_rows(seen_ref[tile * count + i], chunk)
-        bias = bias_ref[rows, :]
+        c = seen_ref[tile * count + i]
+        rows = chunk_rows(c, chunk)
+        bias = mask(code_ref, at_ref[1], run, tile, c, chunk, padded_slots)
         both = six(thirds(sorted_v[rows, :]), dct)
         cross[rows, :] = both
         out, probs = [], []
@@ -386,14 +500,28 @@
     return pl.BlockSpec(memory_space=pltpu.SMEM)
 
 
-def attend(run, mix, tables, queries, keys, values, bias):
+def tables_of(sizes, shape, parent_slot, place):
+    slots, own_slots, padded_slots, tiles, chunks = shape
+    yn = sizes[1]
+    counts = (tiles * chunks, tiles, slots * yn * KN, padded_slots * KN, slots * padded_slots, slots)
+    return pl.pallas_call(
+        lambda *refs: table_kernel(sizes, shape, *refs),
+        in_specs=[table()] * 2,
+        out_specs=[table()] * len(counts),
+        out_shape=[jax.ShapeDtypeStruct((n,), jnp.int32) for n in counts],
+        scratch_shapes=[pltpu.SMEM((slots,), jnp.int32)] * 3,
+        name="tables",
+    )(parent_slot, place)
+
+
+def attend(run, mix, tables, queries, keys, values):
     total, count = keys.shape[0], queries.shape[0]
     chunk = math.gcd(total, CHUNK)
     lanes = lambda rows: pl.BlockSpec((rows, TILE), lambda i: (0, i))
     return pl.pallas_call(
         lambda *refs: forward_kernel(run, *refs),
         grid=(count // TILE,),
-        in_specs=[table()] * 5 + [whole()] * 3 + [lanes(total)],
+        in_specs=[table()] * 7 + [whole()] * 3,
         out_specs=[whole(), lanes(8)],
         out_shape=[
             jax.ShapeDtypeStruct((count, VD), f32), jax.ShapeDtypeStruct((8, count), f32),
@@ -408,17 +536,17 @@
         compiler_params=pltpu.CompilerParams(vmem_limit_bytes=VMEM_BYTES),
         cost_estimate=pl.CostEstimate(flops=4 * 10**10, bytes_accessed=0, transcendentals=0),
         name="attend",
-    )(mix, *tables, queries, keys, values, bias)
-
-
-def attend_back(run, mix, tables, queries, contrast, stat, keys, values, bias):
+    )(mix, *tables, queries, keys, values)
+
+
+def attend_back(run, mix, tables, queries, contrast, stat, keys, values):
     total, count = keys.shape[0], queries.shape[0]
     chunk = math.gcd(total, CHUNK)
     lanes = lambda rows: pl.BlockSpec((rows, TILE), lambda i: (0, i))
     return pl.pallas_call(
         lambda *refs: backward_kernel(run, *refs),
         grid=(count // TILE,),
-        in_specs=[table()] * 5 + [whole()] * 2 + [lanes(8)] + [whole()] * 2 + [lanes(total)],
+        in_specs=[table()] * 7 + [whole()] * 2 + [lanes(8)] + [whole()] * 2,
         out_specs=[whole(), whole(), whole(), lanes(8)],
         out_shape=[
             jax.ShapeDtypeStruct((count, 2 * HD), f32),
@@ -438,7 +566,7 @@
         compiler_params=pltpu.CompilerParams(vmem_limit_bytes=VMEM_BYTES),
         cost_estimate=pl.CostEstimate(flops=4 * 10**10, bytes_accessed=0, transcendentals=0),
         name="attend_back",
-    )(mix, *tables, queries, contrast, stat, keys, values, bias)
+    )(mix, *tables, queries, contrast, stat, keys, values)
 
 
 def layer(xn, yn):
@@ -580,19 +708,44 @@
             [gain_head, lambda_query_first, lambda_key_first, lambda_query_second, lambda_key_second]
         )
         small_sent = home_along(small[None], "x", xn)
-        mine = piece(tokens)
-        scale = lax.rsqrt(jnp.mean(mine * mine, axis=1, keepdims=True) + epsilon)
-        plain_mine = then(to_distance_y(mine) * scale)
-        small = in_order(take_all(small_sent), "x", xn).reshape(1, -1)
-        small_sent = home_along(small, "z", ZN)
-        down_sent = w_down.T
-        then(down_sent)
-        small = in_order(take_all(small_sent), "z", ZN)
         attn_y = in_order(take_all(sent), "y", yn)
         y_gain = part(gain_attn, y, part_rows)[None, :]
         sent = exchanged(attn_y * y_gain, "z", ZN)
         output_sent = along_y(after(packed([w_output], sub), attn_y))
-        small = small.reshape(ZN * xn, -1)
+        sent[: 2] = take_all(sent[: 2])
+        padded = -(-group // TILE) * TILE
+        own_slots = ZN * segs
+        chunks = total // math.gcd(total, CHUNK)
+        *tables, depth_of = tables_of(
+            (xn, yn, segs, run, group // run),
+            (slot_total, own_slots, padded // (KN * run), padded // TILE, chunks),
+            now(parent_slot), jnp.stack([x, y]),
+        )
+        tables = [jnp.stack([x, y])] + tables
+        mine = piece(now(tokens))
+        scale = lax.rsqrt(jnp.mean(mine * mine, axis=1, keepdims=True) + epsilon)
+        plain_mine = then(to_distance_y(mine) * scale)
+        down_sent = now(w_down).T
+        then(down_sent, plain_mine, *tables)
+        small = in_order(take_all(small_sent), "x", xn).reshape(1, -1)
+        small_sent = home_along(small, "z", ZN)
+        output_y = in_order(take_all(output_sent), "y", yn)
+        shares = down_sent.shape[1] // part_rows
+        output_y = output_y.reshape(BLOCKS, shares, VD // shares, part_rows)
+        output_y = jnp.concatenate([output_y[:, i] for i in range(shares)], axis=2)
+        output_down = jnp.concatenate(
+            [output_y, down_sent.reshape(BLOCKS, -1, down_sent.shape[1])], axis=1
+        ).reshape(-1, down_sent.shape[1])
+        then(output_down)
+        attn_z = in_order(sent[:2] + take_all(sent[2:]), "z", ZN, 1)
+        upper, lower = halved(attn_z)
+        upper_out, lower_out = square_out(upper, "x", sizes), square_out(lower, "y", sizes)
+        upper_side, lower_side = side_out(upper, "x", sizes), side_out(lower, "y", sizes)
+        plain_sent = group_gather(after(plain_mine, attn_z))
+        upper_on = square_on(take_all(upper_out), "x", sizes, upper_side)
+        lower_on = square_on(take_all(lower_out), "y", sizes, lower_side)
+
+        small = in_order(take_all(small_sent), "z", ZN).reshape(ZN * xn, -1)
         n_gain, n_lambda = gain_head.shape[0], lambda_key_first.shape[0]
         head_gain = small[:, :n_gain].reshape(1, -1)
         query_first, key_first, query_second, key_second = (
@@ -604,88 +757,13 @@
             + lambda_init
         ).reshape(1)
 
-        slot_ids = jnp.arange(slot_total, dtype=jnp.int32)
-        same = slot_ids[:, None] == slot_ids[None, :]
-        reach = (same | (parent_slot[:, None] == slot_ids[None, :])).astype(f32)
-        for _ in range(4):
-            reach = (jnp.dot(reach, reach) > 0.5).astype(f32)
-        strict = jnp.where(same, 0.0, reach)
-        depth_of = jnp.sum(strict, axis=1)
-
-        ids = slot_ids.astype(f32)
-        root = jnp.sum(reach * jnp.where(depth_of == 0, ids, 0.0)[None, :], axis=1)
-        branch_slot = jnp.sum(reach * jnp.where(depth_of == TRUNK_SEGS, ids + 1.0, 0.0)[None, :], axis=1)
-        leaf = jnp.where(depth_of > TRUNK_SEGS, ids + 1.0, 0.0)
-        place = jnp.where(
-            depth_of < TRUNK_SEGS, depth_of, TRUNK_SEGS + branch_slot * (slot_total + 1) + leaf
-        )
-        ordinal = (root * (TRUNK_SEGS + (slot_total + 1) ** 2 + 1) + place).astype(jnp.int32)
-        before = (ordinal[None, :] < ordinal[:, None]) | (
-            (ordinal[None, :] == ordinal[:, None]) & (slot_ids[None, :] < slot_ids[:, None])
-        )
-        rank = jnp.sum(before, axis=1)
-        mine_too = slot_ids // segs % xn == x
-        own_rank = jnp.sum(before & mine_too[None, :], axis=1)
-        own_slots = ZN * segs
-        key_order = jnp.sum(jnp.where(rank[:, None] == slot_ids[None, :], slot_ids[:, None], 0), axis=0)
-        own_order = jnp.sum(
-            jnp.where(
-                (own_rank[:, None] == jnp.arange(own_slots)[None, :]) & mine_too[:, None],
-                slot_ids[:, None], 0,
-            ),
-            axis=0,
-        )
-
-        def run_at(slot, k_of):
-            return ((slot // (xn * segs)) * KN + k_of) * segs + slot % segs
-
-        ks = jnp.arange(KN, dtype=jnp.int32)
-        own_runs = run_at(own_order[:, None], ks[None, :]).reshape(-1)
-        ys = jnp.arange(yn, dtype=jnp.int32)[None, :, None]
-        slot = key_order[:, None, None]
-        piece_of = ((x + xn - slot // segs % xn) % xn) * yn + (y + yn - ys) % yn
-        key_runs = (piece_of * (group // run) + run_at(slot, ks[None, None, :])).reshape(-1)
-
-        padded = -(-group // TILE) * TILE
-        extra = padded - group
-        own_slot = jnp.repeat(own_order, group // own_slots)
-        own_offset = y * KN * run + jnp.arange(group, dtype=jnp.int32) % (KN * run)
-        key_slot, key_offset = jnp.repeat(key_order, SEG), jnp.arange(total, dtype=jnp.int32) % SEG
-        own_hot = (own_slot[:, None] == slot_ids[None, :]).astype(f32)
-        key_hot = (key_slot[:, None] == slot_ids[None, :]).astype(f32)
-        own_path = jnp.dot(own_hot, strict)
-        seen = jnp.dot(key_hot, own_path.T) > 0.5
-        seen = seen | (
-            (key_slot[:, None] == own_slot[None, :]) & (key_offset[:, None] <= own_offset[None, :])
-        )
-        seen = jnp.pad(seen, ((0, 0), (0, extra)))
-        own_runs = jnp.concatenate([own_runs, jnp.arange(group // run, padded // run, dtype=own_runs.dtype)])
-        bias = jnp.where(seen, 0.0, -1e30).astype(f32)
-        chunk = math.gcd(total, CHUNK)
-        chunks = total // chunk
-        slot_seen = (own_path + own_hot > 0.5).astype(f32)
-        slot_seen = jnp.pad(slot_seen, ((0, extra), (0, 0))).reshape(padded // TILE, TILE, slot_total)
-        slot_seen = jnp.max(slot_seen, axis=1)
-        in_chunk = (rank[:, None] * SEG // chunk == jnp.arange(chunks)[None, :]).astype(f32)
-        visited = jnp.dot(slot_seen, in_chunk) > 0.5
-        visits = jnp.sum(visited, axis=1).astype(jnp.int32)
-        turn = jnp.cumsum(visited, axis=1) - 1
-        listed = (turn[:, :, None] == jnp.arange(chunks)[None, None, :]) & visited[:, :, None]
-        listed = jnp.sum(jnp.where(listed, jnp.arange(chunks)[None, :, None], 0), axis=1)
-        tables = tuple(
-            v.reshape(-1).astype(jnp.int32) for v in (listed, visits, key_runs, own_runs)
-        )
-
         def padded_rows(v):
-            return jnp.pad(v, ((0, extra), (0, 0)))
+            return jnp.pad(v, ((0, padded - group), (0, 0)))
 
         shape = (ZN, KN, segs, run)
-        zs, ks, gs, rs = (lax.broadcasted_iota(jnp.int32, shape, d) for d in range(4))
-        lying_slot = ((zs * xn + x) * segs + gs).reshape(group)
-        own_hot = (lying_slot[:, None] == slot_ids[None, :]).astype(f32)
-        own_offset = ((y * KN + ks) * run + rs).reshape(group)
-        position = jnp.dot(own_hot, depth_of[:, None], precision=lax.Precision.HIGHEST) * SEG
-        position = position + own_offset[:, None].astype(f32)
+        ks, rs = (lax.broadcasted_iota(jnp.int32, shape, d) for d in (1, 3))
+        depths = at(depth_of.reshape(ZN, xn, segs), x, 1)[:, None, :, None]
+        position = (depths * SEG + (y * KN + ks) * run + rs).reshape(group, 1).astype(f32)
         half_dim = HD // 2
         frequency = jnp.exp(-rope_log_base * jnp.arange(half_dim, dtype=f32) / half_dim)
         angles = position * frequency[None, :]
@@ -697,24 +775,12 @@
             parts = [v[:, i * half_dim : (i + 1) * half_dim] for i in (1, 0, 3, 2)]
             return v * cosine + jnp.concatenate(parts, axis=1) * (sign * sine)
 
-        gate_up_sent = packed([w_up * ffn_gain, w_gate * ffn_gain], 1)
         cot_mine = piece(cotangent)
-        then(gate_up_sent, cot_mine, bias, cosine, sine, mix, *tables)
-        output_y = in_order(take_all(output_sent), "y", yn)
-        attn_z = in_order(take_all(sent), "z", ZN, 1)
-        upper, lower = halved(attn_z)
-        upper_out, lower_out = square_out(upper, "x", sizes), square_out(lower, "y", sizes)
-        upper_side, lower_side = side_out(upper, "x", sizes), side_out(lower, "y", sizes)
-        plain_sent = group_gather(after(plain_mine, attn_z))
-        upper_on = square_on(take_all(upper_out), "x", sizes, upper_side)
-        lower_on = square_on(take_all(lower_out), "y", sizes, lower_side)
-
-        plain = take(plain_sent)
-        up_sent, gate_sent = halved(gate_up_sent)
-        down_sent = exchanged(after(down_sent, plain), "z", ZN)
-        output_sent = exchanged(after(output_y, plain), "z", ZN)
         upper = joined_up(dict(zip(places, take_all([upper_on[p] for p in places]), strict=True)))
         lower = joined_up(dict(zip(places, take_all([lower_on[p] for p in places]), strict=True)))
+        plain = take(plain_sent)
+        down_sent = exchanged(after(output_down, plain), "z", ZN)
+        cot_sent = group_gather(after(cot_mine, plain))
         wqkv = jnp.concatenate([upper, lower])
         wqk, wv = wqkv[: 4 * HD], wqkv[4 * HD :]
         then(wqkv)
@@ -725,22 +791,31 @@
         value_sent = square_out(value_own, "y", sizes)
         queries = rotate(fine(now(plain), wqk[: 2 * HD], 1, 1), 1.0)
         queries = then(padded_rows(queries * logit_scale))
+        gate_up_sent = packed([now(w_up) * ffn_gain, now(w_gate) * ffn_gain], BLOCKS)
+        then(queries, gate_up_sent)
         key_sent = square_on(take_all(key_sent), "x", sizes)
         value_sent = square_on(take_all(value_sent), "y", sizes)
-        down_z = in_order(take_all(down_sent), "z", ZN, 1)
-        up_sent = exchanged(after(up_sent, queries), "z", ZN)
-        gate_sent = exchanged(after(gate_sent, down_z), "z", ZN)
-        output_z = in_order(take_all(output_sent), "z", ZN, 1)
+        came = take_all(down_sent)
+        output_rows = VD // shares
+        down_z = in_order([v[output_rows:] for v in came], "z", ZN, 1)
+        output_z = in_order(
+            [
+                jnp.concatenate([v[:output_rows, i * part_rows : (i + 1) * part_rows] for i in range(shares)])
+                for v in came
+            ],
+            "z", ZN, 1,
+        )
+        gate_up_sent = exchanged(after(gate_up_sent, down_z), "z", ZN)
         key_list = take_all([key_sent[p] for p in places])
         value_list = take_all([value_sent[p] for p in places])
-        up_w = in_order(take_all(up_sent), "z", ZN, 1)
         output_sent = direct(after(output_z, *value_list), xn, yn)
         down_z = after(down_z, *value_list)
         down_out, down_side = square_out(down_z, "x", sizes), side_out(down_z, "x", sizes)
         keys, values = jnp.concatenate(key_list), jnp.concatenate(value_list)
-        contrast, stat = attend(run, mix, tables, now(queries), keys, values, bias)
+        cot = take(cot_sent)
+        contrast, stat = attend(run, mix, tables, now(queries), keys, values)
         then(contrast)
-        gate_w = in_order(take_all(gate_sent), "z", ZN, 1)
+        gate_up_sent = take_all(gate_up_sent)
         output_sent = dict(zip(places, take_all([output_sent[p] for p in places]), strict=True))
         wo = joined_up(output_sent)
         contrast = now(contrast)[:group]
@@ -749,6 +824,7 @@
         joined = head_plain * head_gain * (1.0 - lambda_init)
         branch_part = then(fine(joined, wo))
         branch_sent = group_sum(branch_part)
+        up_w, gate_w = halved(in_order(gate_up_sent, "z", ZN, 1))
 
         down_out, down_side = take_all(down_out), take_all(down_side)
         down_on = square_on(down_out, "x", sizes, down_side)
@@ -764,29 +840,39 @@
         ffn_scale = lax.rsqrt(jnp.mean(residual * residual, axis=1, keepdims=True) + epsilon)
         ffn_mine = then(residual * ffn_scale)
         ffn_sent = group_gather(ffn_mine)
-        wd = then(tiled_up(down_pieces))
+        wd = tiled_up(down_pieces)
+        grad_hidden = then(fine(wd, cot, 1, 1))
         top_out, low_side = take_all(top_out), take_all(low_side)
         up_on = square_on(take_all(up_out), "y", sizes, up_side)
         top_on = square_on(top_out, "x", sizes, top_side)
         low_on = square_on(take_all(low_out), "y", sizes, low_side)
         up_pieces = dict(zip(places, take_all([up_on[p] for p in places]), strict=True))
         ffn_plain = take(ffn_sent)
-        cot_sent = group_gather(after(cot_mine, ffn_plain))
-        wu = tiled_up(up_pieces)
-        up_proj = then(fine(wu, ffn_plain, 1, 1))
         top_list = take_all([top_on[p] for p in places])
         low_list = take_all([low_on[p] for p in places])
-        wg = tiled_up({p: jnp.concatenate(v) for p, *v in zip(places, top_list, low_list, strict=True)})
-
-        gating = then(fine(wg, ffn_plain, 1, 1))
+        wug = jnp.concatenate(
+            [
+                jnp.concatenate([v[s, t] for s in range(xn)], axis=1)
+                for t in range(yn)
+                for v in (up_pieces,)
+            ]
+            + [
+                jnp.concatenate([v[s, t] for s in range(xn)], axis=1)
+                for t in range(yn)
+                for v in (dict(zip(places, top_list, strict=True)), dict(zip(places, low_list, strict=True)))
+            ]
+        )
+
+        both = fine(wug, ffn_plain, 1, 1)
+        up_proj, gating = halved(both)
         gate = lax.logistic(gating)
         active = gating * gate
         hidden = active * up_proj
-        cot = take(cot_sent)
-        grad_hidden = fine(wd, cot, 1, 1)
-        grad_up_proj = grad_hidden * active
-        grad_gating = grad_hidden * up_proj * gate * (1.0 + gating * (1.0 - gate))
-        grad_ffn_part = then(fine(grad_gating, wg, 0, 0) + fine(grad_up_proj, wu, 0, 0))
+        grad_both = jnp.concatenate(
+            [grad_hidden * active, grad_hidden * up_proj * gate * (1.0 + gating * (1.0 - gate))]
+        )
+        grad_ffn_part = then(fine(grad_both, wug, 0, 0))
+        grad_up_proj, grad_gating = halved(grad_both)
         grad_ffn_sent = group_sum(grad_ffn_part)
         down_grad = then(dot(now(hidden), cot))
         down_first = tiles(down_grad)
@@ -834,7 +920,7 @@
         low_sent = square_back({p: after(v, up_grad) for p, v in low_first.items()}, "y", sizes)
         grad_contrast = now(grad_contrast)
         grad_queries, grad_keys, grad_values, inner = attend_back(
-            run, mix, tables, queries, grad_contrast, stat, keys, values, bias
+            run, mix, tables, queries, grad_contrast, stat, keys, values
         )
         then(grad_queries, grad_keys, grad_values)
         rows_cut = lambda g: {p: g[i * group : (i + 1) * group] for i, p in enumerate(places)}

time: 1070 us -> 1040 us (0.972)
  waiting for transfers between devices: 399 us -> 369 us
  matrix products: 195 us -> 172 us
  other arithmetic: 100 us -> 116 us
  starting transfers between devices: 183 us -> 167 us
  Pallas kernels: 62.4 us -> 74.2 us
    all_gather x4, waiting for transfers between devices: 52.1 us -> 25.4 us  [group_gather(): return lax.all_gather(v, ('z', 'k'), axis=0, tiled=True)]
    ppermute x104 -> x98, starting transfers between devices: 180 us -> 162 us  [shifted(): return lax.ppermute(v, axis, [(i, (i + shift) % n) for i in range(n)])]
    dot_general x10 -> x8, matrix products: 124 us -> 108 us  [fine(): lax.dot_general(a, b, (((contract_a,), (contract_b,)), ((), ())), precisi...]
    pallas_call x0 -> x1, Pallas kernels: none -> 12.6 us  [tables_of(): pl.pallas_call(lambda *refs: table_kernel(sizes, shape, *refs), in_specs=...]
    unnamed x3 -> x8, other arithmetic: 0.01 us -> 11.6 us
    unnamed x399 -> x376, local copies, waits for them, and re-layouts: 62.6 us -> 68.1 us
    ppermute x104 -> x98, waiting for transfers between devices: 329 us -> 331 us  [shifted(): return lax.ppermute(v, axis, [(i, (i + shift) % n) for i in range(n)])]
  transfers between devices with their start and end apart: 115 -> 109, of which waited for: 44 -> 40; matrix products, arithmetic and copies ran while one was open for 25% -> 27% of each run, Pallas kernels for 6% -> 7%
where the time goes in v2:
time: 1040 us; the launch traced here: 1030 us
  waiting for transfers between devices  369 us (35%)
  matrix products  172 us (17%)
  starting transfers between devices  167 us (16%)
  other arithmetic  116 us (11%)
  local copies, waits for them, and re-layouts  113 us (11%)
  Pallas kernels  74.2 us (7%)
  between operations  19.7 us (2%)
    ppermute x98, waiting for transfers between devices, shifted(): return lax.ppermute(v, axis, [(i, (i + shift) % n) for i in range(n)])  331 us
    ppermute x98, starting transfers between devices, shifted(): return lax.ppermute(v, axis, [(i, (i + shift) % n) for i in range(n)])  162 us
    dot_general x8, matrix products, fine(): lax.dot_general(a, b, (((contract_a,), (contract_b,)), ((), ())), precisi...  108 us
    unnamed x376, local copies, waits for them, and re-layouts  68.1 us
    dot_general x10, matrix products, dot(): lax.dot_general(a, b, (((contract_a,), (contract_b,)), ((), ())), precisi...  63.8 us
    pallas_call x1, Pallas kernels, attend_back(): pl.pallas_call(lambda *refs: backward_kernel(run, *refs), grid=(count //...  36.6 us
    all_gather x4, waiting for transfers between devices, group_gather(): return lax.all_gather(v, ('z', 'k'), axis=0, tiled=True)  25.4 us
    pallas_call x1, Pallas kernels, attend(): pl.pallas_call(lambda *refs: forward_kernel(run, *refs), grid=(count // T...  25.1 us
  transfers between devices with their start and end apart: 109, of which 40 were waited for; matrix products, arithmetic and copies ran while one was open for 27% of the time, Pallas kernels for 7%

profile of v2, /device:TPU:0, one launch (start us, length us, event | category | flops | bytes accessed | tf_op | source)
XLA Modules:
  0.0 1030.5 jit_solution(401858927317905672)
XLA Ops:
  14.4 17.5 %collective-permute-done = f32[1536,128]{1,0:T(8,128)S(1)} collective-permute-done((f32[1536,128]{1,0:T(8,128)S(1)}, f32[1536,128]{1,0:T(8,128)S(1)}, u32[]{:S(2)}, u32[]{:S(2)}) %collective-permute-start) | collective-permute-done | bytes 786464 | tf_op jit(solution)/shard_map/ppermute | solution.py:68
  53.7 12.6 %tables.1 = (s32[50]{0:T(128)}, s32[5]{0:T(128)}, s32[160]{0:T(256)}, s32[40]{0:T(128)}, s32[800]{0:T(1024)}, /*index=5*/s32[40]{0:T(128)}) custom-call(s32[40]{0:T(128)} %refs_0_, s32[2]{0:T(128)} %pad_add_fusion.refs_1_), custom_call_target="tpu_custom_call" | custom-call | tf_op jit(solution)/shard_map/tables/pallas_call | solution.py:507
  75.5 15.8 %collective-permute-start.3 = (f32[1,192]{1,0:T(1,128)S(1)}, f32[1,192]{1,0:T(1,128)S(1)}, u32[]{:S(2)}, u32[]{:S(2)}) collective-permute-start(f32[1,192]{1,0:T(1,128)S(1)} %reshape.197), channel_id=1, source_target_pairs={{0,8},{8,16},{16,24},{24,0},{1,9},{9,17},{17,25},{25,1},{2,10},{10... | collective-permute-start | bytes 2312 | tf_op jit(solution)/shard_map/ppermute | solution.py:68
  92.6 14.0 %collective-permute-done.10 = f32[384,512]{1,0:T(8,128)} collective-permute-done((f32[384,512]{1,0:T(8,128)}, f32[384,512]{1,0:T(8,128)}, u32[]{:S(2)}, u32[]{:S(2)}) %collective-permute-start.10) | collective-permute-done | bytes 786464 | tf_op jit(solution)/shard_map/ppermute | solution.py:68
  106.6 9.7 collective-permute-start.4
  131.6 10.3 all-gather.5.cloned.1.call-done
  186.6 8.9 collective-permute-done.21
  196.1 30.9 %collective-permute-done.22 = f32[480,256]{1,0:T(8,128)} collective-permute-done((f32[480,256]{1,0:T(8,128)}, f32[480,256]{1,0:T(8,128)}, u32[]{:S(2)}, u32[]{:S(2)}) %collective-permute-start.22) | collective-permute-done | bytes 491552 | tf_op jit(solution)/shard_map/ppermute | solution.py:68
  236.3 11.0 %collective-permute-start.27 = (f32[704,256]{1,0:T(8,128)}, f32[704,256]{1,0:T(8,128)S(1)}, u32[]{:S(2)}, u32[]{:S(2)}) collective-permute-start(f32[704,256]{1,0:T(8,128)} %get-tuple-element.536), channel_id=1, source_target_pairs={{0,8},{8,16},{16,24},{24,0},{1,9},{9,17},{17,25},{25,1},{2,10},{10... | collective-permute-start | bytes 2162696 | tf_op jit(solution)/shard_map/ppermute | solution.py:68
  268.1 25.1 %attend.1 = (f32[640,256]{1,0:T(8,128)}, f32[8,640]{1,0:T(8,128)}) custom-call(f32[1]{0:T(128)} %bitcast.15.refs_0_, s32[2]{0:T(128)} %pad_add_fusion.refs_1_, s32[50]{0:T(128)} %get-tuple-element.232.refs_2_, s32[5]{0:T(128)} %get-tuple-element.233.refs_3_, s32[160]{0:T(256)} %get-tuple-element.234.refs_4_, s32[40]{0:T(128)} %get-tuple-element.235.refs_5_, ...), custom_call_target="tpu_custom_call" | custom-call | flops 40000000000 | tf_op jit(solution)/shard_map/attend/pallas_call | solution.py:521
  308.9 31.3 %collective-permute-done.30 = f32[352,1024]{1,0:T(8,128)S(1)} collective-permute-done((f32[352,1024]{1,0:T(8,128)S(1)}, f32[352,1024]{1,0:T(8,128)S(1)}, u32[]{:S(2)}, u32[]{:S(2)}) %collective-permute-start.30) | collective-permute-done | bytes 1441824 | tf_op jit(solution)/shard_map/ppermute | solution.py:68
  346.6 30.6 %collective-permute-done.33 = f32[352,1024]{1,0:T(8,128)S(1)} collective-permute-done((f32[352,1024]{1,0:T(8,128)S(1)}, f32[352,1024]{1,0:T(8,128)S(1)}, u32[]{:S(2)}, u32[]{:S(2)}) %collective-permute-start.33) | collective-permute-done | bytes 1441824 | tf_op jit(solution)/shard_map/ppermute | solution.py:68
  399.3 18.8 %fusion.11 = f32[704,640]{1,0:T(8,128)} fusion(f32[640,2048]{1,0:T(8,128)} %all-gather.7.cloned.1.call-done, f32[352,1024]{1,0:T(8,128)} %copy-done.114, f32[352,1024]{1,0:T(8,128)} %copy-done.112, f32[352,1024]{1,0:T(8,128)} %copy-done.110, f32[352,1024]{1,0:T(8,128)} %pad_maximum_fusion.7), kind=kOutput, calls=%fused_computation.14 | convolution fusion | flops 11077287936 | bytes 12812288 | tf_op jit(solution)/shard_map/dot_general | solution.py:37
  418.1 10.1 collective-permute-done.35
  433.1 16.6 %collective-permute-done.38 = f32[176,1024]{1,0:T(8,128)} collective-permute-done((f32[176,1024]{1,0:T(8,128)S(1)}, f32[176,1024]{1,0:T(8,128)}, u32[]{:S(2)}, u32[]{:S(2)}) %collective-permute-start.38) | collective-permute-done | bytes 720928 | tf_op jit(solution)/shard_map/ppermute | solution.py:68
  450.2 13.3 %collective-permute-done.37 = f32[352,1024]{1,0:T(8,128)S(1)} collective-permute-done((f32[352,1024]{1,0:T(8,128)S(1)}, f32[352,1024]{1,0:T(8,128)S(1)}, u32[]{:S(2)}, u32[]{:S(2)}) %collective-permute-start.37) | collective-permute-done | bytes 1441824 | tf_op jit(solution)/shard_map/ppermute | solution.py:68
  484.8 31.1 %fusion.101 = f32[1408,640]{1,0:T(8,128)S(1)} fusion(f32[1408,2048]{1,0:T(8,128)} %maximum_dynamic-update-slice_fusion.2, f32[640,2048]{1,0:T(8,128)S(1)} %copy-done.7), kind=kOutput, calls=%fused_computation.615 | convolution fusion | flops 22145925120 | bytes 20381696 | tf_op jit(solution)/shard_map/dot_general | solution.py:37
  519.9 28.8 %fusion.3 = f32[640,2048]{1,0:T(8,128)} fusion(f32[1408,2048]{1,0:T(8,128)} %maximum_dynamic-update-slice_fusion.2, f32[704,640]{1,0:T(8,128)S(1)} %get-tuple-element.334, f32[704,640]{1,0:T(8,128)S(1)} %get-tuple-element.333), kind=kOutput, calls=%fused_computation.8 | convolution fusion | flops 22146826240 | bytes 20381696 | tf_op jit(solution)/shard_map/dot_general | solution.py:37
  548.8 9.6 fusion.102
  573.5 9.1 fusion.104
  582.6 10.8 %fusion.10 = f32[640,2048]{1,0:T(8,128)} fusion(f32[704,640]{1,0:T(8,128)S(1)} %copy-done.25, f32[352,1024]{1,0:T(8,128)S(1)} %copy-done.115, f32[352,1024]{1,0:T(8,128)S(1)} %copy-done.113, f32[352,1024]{1,0:T(8,128)S(1)} %copy-done.111, f32[352,1024]{1,0:T(8,128)S(1)} %copy-done.66), kind=kOutput, calls=%fused_computation.13 | convolution fusion | flops 5540806656 | bytes 12812288 | tf_op jit(solution)/shard_map/dot_general | solution.py:31
  593.4 8.8 collective-permute-done.43
  608.9 12.0 %reduce-scatter.7.cloned.1.call-done = f32[80,2048]{1,0:T(8,128)} async-done(((f32[640,2048]{1,0:T(8,128)}), f32[80,2048]{1,0:T(8,128)}) %reduce-scatter.7.cloned.1.call-update) | async-done | bytes 655376 | tf_op jit(solution)/shard_map/reduce_scatter | solution.py:639
  640.2 19.5 %collective-permute-done.44 = f32[352,1024]{1,0:T(8,128)} collective-permute-done((f32[352,1024]{1,0:T(8,128)}, f32[352,1024]{1,0:T(8,128)}, u32[]{:S(2)}, u32[]{:S(2)}) %collective-permute-start.44) | collective-permute-done | bytes 1441824 | tf_op jit(solution)/shard_map/ppermute | solution.py:68
  666.3 15.1 %all-gather.11.cloned.1.call-done = f32[640,2048]{1,0:T(8,128)} async-done(((f32[80,2048]{1,0:T(8,128)}), f32[640,2048]{1,0:T(8,128)}) %all-gather.11.cloned.1.call-update) | async-done | bytes 5242896 | tf_op jit(solution)/shard_map/all_gather | solution.py:636
  681.6 7.6 multiply_reduce_fusion.3
  699.1 36.6 %attend_back.1 = (f32[640,256]{1,0:T(8,128)}, f32[2560,256]{1,0:T(8,128)}, f32[2560,256]{1,0:T(8,128)}, f32[8,640]{1,0:T(8,128)}) custom-call(f32[1]{0:T(128)} %bitcast.15.refs_0_, s32[2]{0:T(128)} %pad_add_fusion.refs_1_, s32[50]{0:T(128)} %get-tuple-element.232.refs_2_, s32[5]{0:T(128)} %get-tuple-element.233.refs_3_, s32[160]{0:T(256)} %get-tuple-element.234.refs_4_, ...), custom_call_target="tpu_custom_call" | custom-call | flops 40000000000 | tf_op jit(solution)/shard_map/attend_back/pallas_call | solution.py:546
  768.2 11.0 %collective-permute-done.53 = f32[640,256]{1,0:T(8,128)} collective-permute-done((f32[640,256]{1,0:T(8,128)}, f32[640,256]{1,0:T(8,128)}, u32[]{:S(2)}, u32[]{:S(2)}) %collective-permute-start.53) | collective-permute-done | bytes 655392 | tf_op jit(solution)/shard_map/ppermute | solution.py:68
  839.9 25.5 %collective-permute-done.74 = f32[176,1024]{1,0:T(8,128)S(1)} collective-permute-done((f32[176,1024]{1,0:T(8,128)}, f32[176,1024]{1,0:T(8,128)S(1)}, u32[]{:S(2)}, u32[]{:S(2)}) %collective-permute-start.74) | collective-permute-done | bytes 720928 | tf_op jit(solution)/shard_map/ppermute | solution.py:68
  902.8 7.2 collective-permute-done.50
  940.6 12.9 %collective-permute-start.90 = (f32[512,128]{1,0:T(8,128)}, f32[512,128]{1,0:T(8,128)}, u32[]{:S(2)}, u32[]{:S(2)}) collective-permute-start(f32[512,128]{1,0:T(8,128)} %get-tuple-element.648), channel_id=1, source_target_pairs={{0,8},{8,16},{16,24},{24,0},{1,9},{9,17},{17,25},{25,1},{2,10},{10... | collective-permute-start | bytes 786440 | tf_op jit(solution)/shard_map/ppermute | solution.py:68
  980.7 14.1 %collective-permute-done.89 = f32[80,2048]{1,0:T(8,128)S(1)} collective-permute-done((f32[80,2048]{1,0:T(8,128)S(1)}, f32[80,2048]{1,0:T(8,128)S(1)}, u32[]{:S(2)}, u32[]{:S(2)}) %collective-permute-start.89) | collective-permute-done | bytes 655392 | tf_op jit(solution)/shard_map/ppermute | solution.py:68
  (809 shorter events, 474.5 us)
Async XLA Ops:
  7.2 134.7 %all-gather.5.cloned.1.call-start = ((), (), s32[]{:S(2)}) async-start(), calls=%async_computation.4 | async-start | bytes 5898240 | tf_op jit(solution)/shard_map/all_gather | solution.py:636
  70.2 191.4 %all-gather.7.cloned.1.call-start = ((), (), s32[]{:S(2)}) async-start(), calls=%async_computation.5 | async-start | bytes 5898240 | tf_op jit(solution)/shard_map/all_gather | solution.py:636
  71.4 44.9 %collective-permute-start.9 = (f32[384,512]{1,0:T(8,128)S(1)}, f32[384,512]{1,0:T(8,128)S(1)}, u32[]{:S(2)}, u32[]{:S(2)}) collective-permute-start(f32[384,512]{1,0:T(8,128)S(1)} %get-tuple-element.257), channel_id=1, source_target_pairs={{0,2},{2,0},{1,3},{3,1},{4,6},{6,4},{5,7},{7,5},{8,10},{10,8},{9,1... | collective-permute-start | bytes 2359304 | tf_op jit(solution)/shard_map/ppermute | solution.py:68
  73.2 55.4 %collective-permute-start.11 = (f32[384,512]{1,0:T(8,128)S(1)}, f32[384,512]{1,0:T(8,128)S(1)}, u32[]{:S(2)}, u32[]{:S(2)}) collective-permute-start(f32[384,512]{1,0:T(8,128)S(1)} %get-tuple-element.257), channel_id=1, source_target_pairs={{0,4},{4,0},{1,5},{5,1},{2,6},{6,2},{3,7},{7,3},{8,12},{12,8},{9,1... | collective-permute-start | bytes 2359304 | tf_op jit(solution)/shard_map/ppermute | solution.py:68
  75.2 50.1 %collective-permute-start.13 = (f32[384,512]{1,0:T(8,128)}, f32[384,512]{1,0:T(8,128)}, u32[]{:S(2)}, u32[]{:S(2)}) collective-permute-start(f32[384,512]{1,0:T(8,128)} %get-tuple-element.253), channel_id=1, source_target_pairs={{0,2},{2,0},{1,3},{3,1},{4,6},{6,4},{5,7},{7,5},{8,10},{10,8},{9,1... | collective-permute-start | bytes 2359304 | tf_op jit(solution)/shard_map/ppermute | solution.py:68
  75.5 41.1 %collective-permute-start.3 = (f32[1,192]{1,0:T(1,128)S(1)}, f32[1,192]{1,0:T(1,128)S(1)}, u32[]{:S(2)}, u32[]{:S(2)}) collective-permute-start(f32[1,192]{1,0:T(1,128)S(1)} %reshape.197), channel_id=1, source_target_pairs={{0,8},{8,16},{16,24},{24,0},{1,9},{9,17},{17,25},{25,1},{2,10},{10... | collective-permute-start | bytes 2312 | tf_op jit(solution)/shard_map/ppermute | solution.py:68
  141.9 237.3 %reduce-scatter.5.cloned.1.call-start = ((), (), s32[]{:S(2)}) async-start(), calls=%async_computation.6 | async-start | bytes 5898240 | tf_op jit(solution)/shard_map/reduce_scatter | solution.py:639
  168.8 58.2 %collective-permute-start.22 = (f32[480,256]{1,0:T(8,128)}, f32[480,256]{1,0:T(8,128)}, u32[]{:S(2)}, u32[]{:S(2)}) collective-permute-start(f32[480,256]{1,0:T(8,128)} %get-tuple-element.567), channel_id=1, source_target_pairs={{0,16},{8,24},{16,0},{24,8},{1,17},{9,25},{17,1},{25,9},{2,18},{10... | collective-permute-start | bytes 1474568 | tf_op jit(solution)/shard_map/ppermute | solution.py:68
  170.4 57.9 %collective-permute-start.23 = (f32[480,256]{1,0:T(8,128)}, f32[480,256]{1,0:T(8,128)}, u32[]{:S(2)}, u32[]{:S(2)}) collective-permute-start(f32[480,256]{1,0:T(8,128)} %get-tuple-element.566), channel_id=1, source_target_pairs={{0,24},{8,0},{16,8},{24,16},{1,25},{9,1},{17,9},{25,17},{2,26},{10... | collective-permute-start | bytes 1474568 | tf_op jit(solution)/shard_map/ppermute | solution.py:68
  184.5 63.0 %collective-permute-start.19 = (f32[640,256]{1,0:T(8,128)}, f32[640,256]{1,0:T(8,128)S(1)}, u32[]{:S(2)}, u32[]{:S(2)}) collective-permute-start(f32[640,256]{1,0:T(8,128)} %fusion.22), channel_id=1, source_target_pairs={{0,2},{2,0},{1,3},{3,1},{4,6},{6,4},{5,7},{7,5},{8,10},{10,8},{9,1... | collective-permute-start | bytes 1966088 | tf_op jit(solution)/shard_map/ppermute | solution.py:68
  185.2 64.9 %collective-permute-start.20 = (f32[640,256]{1,0:T(8,128)}, f32[640,256]{1,0:T(8,128)S(1)}, u32[]{:S(2)}, u32[]{:S(2)}) collective-permute-start(f32[640,256]{1,0:T(8,128)} %collective-permute-done.16), channel_id=1, source_target_pairs={{0,2},{2,0},{1,3},{3,1},{4,6},{6,4},{5,7},{7,5},{8,10},{10,8},{9,1... | collective-permute-start | bytes 1966088 | tf_op jit(solution)/shard_map/ppermute | solution.py:68
  195.5 54.7 %collective-permute-start.17 = (f32[640,256]{1,0:T(8,128)}, f32[640,256]{1,0:T(8,128)S(1)}, u32[]{:S(2)}, u32[]{:S(2)}) collective-permute-start(f32[640,256]{1,0:T(8,128)} %fusion.19), channel_id=1, source_target_pairs={{0,4},{4,0},{1,5},{5,1},{2,6},{6,2},{3,7},{7,3},{8,12},{12,8},{9,1... | collective-permute-start | bytes 1966088 | tf_op jit(solution)/shard_map/ppermute | solution.py:68
  247.5 48.8 %collective-permute-start.28 = (f32[704,256]{1,0:T(8,128)}, f32[704,256]{1,0:T(8,128)S(1)}, u32[]{:S(2)}, u32[]{:S(2)}) collective-permute-start(f32[704,256]{1,0:T(8,128)} %get-tuple-element.535), channel_id=1, source_target_pairs={{0,16},{8,24},{16,0},{24,8},{1,17},{9,25},{17,1},{25,9},{2,18},{10... | collective-permute-start | bytes 2162696 | tf_op jit(solution)/shard_map/ppermute | solution.py:68
  250.1 46.2 %collective-permute-start.29 = (f32[704,256]{1,0:T(8,128)}, f32[704,256]{1,0:T(8,128)}, u32[]{:S(2)}, u32[]{:S(2)}) collective-permute-start(f32[704,256]{1,0:T(8,128)} %get-tuple-element.534), channel_id=1, source_target_pairs={{0,24},{8,0},{16,8},{24,16},{1,25},{9,1},{17,9},{25,17},{2,26},{10... | collective-permute-start | bytes 2162696 | tf_op jit(solution)/shard_map/ppermute | solution.py:68
  250.3 46.0 %collective-permute-start.24 = (f32[256,512]{1,0:T(8,128)S(1)}, f32[256,512]{1,0:T(8,128)S(1)}, u32[]{:S(2)}, u32[]{:S(2)}) collective-permute-start(f32[256,512]{1,0:T(8,128)S(1)} %pad_maximum_fusion.18), channel_id=1, source_target_pairs={{0,2},{2,0},{4,6},{6,4},{1,3},{3,1},{5,7},{7,5},{8,10},{10,8},{12,... | collective-permute-start | bytes 1572872 | tf_op jit(solution)/shard_map/ppermute | solution.py:118
  251.8 44.5 %collective-permute-start.25 = (f32[256,512]{1,0:T(8,128)S(1)}, f32[256,512]{1,0:T(8,128)}, u32[]{:S(2)}, u32[]{:S(2)}) collective-permute-start(f32[256,512]{1,0:T(8,128)S(1)} %pad_maximum_fusion.18), channel_id=1, source_target_pairs={{0,4},{2,6},{4,0},{6,2},{1,5},{3,7},{5,1},{7,3},{8,12},{10,14},{12... | collective-permute-start | bytes 1572872 | tf_op jit(solution)/shard_map/ppermute | solution.py:118
  305.5 163.3 %all-gather.9.cloned.1.call-start = ((), (), s32[]{:S(2)}) async-start(), calls=%async_computation.7 | async-start | bytes 5898240 | tf_op jit(solution)/shard_map/all_gather | solution.py:636
  307.4 39.2 %collective-permute-start.32 = (f32[352,1024]{1,0:T(8,128)S(1)}, f32[352,1024]{1,0:T(8,128)S(1)}, u32[]{:S(2)}, u32[]{:S(2)}) collective-permute-start(f32[352,1024]{1,0:T(8,128)S(1)} %copy-done.65), channel_id=1, source_target_pairs={{0,2},{2,0},{1,3},{3,1},{4,6},{6,4},{5,7},{7,5},{8,10},{10,8},{9,1... | collective-permute-start | bytes 4325384 | tf_op jit(solution)/shard_map/ppermute | solution.py:68
  394.2 226.7 %reduce-scatter.7.cloned.1.call-start = ((), (), s32[]{:S(2)}) async-start(), calls=%async_computation.8 | async-start | bytes 5898240 | tf_op jit(solution)/shard_map/reduce_scatter | solution.py:639
  432.5 43.3 %collective-permute-start.40 = (f32[176,1024]{1,0:T(8,128)}, f32[176,1024]{1,0:T(8,128)}, u32[]{:S(2)}, u32[]{:S(2)}) collective-permute-start(f32[176,1024]{1,0:T(8,128)} %collective-permute-done.36), channel_id=1, source_target_pairs={{0,2},{2,0},{1,3},{3,1},{4,6},{6,4},{5,7},{7,5},{8,10},{10,8},{9,1... | collective-permute-start | bytes 2162696 | tf_op jit(solution)/shard_map/ppermute | solution.py:68
  548.7 132.6 %all-gather.11.cloned.1.call-start = ((), (), s32[]{:S(2)}) async-start(), calls=%async_computation.9 | async-start | bytes 5898240 | tf_op jit(solution)/shard_map/all_gather | solution.py:636
  624.8 295.2 %reduce-scatter.9.cloned.1.call-start = ((), (), s32[]{:S(2)}) async-start(), calls=%async_computation.10 | async-start | bytes 5898240 | tf_op jit(solution)/shard_map/reduce_scatter | solution.py:639
  638.8 53.6 %collective-permute-start.46 = (f32[352,1024]{1,0:T(8,128)}, f32[352,1024]{1,0:T(8,128)}, u32[]{:S(2)}, u32[]{:S(2)}) collective-permute-start(f32[352,1024]{1,0:T(8,128)} %slice_add_fusion.2), channel_id=1, source_target_pairs={{0,4},{4,0},{1,5},{5,1},{2,6},{6,2},{3,7},{7,3},{8,12},{12,8},{9,1... | collective-permute-start | bytes 4325384 | tf_op jit(solution)/shard_map/ppermute | solution.py:68
  639.3 51.0 %collective-permute-start.47 = (f32[352,1024]{1,0:T(8,128)}, f32[352,1024]{1,0:T(8,128)}, u32[]{:S(2)}, u32[]{:S(2)}) collective-permute-start(f32[352,1024]{1,0:T(8,128)} %slice_add_fusion.3), channel_id=1, source_target_pairs={{0,2},{2,0},{1,3},{3,1},{4,6},{6,4},{5,7},{7,5},{8,10},{10,8},{9,1... | collective-permute-start | bytes 4325384 | tf_op jit(solution)/shard_map/ppermute | solution.py:68
  681.4 284.5 %reduce-scatter.11.cloned.1.call-start = ((), (), s32[]{:S(2)}) async-start(), calls=%async_computation.11 | async-start | bytes 5898240 | tf_op jit(solution)/shard_map/reduce_scatter | solution.py:639
  695.1 60.3 %collective-permute-start.56 = (f32[176,1024]{1,0:T(8,128)}, f32[176,1024]{1,0:T(8,128)}, u32[]{:S(2)}, u32[]{:S(2)}) collective-permute-start(f32[176,1024]{1,0:T(8,128)} %get-tuple-element.355), channel_id=1, source_target_pairs={{0,2},{2,0},{1,3},{3,1},{4,6},{6,4},{5,7},{7,5},{8,10},{10,8},{9,1... | collective-permute-start | bytes 2162696 | tf_op jit(solution)/shard_map/ppermute | solution.py:68
  696.6 60.3 %collective-permute-start.57 = (f32[176,1024]{1,0:T(8,128)}, f32[176,1024]{1,0:T(8,128)}, u32[]{:S(2)}, u32[]{:S(2)}) collective-permute-start(f32[176,1024]{1,0:T(8,128)} %get-tuple-element.356), channel_id=1, source_target_pairs={{0,2},{2,0},{1,3},{3,1},{4,6},{6,4},{5,7},{7,5},{8,10},{10,8},{9,1... | collective-permute-start | bytes 2162696 | tf_op jit(solution)/shard_map/ppermute | solution.py:68
  697.1 54.8 %collective-permute-start.54 = (f32[176,1024]{1,0:T(8,128)}, f32[176,1024]{1,0:T(8,128)}, u32[]{:S(2)}, u32[]{:S(2)}) collective-permute-start(f32[176,1024]{1,0:T(8,128)} %get-tuple-element.349), channel_id=1, source_target_pairs={{0,4},{4,0},{1,5},{5,1},{2,6},{6,2},{3,7},{7,3},{8,12},{12,8},{9,1... | collective-permute-start | bytes 2162696 | tf_op jit(solution)/shard_map/ppermute | solution.py:68
  698.6 56.7 %collective-permute-start.55 = (f32[176,1024]{1,0:T(8,128)}, f32[176,1024]{1,0:T(8,128)}, u32[]{:S(2)}, u32[]{:S(2)}) collective-permute-start(f32[176,1024]{1,0:T(8,128)} %get-tuple-element.350), channel_id=1, source_target_pairs={{0,4},{4,0},{1,5},{5,1},{2,6},{6,2},{3,7},{7,3},{8,12},{12,8},{9,1... | collective-permute-start | bytes 2162696 | tf_op jit(solution)/shard_map/ppermute | solution.py:68
  827.1 39.8 %collective-permute-start.72 = (f32[256,512]{1,0:T(8,128)}, f32[256,512]{1,0:T(8,128)S(1)}, u32[]{:S(2)}, u32[]{:S(2)}) collective-permute-start(f32[256,512]{1,0:T(8,128)} %get-tuple-element.559), channel_id=1, source_target_pairs={{0,4},{4,0},{1,5},{5,1},{2,6},{6,2},{3,7},{7,3},{8,12},{12,8},{9,1... | collective-permute-start | bytes 1572872 | tf_op jit(solution)/shard_map/ppermute | solution.py:68
  828.6 39.8 %collective-permute-start.73 = (f32[256,512]{1,0:T(8,128)}, f32[256,512]{1,0:T(8,128)S(1)}, u32[]{:S(2)}, u32[]{:S(2)}) collective-permute-start(f32[256,512]{1,0:T(8,128)} %get-tuple-element.558), channel_id=1, source_target_pairs={{0,4},{4,0},{1,5},{5,1},{2,6},{6,2},{3,7},{7,3},{8,12},{12,8},{9,1... | collective-permute-start | bytes 1572872 | tf_op jit(solution)/shard_map/ppermute | solution.py:68
  957.0 38.0 %collective-permute-start.94 = (f32[512,128]{1,0:T(8,128)}, f32[512,128]{1,0:T(8,128)}, u32[]{:S(2)}, u32[]{:S(2)}) collective-permute-start(f32[512,128]{1,0:T(8,128)} %get-tuple-element.644), channel_id=1, source_target_pairs={{0,8},{8,16},{16,24},{24,0},{1,9},{9,17},{17,25},{25,1},{2,10},{10... | collective-permute-start | bytes 786440 | tf_op jit(solution)/shard_map/ppermute | solution.py:68
  (199 other events, 2906.7 us)
Sparse Core Ops, SparseCore 0:
  70.4 71.4 all-gather.4
  143.5 87.6 all-gather.6
  305.6 73.5 reduce-scatter.4
  394.3 67.8 all-gather.8
  548.8 72.0 reduce-scatter.6
  624.9 56.3 all-gather.10
  683.7 58.6 reduce-scatter.8
  816.4 67.5 reduce-scatter.10

commit v3 on v2

--- a/solution.py
+++ b/solution.py
@@ -724,7 +724,8 @@
         tables = [jnp.stack([x, y])] + tables
         mine = piece(now(tokens))
         scale = lax.rsqrt(jnp.mean(mine * mine, axis=1, keepdims=True) + epsilon)
-        plain_mine = then(to_distance_y(mine) * scale)
+        mine_attn = to_distance_y(mine)
+        plain_mine = then(mine_attn * scale)
         down_sent = now(w_down).T
         then(down_sent, plain_mine, *tables)
         small = in_order(take_all(small_sent), "x", xn).reshape(1, -1)
@@ -836,7 +837,7 @@
         top_out, low_out = square_out(gate_top, "x", sizes), square_out(gate_low, "y", sizes)
         top_side, low_side = side_out(gate_top, "x", sizes), side_out(gate_low, "y", sizes)
         branch = take(branch_sent)
-        residual = mine + from_distance_y(branch)
+        residual = from_distance_y(mine_attn + branch)
         ffn_scale = lax.rsqrt(jnp.mean(residual * residual, axis=1, keepdims=True) + epsilon)
         ffn_mine = then(residual * ffn_scale)
         ffn_sent = group_gather(ffn_mine)

time: 1040 us -> 1020 us (0.981)
  local copies, waits for them, and re-layouts: 113 us -> 99.1 us
    unnamed x376 -> x374, local copies, waits for them, and re-layouts: 68.1 us -> 55.1 us
where the time goes in v3:
time: 1020 us
  waiting for transfers between devices  368 us (36%)
  matrix products  173 us (17%)
  starting transfers between devices  165 us (16%)
  other arithmetic  117 us (11%)
  local copies, waits for them, and re-layouts  99.1 us (10%)
  Pallas kernels  76.2 us (7%)
  between operations  19.8 us (2%)
    ppermute x98, waiting for transfers between devices, shifted(): return lax.ppermute(v, axis, [(i, (i + shift) % n) for i in range(n)])  329 us
    ppermute x98, starting transfers between devices, shifted(): return lax.ppermute(v, axis, [(i, (i + shift) % n) for i in range(n)])  160 us
    dot_general x8, matrix products, fine(): lax.dot_general(a, b, (((contract_a,), (contract_b,)), ((), ())), precisi...  108 us
    dot_general x10, matrix products, dot(): lax.dot_general(a, b, (((contract_a,), (contract_b,)), ((), ())), precisi...  64.4 us
    unnamed x374, local copies, waits for them, and re-layouts  55.1 us
    pallas_call x1, Pallas kernels, attend_back(): pl.pallas_call(lambda *refs: backward_kernel(run, *refs), grid=(count //...  37.8 us
    pallas_call x1, Pallas kernels, attend(): pl.pallas_call(lambda *refs: forward_kernel(run, *refs), grid=(count // T...  25.9 us
    all_gather x4, waiting for transfers between devices, group_gather(): return lax.all_gather(v, ('z', 'k'), axis=0, tiled=True)  25.8 us
  transfers between devices with their start and end apart: 109, of which 40 were waited for; matrix products, arithmetic and copies ran while one was open for 27% of the time, Pallas kernels for 7%

profile of v3, /device:TPU:0, one launch (start us, length us, event | category | flops | bytes accessed | tf_op | source)
XLA Modules:
  0.0 1017.3 jit_solution(14258232245608621753)
XLA Ops:
  14.4 17.5 %collective-permute-done = f32[1536,128]{1,0:T(8,128)S(1)} collective-permute-done((f32[1536,128]{1,0:T(8,128)S(1)}, f32[1536,128]{1,0:T(8,128)S(1)}, u32[]{:S(2)}, u32[]{:S(2)}) %collective-permute-start) | collective-permute-done | bytes 786464 | tf_op jit(solution)/shard_map/ppermute | solution.py:68
  54.2 12.6 %tables.1 = (s32[50]{0:T(128)}, s32[5]{0:T(128)}, s32[160]{0:T(256)}, s32[40]{0:T(128)}, s32[800]{0:T(1024)}, /*index=5*/s32[40]{0:T(128)}) custom-call(s32[40]{0:T(128)} %refs_0_, s32[2]{0:T(128)} %pad_add_fusion.refs_1_), custom_call_target="tpu_custom_call" | custom-call | tf_op jit(solution)/shard_map/tables/pallas_call | solution.py:507
  76.1 15.8 %collective-permute-start.3 = (f32[1,192]{1,0:T(1,128)S(1)}, f32[1,192]{1,0:T(1,128)S(1)}, u32[]{:S(2)}, u32[]{:S(2)}) collective-permute-start(f32[1,192]{1,0:T(1,128)S(1)} %reshape.197), channel_id=1, source_target_pairs={{0,8},{8,16},{16,24},{24,0},{1,9},{9,17},{17,25},{25,1},{2,10},{10... | collective-permute-start | bytes 2312 | tf_op jit(solution)/shard_map/ppermute | solution.py:68
  93.1 14.0 %collective-permute-done.10 = f32[384,512]{1,0:T(8,128)} collective-permute-done((f32[384,512]{1,0:T(8,128)}, f32[384,512]{1,0:T(8,128)}, u32[]{:S(2)}, u32[]{:S(2)}) %collective-permute-start.10) | collective-permute-done | bytes 786464 | tf_op jit(solution)/shard_map/ppermute | solution.py:68
  107.1 9.2 collective-permute-start.4
  131.7 10.7 %all-gather.5.cloned.1.call-done = f32[640,2048]{1,0:T(8,128)} async-done(((f32[80,2048]{1,0:T(8,128)}), f32[640,2048]{1,0:T(8,128)}) %all-gather.5.cloned.1.call-update) | async-done | bytes 5242896 | tf_op jit(solution)/shard_map/all_gather | solution.py:636
  187.2 8.8 collective-permute-done.21
  196.6 31.0 %collective-permute-done.22 = f32[480,256]{1,0:T(8,128)} collective-permute-done((f32[480,256]{1,0:T(8,128)}, f32[480,256]{1,0:T(8,128)}, u32[]{:S(2)}, u32[]{:S(2)}) %collective-permute-start.22) | collective-permute-done | bytes 491552 | tf_op jit(solution)/shard_map/ppermute | solution.py:68
  236.9 11.0 %collective-permute-start.27 = (f32[704,256]{1,0:T(8,128)}, f32[704,256]{1,0:T(8,128)S(1)}, u32[]{:S(2)}, u32[]{:S(2)}) collective-permute-start(f32[704,256]{1,0:T(8,128)} %get-tuple-element.536), channel_id=1, source_target_pairs={{0,8},{8,16},{16,24},{24,0},{1,9},{9,17},{17,25},{25,1},{2,10},{10... | collective-permute-start | bytes 2162696 | tf_op jit(solution)/shard_map/ppermute | solution.py:68
  268.7 25.9 %attend.1 = (f32[640,256]{1,0:T(8,128)}, f32[8,640]{1,0:T(8,128)}) custom-call(f32[1]{0:T(128)} %bitcast.15.refs_0_, s32[2]{0:T(128)} %pad_add_fusion.refs_1_, s32[50]{0:T(128)} %get-tuple-element.232.refs_2_, s32[5]{0:T(128)} %get-tuple-element.233.refs_3_, s32[160]{0:T(256)} %get-tuple-element.234.refs_4_, s32[40]{0:T(128)} %get-tuple-element.235.refs_5_, ...), custom_call_target="tpu_custom_call" | custom-call | flops 40000000000 | tf_op jit(solution)/shard_map/attend/pallas_call | solution.py:521
  308.7 31.6 %collective-permute-done.30 = f32[352,1024]{1,0:T(8,128)S(1)} collective-permute-done((f32[352,1024]{1,0:T(8,128)}, f32[352,1024]{1,0:T(8,128)S(1)}, u32[]{:S(2)}, u32[]{:S(2)}) %collective-permute-start.30) | collective-permute-done | bytes 1441824 | tf_op jit(solution)/shard_map/ppermute | solution.py:68
  346.4 30.6 %collective-permute-done.33 = f32[352,1024]{1,0:T(8,128)S(1)} collective-permute-done((f32[352,1024]{1,0:T(8,128)S(1)}, f32[352,1024]{1,0:T(8,128)S(1)}, u32[]{:S(2)}, u32[]{:S(2)}) %collective-permute-start.33) | collective-permute-done | bytes 1441824 | tf_op jit(solution)/shard_map/ppermute | solution.py:68
  388.1 18.8 %fusion.11 = f32[704,640]{1,0:T(8,128)} fusion(f32[640,2048]{1,0:T(8,128)} %all-gather.7.cloned.1.call-done, f32[352,1024]{1,0:T(8,128)} %copy-done.113, f32[352,1024]{1,0:T(8,128)} %copy-done.111, f32[352,1024]{1,0:T(8,128)} %copy-done.109, f32[352,1024]{1,0:T(8,128)} %pad_maximum_fusion.7), kind=kOutput, calls=%fused_computation.14 | convolution fusion | flops 11077287936 | bytes 12812288 | tf_op jit(solution)/shard_map/dot_general | solution.py:37
  406.9 10.1 collective-permute-done.35
  421.9 16.6 %collective-permute-done.38 = f32[176,1024]{1,0:T(8,128)} collective-permute-done((f32[176,1024]{1,0:T(8,128)S(1)}, f32[176,1024]{1,0:T(8,128)}, u32[]{:S(2)}, u32[]{:S(2)}) %collective-permute-start.38) | collective-permute-done | bytes 720928 | tf_op jit(solution)/shard_map/ppermute | solution.py:68
  439.1 13.3 %collective-permute-done.37 = f32[352,1024]{1,0:T(8,128)S(1)} collective-permute-done((f32[352,1024]{1,0:T(8,128)S(1)}, f32[352,1024]{1,0:T(8,128)S(1)}, u32[]{:S(2)}, u32[]{:S(2)}) %collective-permute-start.37) | collective-permute-done | bytes 1441824 | tf_op jit(solution)/shard_map/ppermute | solution.py:68
  473.6 31.1 %fusion.102 = f32[1408,640]{1,0:T(8,128)S(1)} fusion(f32[1408,2048]{1,0:T(8,128)} %maximum_dynamic-update-slice_fusion.2, f32[640,2048]{1,0:T(8,128)S(1)} %copy-done.7), kind=kOutput, calls=%fused_computation.617 | convolution fusion | flops 22145925120 | bytes 20381696 | tf_op jit(solution)/shard_map/dot_general | solution.py:37
  508.7 28.8 %fusion.3 = f32[640,2048]{1,0:T(8,128)} fusion(f32[1408,2048]{1,0:T(8,128)} %maximum_dynamic-update-slice_fusion.2, f32[704,640]{1,0:T(8,128)S(1)} %get-tuple-element.334, f32[704,640]{1,0:T(8,128)S(1)} %get-tuple-element.333), kind=kOutput, calls=%fused_computation.8 | convolution fusion | flops 22146826240 | bytes 20381696 | tf_op jit(solution)/shard_map/dot_general | solution.py:37
  537.6 9.6 fusion.103
  562.3 9.1 fusion.105
  571.5 11.5 %fusion.10 = f32[640,2048]{1,0:T(8,128)} fusion(f32[704,640]{1,0:T(8,128)S(1)} %copy-done.23, f32[352,1024]{1,0:T(8,128)S(1)} %copy-done.114, f32[352,1024]{1,0:T(8,128)S(1)} %copy-done.112, f32[352,1024]{1,0:T(8,128)S(1)} %copy-done.110, f32[352,1024]{1,0:T(8,128)} %pad_maximum_fusion.7), kind=kOutput, calls=%fused_computation.13 | convolution fusion | flops 5540806656 | bytes 12812288 | tf_op jit(solution)/shard_map/dot_general | solution.py:31
  583.0 7.7 collective-permute-done.43
  597.2 10.7 %reduce-scatter.7.cloned.1.call-done = f32[80,2048]{1,0:T(8,128)} async-done(((f32[640,2048]{1,0:T(8,128)}), f32[80,2048]{1,0:T(8,128)}) %reduce-scatter.7.cloned.1.call-update) | async-done | bytes 655376 | tf_op jit(solution)/shard_map/reduce_scatter | solution.py:639
  627.2 19.5 %collective-permute-done.44 = f32[352,1024]{1,0:T(8,128)} collective-permute-done((f32[352,1024]{1,0:T(8,128)}, f32[352,1024]{1,0:T(8,128)}, u32[]{:S(2)}, u32[]{:S(2)}) %collective-permute-start.44) | collective-permute-done | bytes 1441824 | tf_op jit(solution)/shard_map/ppermute | solution.py:68
  653.2 15.1 %all-gather.11.cloned.1.call-done = f32[640,2048]{1,0:T(8,128)} async-done(((f32[80,2048]{1,0:T(8,128)}), f32[640,2048]{1,0:T(8,128)}) %all-gather.11.cloned.1.call-update) | async-done | bytes 5242896 | tf_op jit(solution)/shard_map/all_gather | solution.py:636
  668.5 7.6 multiply_reduce_fusion.3
  686.0 37.8 %attend_back.1 = (f32[640,256]{1,0:T(8,128)}, f32[2560,256]{1,0:T(8,128)}, f32[2560,256]{1,0:T(8,128)}, f32[8,640]{1,0:T(8,128)}) custom-call(f32[1]{0:T(128)} %bitcast.15.refs_0_, s32[2]{0:T(128)} %pad_add_fusion.refs_1_, s32[50]{0:T(128)} %get-tuple-element.232.refs_2_, s32[5]{0:T(128)} %get-tuple-element.233.refs_3_, s32[160]{0:T(256)} %get-tuple-element.234.refs_4_, ...), custom_call_target="tpu_custom_call" | custom-call | flops 40000000000 | tf_op jit(solution)/shard_map/attend_back/pallas_call | solution.py:546
  755.7 10.7 %collective-permute-done.53 = f32[640,256]{1,0:T(8,128)} collective-permute-done((f32[640,256]{1,0:T(8,128)}, f32[640,256]{1,0:T(8,128)}, u32[]{:S(2)}, u32[]{:S(2)}) %collective-permute-start.53) | collective-permute-done | bytes 655392 | tf_op jit(solution)/shard_map/ppermute | solution.py:68
  826.6 25.7 %collective-permute-done.74 = f32[176,1024]{1,0:T(8,128)S(1)} collective-permute-done((f32[176,1024]{1,0:T(8,128)}, f32[176,1024]{1,0:T(8,128)S(1)}, u32[]{:S(2)}, u32[]{:S(2)}) %collective-permute-start.74) | collective-permute-done | bytes 720928 | tf_op jit(solution)/shard_map/ppermute | solution.py:68
  889.6 7.2 collective-permute-done.50
  927.4 12.9 %collective-permute-start.90 = (f32[512,128]{1,0:T(8,128)}, f32[512,128]{1,0:T(8,128)}, u32[]{:S(2)}, u32[]{:S(2)}) collective-permute-start(f32[512,128]{1,0:T(8,128)} %get-tuple-element.648), channel_id=1, source_target_pairs={{0,8},{8,16},{16,24},{24,0},{1,9},{9,17},{17,25},{25,1},{2,10},{10... | collective-permute-start | bytes 786440 | tf_op jit(solution)/shard_map/ppermute | solution.py:68
  967.6 14.1 %collective-permute-done.89 = f32[80,2048]{1,0:T(8,128)S(1)} collective-permute-done((f32[80,2048]{1,0:T(8,128)S(1)}, f32[80,2048]{1,0:T(8,128)S(1)}, u32[]{:S(2)}, u32[]{:S(2)}) %collective-permute-start.89) | collective-permute-done | bytes 655392 | tf_op jit(solution)/shard_map/ppermute | solution.py:68
  (808 shorter events, 461.0 us)
Async XLA Ops:
  7.2 135.2 %all-gather.5.cloned.1.call-start = ((), (), s32[]{:S(2)}) async-start(), calls=%async_computation.4 | async-start | bytes 5898240 | tf_op jit(solution)/shard_map/all_gather | solution.py:636
  70.8 191.5 %all-gather.7.cloned.1.call-start = ((), (), s32[]{:S(2)}) async-start(), calls=%async_computation.5 | async-start | bytes 5898240 | tf_op jit(solution)/shard_map/all_gather | solution.py:636
  71.9 44.4 %collective-permute-start.9 = (f32[384,512]{1,0:T(8,128)S(1)}, f32[384,512]{1,0:T(8,128)S(1)}, u32[]{:S(2)}, u32[]{:S(2)}) collective-permute-start(f32[384,512]{1,0:T(8,128)S(1)} %get-tuple-element.257), channel_id=1, source_target_pairs={{0,2},{2,0},{1,3},{3,1},{4,6},{6,4},{5,7},{7,5},{8,10},{10,8},{9,1... | collective-permute-start | bytes 2359304 | tf_op jit(solution)/shard_map/ppermute | solution.py:68
  73.7 55.0 %collective-permute-start.11 = (f32[384,512]{1,0:T(8,128)S(1)}, f32[384,512]{1,0:T(8,128)S(1)}, u32[]{:S(2)}, u32[]{:S(2)}) collective-permute-start(f32[384,512]{1,0:T(8,128)S(1)} %get-tuple-element.257), channel_id=1, source_target_pairs={{0,4},{4,0},{1,5},{5,1},{2,6},{6,2},{3,7},{7,3},{8,12},{12,8},{9,1... | collective-permute-start | bytes 2359304 | tf_op jit(solution)/shard_map/ppermute | solution.py:68
  75.7 50.0 %collective-permute-start.13 = (f32[384,512]{1,0:T(8,128)}, f32[384,512]{1,0:T(8,128)}, u32[]{:S(2)}, u32[]{:S(2)}) collective-permute-start(f32[384,512]{1,0:T(8,128)} %get-tuple-element.253), channel_id=1, source_target_pairs={{0,2},{2,0},{1,3},{3,1},{4,6},{6,4},{5,7},{7,5},{8,10},{10,8},{9,1... | collective-permute-start | bytes 2359304 | tf_op jit(solution)/shard_map/ppermute | solution.py:68
  76.1 40.6 %collective-permute-start.3 = (f32[1,192]{1,0:T(1,128)S(1)}, f32[1,192]{1,0:T(1,128)S(1)}, u32[]{:S(2)}, u32[]{:S(2)}) collective-permute-start(f32[1,192]{1,0:T(1,128)S(1)} %reshape.197), channel_id=1, source_target_pairs={{0,8},{8,16},{16,24},{24,0},{1,9},{9,17},{17,25},{25,1},{2,10},{10... | collective-permute-start | bytes 2312 | tf_op jit(solution)/shard_map/ppermute | solution.py:68
  142.5 237.9 %reduce-scatter.5.cloned.1.call-start = ((), (), s32[]{:S(2)}) async-start(), calls=%async_computation.6 | async-start | bytes 5898240 | tf_op jit(solution)/shard_map/reduce_scatter | solution.py:639
  169.4 58.2 %collective-permute-start.22 = (f32[480,256]{1,0:T(8,128)}, f32[480,256]{1,0:T(8,128)}, u32[]{:S(2)}, u32[]{:S(2)}) collective-permute-start(f32[480,256]{1,0:T(8,128)} %get-tuple-element.567), channel_id=1, source_target_pairs={{0,16},{8,24},{16,0},{24,8},{1,17},{9,25},{17,1},{25,9},{2,18},{10... | collective-permute-start | bytes 1474568 | tf_op jit(solution)/shard_map/ppermute | solution.py:68
  171.0 57.8 %collective-permute-start.23 = (f32[480,256]{1,0:T(8,128)}, f32[480,256]{1,0:T(8,128)}, u32[]{:S(2)}, u32[]{:S(2)}) collective-permute-start(f32[480,256]{1,0:T(8,128)} %get-tuple-element.566), channel_id=1, source_target_pairs={{0,24},{8,0},{16,8},{24,16},{1,25},{9,1},{17,9},{25,17},{2,26},{10... | collective-permute-start | bytes 1474568 | tf_op jit(solution)/shard_map/ppermute | solution.py:68
  185.2 63.0 %collective-permute-start.19 = (f32[640,256]{1,0:T(8,128)}, f32[640,256]{1,0:T(8,128)S(1)}, u32[]{:S(2)}, u32[]{:S(2)}) collective-permute-start(f32[640,256]{1,0:T(8,128)} %fusion.22), channel_id=1, source_target_pairs={{0,2},{2,0},{1,3},{3,1},{4,6},{6,4},{5,7},{7,5},{8,10},{10,8},{9,1... | collective-permute-start | bytes 1966088 | tf_op jit(solution)/shard_map/ppermute | solution.py:68
  185.7 65.0 %collective-permute-start.20 = (f32[640,256]{1,0:T(8,128)}, f32[640,256]{1,0:T(8,128)S(1)}, u32[]{:S(2)}, u32[]{:S(2)}) collective-permute-start(f32[640,256]{1,0:T(8,128)} %collective-permute-done.16), channel_id=1, source_target_pairs={{0,2},{2,0},{1,3},{3,1},{4,6},{6,4},{5,7},{7,5},{8,10},{10,8},{9,1... | collective-permute-start | bytes 1966088 | tf_op jit(solution)/shard_map/ppermute | solution.py:68
  196.1 54.8 %collective-permute-start.17 = (f32[640,256]{1,0:T(8,128)}, f32[640,256]{1,0:T(8,128)S(1)}, u32[]{:S(2)}, u32[]{:S(2)}) collective-permute-start(f32[640,256]{1,0:T(8,128)} %fusion.19), channel_id=1, source_target_pairs={{0,4},{4,0},{1,5},{5,1},{2,6},{6,2},{3,7},{7,3},{8,12},{12,8},{9,1... | collective-permute-start | bytes 1966088 | tf_op jit(solution)/shard_map/ppermute | solution.py:68
  248.1 48.8 %collective-permute-start.28 = (f32[704,256]{1,0:T(8,128)}, f32[704,256]{1,0:T(8,128)S(1)}, u32[]{:S(2)}, u32[]{:S(2)}) collective-permute-start(f32[704,256]{1,0:T(8,128)} %get-tuple-element.535), channel_id=1, source_target_pairs={{0,16},{8,24},{16,0},{24,8},{1,17},{9,25},{17,1},{25,9},{2,18},{10... | collective-permute-start | bytes 2162696 | tf_op jit(solution)/shard_map/ppermute | solution.py:68
  250.7 46.2 %collective-permute-start.29 = (f32[704,256]{1,0:T(8,128)}, f32[704,256]{1,0:T(8,128)}, u32[]{:S(2)}, u32[]{:S(2)}) collective-permute-start(f32[704,256]{1,0:T(8,128)} %get-tuple-element.534), channel_id=1, source_target_pairs={{0,24},{8,0},{16,8},{24,16},{1,25},{9,1},{17,9},{25,17},{2,26},{10... | collective-permute-start | bytes 2162696 | tf_op jit(solution)/shard_map/ppermute | solution.py:68
  250.9 46.9 %collective-permute-start.24 = (f32[256,512]{1,0:T(8,128)S(1)}, f32[256,512]{1,0:T(8,128)S(1)}, u32[]{:S(2)}, u32[]{:S(2)}) collective-permute-start(f32[256,512]{1,0:T(8,128)S(1)} %pad_maximum_fusion.18), channel_id=1, source_target_pairs={{0,2},{2,0},{4,6},{6,4},{1,3},{3,1},{5,7},{7,5},{8,10},{10,8},{12,... | collective-permute-start | bytes 1572872 | tf_op jit(solution)/shard_map/ppermute | solution.py:118
  252.4 45.4 %collective-permute-start.25 = (f32[256,512]{1,0:T(8,128)S(1)}, f32[256,512]{1,0:T(8,128)}, u32[]{:S(2)}, u32[]{:S(2)}) collective-permute-start(f32[256,512]{1,0:T(8,128)S(1)} %pad_maximum_fusion.18), channel_id=1, source_target_pairs={{0,4},{2,6},{4,0},{6,2},{1,5},{3,7},{5,1},{7,3},{8,12},{10,14},{12... | collective-permute-start | bytes 1572872 | tf_op jit(solution)/shard_map/ppermute | solution.py:118
  306.6 151.0 %all-gather.9.cloned.1.call-start = ((), (), s32[]{:S(2)}) async-start(), calls=%async_computation.7 | async-start | bytes 5898240 | tf_op jit(solution)/shard_map/all_gather | solution.py:636
  307.2 39.1 %collective-permute-start.32 = (f32[352,1024]{1,0:T(8,128)}, f32[352,1024]{1,0:T(8,128)S(1)}, u32[]{:S(2)}, u32[]{:S(2)}) collective-permute-start(f32[352,1024]{1,0:T(8,128)} %pad_maximum_fusion.7), channel_id=1, source_target_pairs={{0,2},{2,0},{1,3},{3,1},{4,6},{6,4},{5,7},{7,5},{8,10},{10,8},{9,1... | collective-permute-start | bytes 4325384 | tf_op jit(solution)/shard_map/ppermute | solution.py:68
  383.0 224.8 %reduce-scatter.7.cloned.1.call-start = ((), (), s32[]{:S(2)}) async-start(), calls=%async_computation.8 | async-start | bytes 5898240 | tf_op jit(solution)/shard_map/reduce_scatter | solution.py:639
  421.3 43.3 %collective-permute-start.40 = (f32[176,1024]{1,0:T(8,128)}, f32[176,1024]{1,0:T(8,128)}, u32[]{:S(2)}, u32[]{:S(2)}) collective-permute-start(f32[176,1024]{1,0:T(8,128)} %collective-permute-done.36), channel_id=1, source_target_pairs={{0,2},{2,0},{1,3},{3,1},{4,6},{6,4},{5,7},{7,5},{8,10},{10,8},{9,1... | collective-permute-start | bytes 2162696 | tf_op jit(solution)/shard_map/ppermute | solution.py:68
  537.5 130.7 %all-gather.11.cloned.1.call-start = ((), (), s32[]{:S(2)}) async-start(), calls=%async_computation.9 | async-start | bytes 5898240 | tf_op jit(solution)/shard_map/all_gather | solution.py:636
  611.7 295.1 %reduce-scatter.9.cloned.1.call-start = ((), (), s32[]{:S(2)}) async-start(), calls=%async_computation.10 | async-start | bytes 5898240 | tf_op jit(solution)/shard_map/reduce_scatter | solution.py:639
  625.7 53.5 %collective-permute-start.46 = (f32[352,1024]{1,0:T(8,128)}, f32[352,1024]{1,0:T(8,128)}, u32[]{:S(2)}, u32[]{:S(2)}) collective-permute-start(f32[352,1024]{1,0:T(8,128)} %slice_add_fusion.2), channel_id=1, source_target_pairs={{0,4},{4,0},{1,5},{5,1},{2,6},{6,2},{3,7},{7,3},{8,12},{12,8},{9,1... | collective-permute-start | bytes 4325384 | tf_op jit(solution)/shard_map/ppermute | solution.py:68
  626.3 50.9 %collective-permute-start.47 = (f32[352,1024]{1,0:T(8,128)}, f32[352,1024]{1,0:T(8,128)}, u32[]{:S(2)}, u32[]{:S(2)}) collective-permute-start(f32[352,1024]{1,0:T(8,128)} %slice_add_fusion.3), channel_id=1, source_target_pairs={{0,2},{2,0},{1,3},{3,1},{4,6},{6,4},{5,7},{7,5},{8,10},{10,8},{9,1... | collective-permute-start | bytes 4325384 | tf_op jit(solution)/shard_map/ppermute | solution.py:68
  668.3 284.4 %reduce-scatter.11.cloned.1.call-start = ((), (), s32[]{:S(2)}) async-start(), calls=%async_computation.11 | async-start | bytes 5898240 | tf_op jit(solution)/shard_map/reduce_scatter | solution.py:639
  682.0 60.3 %collective-permute-start.56 = (f32[176,1024]{1,0:T(8,128)}, f32[176,1024]{1,0:T(8,128)}, u32[]{:S(2)}, u32[]{:S(2)}) collective-permute-start(f32[176,1024]{1,0:T(8,128)} %get-tuple-element.355), channel_id=1, source_target_pairs={{0,2},{2,0},{1,3},{3,1},{4,6},{6,4},{5,7},{7,5},{8,10},{10,8},{9,1... | collective-permute-start | bytes 2162696 | tf_op jit(solution)/shard_map/ppermute | solution.py:68
  683.5 60.3 %collective-permute-start.57 = (f32[176,1024]{1,0:T(8,128)}, f32[176,1024]{1,0:T(8,128)}, u32[]{:S(2)}, u32[]{:S(2)}) collective-permute-start(f32[176,1024]{1,0:T(8,128)} %get-tuple-element.356), channel_id=1, source_target_pairs={{0,2},{2,0},{1,3},{3,1},{4,6},{6,4},{5,7},{7,5},{8,10},{10,8},{9,1... | collective-permute-start | bytes 2162696 | tf_op jit(solution)/shard_map/ppermute | solution.py:68
  684.0 54.8 %collective-permute-start.54 = (f32[176,1024]{1,0:T(8,128)}, f32[176,1024]{1,0:T(8,128)}, u32[]{:S(2)}, u32[]{:S(2)}) collective-permute-start(f32[176,1024]{1,0:T(8,128)} %get-tuple-element.349), channel_id=1, source_target_pairs={{0,4},{4,0},{1,5},{5,1},{2,6},{6,2},{3,7},{7,3},{8,12},{12,8},{9,1... | collective-permute-start | bytes 2162696 | tf_op jit(solution)/shard_map/ppermute | solution.py:68
  685.5 56.7 %collective-permute-start.55 = (f32[176,1024]{1,0:T(8,128)}, f32[176,1024]{1,0:T(8,128)}, u32[]{:S(2)}, u32[]{:S(2)}) collective-permute-start(f32[176,1024]{1,0:T(8,128)} %get-tuple-element.350), channel_id=1, source_target_pairs={{0,4},{4,0},{1,5},{5,1},{2,6},{6,2},{3,7},{7,3},{8,12},{12,8},{9,1... | collective-permute-start | bytes 2162696 | tf_op jit(solution)/shard_map/ppermute | solution.py:68
  813.9 39.8 %collective-permute-start.72 = (f32[256,512]{1,0:T(8,128)}, f32[256,512]{1,0:T(8,128)S(1)}, u32[]{:S(2)}, u32[]{:S(2)}) collective-permute-start(f32[256,512]{1,0:T(8,128)} %get-tuple-element.559), channel_id=1, source_target_pairs={{0,4},{4,0},{1,5},{5,1},{2,6},{6,2},{3,7},{7,3},{8,12},{12,8},{9,1... | collective-permute-start | bytes 1572872 | tf_op jit(solution)/shard_map/ppermute | solution.py:68
  815.5 39.8 %collective-permute-start.73 = (f32[256,512]{1,0:T(8,128)}, f32[256,512]{1,0:T(8,128)S(1)}, u32[]{:S(2)}, u32[]{:S(2)}) collective-permute-start(f32[256,512]{1,0:T(8,128)} %get-tuple-element.558), channel_id=1, source_target_pairs={{0,4},{4,0},{1,5},{5,1},{2,6},{6,2},{3,7},{7,3},{8,12},{12,8},{9,1... | collective-permute-start | bytes 1572872 | tf_op jit(solution)/shard_map/ppermute | solution.py:68
  943.9 38.0 %collective-permute-start.94 = (f32[512,128]{1,0:T(8,128)}, f32[512,128]{1,0:T(8,128)}, u32[]{:S(2)}, u32[]{:S(2)}) collective-permute-start(f32[512,128]{1,0:T(8,128)} %get-tuple-element.644), channel_id=1, source_target_pairs={{0,8},{8,16},{16,24},{24,0},{1,9},{9,17},{17,25},{25,1},{2,10},{10... | collective-permute-start | bytes 786440 | tf_op jit(solution)/shard_map/ppermute | solution.py:68
  (198 other events, 2896.2 us)
Sparse Core Ops, SparseCore 0:
  70.9 71.4 all-gather.4
  144.1 87.7 all-gather.6
  306.7 73.5 reduce-scatter.4
  383.1 66.3 all-gather.8
  537.7 70.1 reduce-scatter.6
  611.9 56.3 all-gather.10
  670.6 58.6 reduce-scatter.8
  803.2 67.5 reduce-scatter.10

commit v4 on v3

--- a/solution.py
+++ b/solution.py
@@ -833,9 +833,8 @@
         up_out, up_side = square_out(up_w, "y", sizes), side_out(up_w, "y", sizes)
         down_pieces = dict(zip(places, take_all([down_on[p] for p in places]), strict=True))
         up_side = take_all(up_side)
-        gate_top, gate_low = halved(after(gate_w, *up_side))
-        top_out, low_out = square_out(gate_top, "x", sizes), square_out(gate_low, "y", sizes)
-        top_side, low_side = side_out(gate_top, "x", sizes), side_out(gate_low, "y", sizes)
+        gate_w = after(gate_w, *up_side)
+        gate_out, gate_side = square_out(gate_w, "x", sizes), side_out(gate_w, "x", sizes)
         branch = take(branch_sent)
         residual = from_distance_y(mine_attn + branch)
         ffn_scale = lax.rsqrt(jnp.mean(residual * residual, axis=1, keepdims=True) + epsilon)
@@ -843,14 +842,12 @@
         ffn_sent = group_gather(ffn_mine)
         wd = tiled_up(down_pieces)
         grad_hidden = then(fine(wd, cot, 1, 1))
-        top_out, low_side = take_all(top_out), take_all(low_side)
+        gate_out = take_all(gate_out)
         up_on = square_on(take_all(up_out), "y", sizes, up_side)
-        top_on = square_on(top_out, "x", sizes, top_side)
-        low_on = square_on(take_all(low_out), "y", sizes, low_side)
+        gate_on = square_on(gate_out, "x", sizes, gate_side)
         up_pieces = dict(zip(places, take_all([up_on[p] for p in places]), strict=True))
         ffn_plain = take(ffn_sent)
-        top_list = take_all([top_on[p] for p in places])
-        low_list = take_all([low_on[p] for p in places])
+        gate_list = take_all([gate_on[p] for p in places])
         wug = jnp.concatenate(
             [
                 jnp.concatenate([v[s, t] for s in range(xn)], axis=1)
@@ -860,7 +857,7 @@
             + [
                 jnp.concatenate([v[s, t] for s in range(xn)], axis=1)
                 for t in range(yn)
-                for v in (dict(zip(places, top_list, strict=True)), dict(zip(places, low_list, strict=True)))
+                for v in (dict(zip(places, gate_list, strict=True)),)
             ]
         )
 

time: 1020 us -> 1060 us (1.039)
  matrix products: 173 us -> 198 us
  waiting for transfers between devices: 368 us -> 393 us
  other arithmetic: 117 us -> 104 us
    dot_general x8, matrix products: 108 us -> 133 us  [fine(): lax.dot_general(a, b, (((contract_a,), (contract_b,)), ((), ())), precisi...]
    ppermute x98 -> x95, waiting for transfers between devices: 329 us -> 351 us  [shifted(): return lax.ppermute(v, axis, [(i, (i + shift) % n) for i in range(n)])]
    unnamed x8 -> x3, other arithmetic: 11.6 us -> 0.01 us
    ppermute x98 -> x95, starting transfers between devices: 160 us -> 159 us  [shifted(): return lax.ppermute(v, axis, [(i, (i + shift) % n) for i in range(n)])]
    unnamed x374 -> x368, local copies, waits for them, and re-layouts: 55.1 us -> 55.2 us
  transfers between devices with their start and end apart: 109 -> 106, of which waited for: 40 -> 42; matrix products, arithmetic and copies ran while one was open for 27% -> 25% of each run, Pallas kernels for 7% -> 7%
where the time goes in v4:
time: 1060 us; the launch traced here: 1050 us
  waiting for transfers between devices  393 us (37%)
  matrix products  198 us (19%)
  starting transfers between devices  165 us (16%)
  other arithmetic  104 us (10%)
  local copies, waits for them, and re-layouts  97.9 us (9%)
  Pallas kernels  72.2 us (7%)
  between operations  19.9 us (2%)
    ppermute x95, waiting for transfers between devices, shifted(): return lax.ppermute(v, axis, [(i, (i + shift) % n) for i in range(n)])  351 us
    ppermute x95, starting transfers between devices, shifted(): return lax.ppermute(v, axis, [(i, (i + shift) % n) for i in range(n)])  159 us
    dot_general x8, matrix products, fine(): lax.dot_general(a, b, (((contract_a,), (contract_b,)), ((), ())), precisi...  133 us
    dot_general x10, matrix products, dot(): lax.dot_general(a, b, (((contract_a,), (contract_b,)), ((), ())), precisi...  64.7 us
    unnamed x368, local copies, waits for them, and re-layouts  55.2 us
    pallas_call x1, Pallas kernels, attend_back(): pl.pallas_call(lambda *refs: backward_kernel(run, *refs), grid=(count //...  35.4 us
    all_gather x4, waiting for transfers between devices, group_gather(): return lax.all_gather(v, ('z', 'k'), axis=0, tiled=True)  29.6 us
    pallas_call x1, Pallas kernels, attend(): pl.pallas_call(lambda *refs: forward_kernel(run, *refs), grid=(count // T...  24.3 us
  transfers between devices with their start and end apart: 106, of which 42 were waited for; matrix products, arithmetic and copies ran while one was open for 25% of the time, Pallas kernels for 7%

profile of v4, /device:TPU:0, one launch (start us, length us, event | category | flops | bytes accessed | tf_op | source)
XLA Modules:
  0.0 1050.0 jit_solution(14048048375173092162)
XLA Ops:
  14.4 17.5 %collective-permute-done = f32[1536,128]{1,0:T(8,128)S(1)} collective-permute-done((f32[1536,128]{1,0:T(8,128)S(1)}, f32[1536,128]{1,0:T(8,128)S(1)}, u32[]{:S(2)}, u32[]{:S(2)}) %collective-permute-start) | collective-permute-done | bytes 786464 | tf_op jit(solution)/shard_map/ppermute | solution.py:68
  54.2 12.6 %tables.1 = (s32[50]{0:T(128)}, s32[5]{0:T(128)}, s32[160]{0:T(256)}, s32[40]{0:T(128)}, s32[800]{0:T(1024)}, /*index=5*/s32[40]{0:T(128)}) custom-call(s32[40]{0:T(128)} %refs_0_, s32[2]{0:T(128)} %pad_add_fusion.refs_1_), custom_call_target="tpu_custom_call" | custom-call | tf_op jit(solution)/shard_map/tables/pallas_call | solution.py:507
  76.1 15.8 %collective-permute-start.3 = (f32[1,192]{1,0:T(1,128)S(1)}, f32[1,192]{1,0:T(1,128)S(1)}, u32[]{:S(2)}, u32[]{:S(2)}) collective-permute-start(f32[1,192]{1,0:T(1,128)S(1)} %reshape.197), channel_id=1, source_target_pairs={{0,8},{8,16},{16,24},{24,0},{1,9},{9,17},{17,25},{25,1},{2,10},{10... | collective-permute-start | bytes 2312 | tf_op jit(solution)/shard_map/ppermute | solution.py:68
  93.1 14.0 %collective-permute-done.10 = f32[384,512]{1,0:T(8,128)} collective-permute-done((f32[384,512]{1,0:T(8,128)}, f32[384,512]{1,0:T(8,128)}, u32[]{:S(2)}, u32[]{:S(2)}) %collective-permute-start.10) | collective-permute-done | bytes 786464 | tf_op jit(solution)/shard_map/ppermute | solution.py:68
  107.1 9.2 collective-permute-start.4
  131.7 10.7 %all-gather.5.cloned.1.call-done = f32[640,2048]{1,0:T(8,128)} async-done(((f32[80,2048]{1,0:T(8,128)}), f32[640,2048]{1,0:T(8,128)}) %all-gather.5.cloned.1.call-update) | async-done | bytes 5242896 | tf_op jit(solution)/shard_map/all_gather | solution.py:636
  187.0 8.9 collective-permute-done.21
  196.5 31.1 %collective-permute-done.22 = f32[480,256]{1,0:T(8,128)} collective-permute-done((f32[480,256]{1,0:T(8,128)}, f32[480,256]{1,0:T(8,128)}, u32[]{:S(2)}, u32[]{:S(2)}) %collective-permute-start.22) | collective-permute-done | bytes 491552 | tf_op jit(solution)/shard_map/ppermute | solution.py:68
  236.9 11.1 %collective-permute-start.27 = (f32[704,256]{1,0:T(8,128)}, f32[704,256]{1,0:T(8,128)S(1)}, u32[]{:S(2)}, u32[]{:S(2)}) collective-permute-start(f32[704,256]{1,0:T(8,128)} %get-tuple-element.522), channel_id=1, source_target_pairs={{0,8},{8,16},{16,24},{24,0},{1,9},{9,17},{17,25},{25,1},{2,10},{10... | collective-permute-start | bytes 2162696 | tf_op jit(solution)/shard_map/ppermute | solution.py:68
  268.7 24.3 %attend.1 = (f32[640,256]{1,0:T(8,128)}, f32[8,640]{1,0:T(8,128)}) custom-call(f32[1]{0:T(128)} %bitcast.15.refs_0_, s32[2]{0:T(128)} %pad_add_fusion.refs_1_, s32[50]{0:T(128)} %get-tuple-element.225.refs_2_, s32[5]{0:T(128)} %get-tuple-element.226.refs_3_, s32[160]{0:T(256)} %get-tuple-element.227.refs_4_, s32[40]{0:T(128)} %get-tuple-element.228.refs_5_, ...), custom_call_target="tpu_custom_call" | custom-call | flops 40000000000 | tf_op jit(solution)/shard_map/attend/pallas_call | solution.py:521
  308.8 31.6 %collective-permute-done.30 = f32[352,1024]{1,0:T(8,128)S(1)} collective-permute-done((f32[352,1024]{1,0:T(8,128)}, f32[352,1024]{1,0:T(8,128)S(1)}, u32[]{:S(2)}, u32[]{:S(2)}) %collective-permute-start.30) | collective-permute-done | bytes 1441824 | tf_op jit(solution)/shard_map/ppermute | solution.py:68
  346.4 30.6 %collective-permute-done.33 = f32[352,1024]{1,0:T(8,128)S(1)} collective-permute-done((f32[352,1024]{1,0:T(8,128)S(1)}, f32[352,1024]{1,0:T(8,128)S(1)}, u32[]{:S(2)}, u32[]{:S(2)}) %collective-permute-start.33) | collective-permute-done | bytes 1441824 | tf_op jit(solution)/shard_map/ppermute | solution.py:68
  386.4 18.8 %fusion.11 = f32[704,640]{1,0:T(8,128)} fusion(f32[640,2048]{1,0:T(8,128)} %all-gather.7.cloned.1.call-done, f32[352,1024]{1,0:T(8,128)} %copy-done.109, f32[352,1024]{1,0:T(8,128)} %copy-done.107, f32[352,1024]{1,0:T(8,128)} %copy-done.105, f32[352,1024]{1,0:T(8,128)} %pad_maximum_fusion.7), kind=kOutput, calls=%fused_computation.15 | convolution fusion | flops 11077287936 | bytes 12812288 | tf_op jit(solution)/shard_map/dot_general | solution.py:37
  405.2 9.8 collective-permute-done.35
  419.8 27.6 %collective-permute-done.36 = f32[352,1024]{1,0:T(8,128)} collective-permute-done((f32[352,1024]{1,0:T(8,128)S(1)}, f32[352,1024]{1,0:T(8,128)}, u32[]{:S(2)}, u32[]{:S(2)}) %collective-permute-start.36) | collective-permute-done | bytes 1441824 | tf_op jit(solution)/shard_map/ppermute | solution.py:68
  452.6 26.2 %collective-permute-done.38 = f32[352,1024]{1,0:T(8,128)} collective-permute-done((f32[352,1024]{1,0:T(8,128)}, f32[352,1024]{1,0:T(8,128)}, u32[]{:S(2)}, u32[]{:S(2)}) %collective-permute-start.38) | collective-permute-done | bytes 1441824 | tf_op jit(solution)/shard_map/ppermute | solution.py:68
  478.8 51.8 %fusion.22 = f32[1408,640]{1,0:T(8,128)S(1)} fusion(f32[640,2048]{1,0:T(8,128)} %all-gather.9.cloned.1.call-done, f32[352,1024]{1,0:T(8,128)} %collective-permute-done.38, f32[352,1024]{1,0:T(8,128)} %collective-permute-done.37, f32[352,1024]{1,0:T(8,128)} %collective-permute-done.35, f32[352,1024]{1,0:T(8,128)} %get-tuple-element.314, ...), kind=kOutput, calls=%fused_computation.85 | convolution fusion | flops 22166110208 | bytes 20381696 | tf_op jit(solution)/shard_map/dot_general | solution.py:37
  536.1 33.3 %fusion.3 = f32[640,2048]{1,0:T(8,128)} fusion(f32[704,640]{1,0:T(8,128)S(1)} %get-tuple-element.320, f32[704,640]{1,0:T(8,128)S(1)} %get-tuple-element.319, f32[352,1024]{1,0:T(8,128)} %collective-permute-done.38, f32[352,1024]{1,0:T(8,128)} %collective-permute-done.37, f32[352,1024]{1,0:T(8,128)} %collective-permute-done.35, ...), kind=kOutput, calls=%fused_computation.9 | convolution fusion | flops 22167011328 | bytes 20381696 | tf_op jit(solution)/shard_map/dot_general | solution.py:37
  569.6 10.1 fusion.103
  584.5 7.0 fusion.104
  596.6 8.9 fusion.105
  605.5 11.7 %fusion.10 = f32[640,2048]{1,0:T(8,128)} fusion(f32[704,640]{1,0:T(8,128)S(1)} %copy-done.22, f32[352,1024]{1,0:T(8,128)S(1)} %copy-done.110, f32[352,1024]{1,0:T(8,128)S(1)} %copy-done.108, f32[352,1024]{1,0:T(8,128)S(1)} %copy-done.106, f32[352,1024]{1,0:T(8,128)} %pad_maximum_fusion.7), kind=kOutput, calls=%fused_computation.14 | convolution fusion | flops 5540806656 | bytes 12812288 | tf_op jit(solution)/shard_map/dot_general | solution.py:31
  630.6 10.1 reduce-scatter.7.cloned.1.call-done
  659.7 19.7 %collective-permute-done.41 = f32[352,1024]{1,0:T(8,128)} collective-permute-done((f32[352,1024]{1,0:T(8,128)}, f32[352,1024]{1,0:T(8,128)}, u32[]{:S(2)}, u32[]{:S(2)}) %collective-permute-start.41) | collective-permute-done | bytes 1441824 | tf_op jit(solution)/shard_map/ppermute | solution.py:68
  685.9 16.5 %all-gather.11.cloned.1.call-done = f32[640,2048]{1,0:T(8,128)} async-done(((f32[80,2048]{1,0:T(8,128)}), f32[640,2048]{1,0:T(8,128)}) %all-gather.11.cloned.1.call-update) | async-done | bytes 5242896 | tf_op jit(solution)/shard_map/all_gather | solution.py:636
  702.7 7.6 multiply_reduce_fusion.3
  720.2 35.4 %attend_back.1 = (f32[640,256]{1,0:T(8,128)}, f32[2560,256]{1,0:T(8,128)}, f32[2560,256]{1,0:T(8,128)}, f32[8,640]{1,0:T(8,128)}) custom-call(f32[1]{0:T(128)} %bitcast.15.refs_0_, s32[2]{0:T(128)} %pad_add_fusion.refs_1_, s32[50]{0:T(128)} %get-tuple-element.225.refs_2_, s32[5]{0:T(128)} %get-tuple-element.226.refs_3_, s32[160]{0:T(256)} %get-tuple-element.227.refs_4_, ...), custom_call_target="tpu_custom_call" | custom-call | flops 40000000000 | tf_op jit(solution)/shard_map/attend_back/pallas_call | solution.py:546
  788.1 10.9 %collective-permute-done.50 = f32[640,256]{1,0:T(8,128)} collective-permute-done((f32[640,256]{1,0:T(8,128)}, f32[640,256]{1,0:T(8,128)}, u32[]{:S(2)}, u32[]{:S(2)}) %collective-permute-start.50) | collective-permute-done | bytes 655392 | tf_op jit(solution)/shard_map/ppermute | solution.py:68
  859.9 25.4 %collective-permute-done.71 = f32[176,1024]{1,0:T(8,128)S(1)} collective-permute-done((f32[176,1024]{1,0:T(8,128)}, f32[176,1024]{1,0:T(8,128)S(1)}, u32[]{:S(2)}, u32[]{:S(2)}) %collective-permute-start.71) | collective-permute-done | bytes 720928 | tf_op jit(solution)/shard_map/ppermute | solution.py:68
  922.3 7.1 collective-permute-done.47
  960.0 12.9 %collective-permute-start.87 = (f32[512,128]{1,0:T(8,128)}, f32[512,128]{1,0:T(8,128)}, u32[]{:S(2)}, u32[]{:S(2)}) collective-permute-start(f32[512,128]{1,0:T(8,128)} %get-tuple-element.632), channel_id=1, source_target_pairs={{0,8},{8,16},{16,24},{24,0},{1,9},{9,17},{17,25},{25,1},{2,10},{10... | collective-permute-start | bytes 786440 | tf_op jit(solution)/shard_map/ppermute | solution.py:68
  1000.2 14.1 %collective-permute-done.86 = f32[80,2048]{1,0:T(8,128)S(1)} collective-permute-done((f32[80,2048]{1,0:T(8,128)S(1)}, f32[80,2048]{1,0:T(8,128)S(1)}, u32[]{:S(2)}, u32[]{:S(2)}) %collective-permute-start.86) | collective-permute-done | bytes 655392 | tf_op jit(solution)/shard_map/ppermute | solution.py:68
  (789 shorter events, 448.0 us)
Async XLA Ops:
  7.2 135.3 %all-gather.5.cloned.1.call-start = ((), (), s32[]{:S(2)}) async-start(), calls=%async_computation.4 | async-start | bytes 5898240 | tf_op jit(solution)/shard_map/all_gather | solution.py:636
  70.8 191.3 %all-gather.7.cloned.1.call-start = ((), (), s32[]{:S(2)}) async-start(), calls=%async_computation.5 | async-start | bytes 5898240 | tf_op jit(solution)/shard_map/all_gather | solution.py:636
  71.9 44.4 %collective-permute-start.9 = (f32[384,512]{1,0:T(8,128)S(1)}, f32[384,512]{1,0:T(8,128)S(1)}, u32[]{:S(2)}, u32[]{:S(2)}) collective-permute-start(f32[384,512]{1,0:T(8,128)S(1)} %get-tuple-element.250), channel_id=1, source_target_pairs={{0,2},{2,0},{1,3},{3,1},{4,6},{6,4},{5,7},{7,5},{8,10},{10,8},{9,1... | collective-permute-start | bytes 2359304 | tf_op jit(solution)/shard_map/ppermute | solution.py:68
  73.7 55.0 %collective-permute-start.11 = (f32[384,512]{1,0:T(8,128)S(1)}, f32[384,512]{1,0:T(8,128)S(1)}, u32[]{:S(2)}, u32[]{:S(2)}) collective-permute-start(f32[384,512]{1,0:T(8,128)S(1)} %get-tuple-element.250), channel_id=1, source_target_pairs={{0,4},{4,0},{1,5},{5,1},{2,6},{6,2},{3,7},{7,3},{8,12},{12,8},{9,1... | collective-permute-start | bytes 2359304 | tf_op jit(solution)/shard_map/ppermute | solution.py:68
  75.7 50.0 %collective-permute-start.13 = (f32[384,512]{1,0:T(8,128)}, f32[384,512]{1,0:T(8,128)}, u32[]{:S(2)}, u32[]{:S(2)}) collective-permute-start(f32[384,512]{1,0:T(8,128)} %get-tuple-element.246), channel_id=1, source_target_pairs={{0,2},{2,0},{1,3},{3,1},{4,6},{6,4},{5,7},{7,5},{8,10},{10,8},{9,1... | collective-permute-start | bytes 2359304 | tf_op jit(solution)/shard_map/ppermute | solution.py:68
  76.1 40.6 %collective-permute-start.3 = (f32[1,192]{1,0:T(1,128)S(1)}, f32[1,192]{1,0:T(1,128)S(1)}, u32[]{:S(2)}, u32[]{:S(2)}) collective-permute-start(f32[1,192]{1,0:T(1,128)S(1)} %reshape.197), channel_id=1, source_target_pairs={{0,8},{8,16},{16,24},{24,0},{1,9},{9,17},{17,25},{25,1},{2,10},{10... | collective-permute-start | bytes 2312 | tf_op jit(solution)/shard_map/ppermute | solution.py:68
  142.5 238.0 %reduce-scatter.5.cloned.1.call-start = ((), (), s32[]{:S(2)}) async-start(), calls=%async_computation.6 | async-start | bytes 5898240 | tf_op jit(solution)/shard_map/reduce_scatter | solution.py:639
  169.2 58.4 %collective-permute-start.22 = (f32[480,256]{1,0:T(8,128)}, f32[480,256]{1,0:T(8,128)}, u32[]{:S(2)}, u32[]{:S(2)}) collective-permute-start(f32[480,256]{1,0:T(8,128)} %get-tuple-element.553), channel_id=1, source_target_pairs={{0,16},{8,24},{16,0},{24,8},{1,17},{9,25},{17,1},{25,9},{2,18},{10... | collective-permute-start | bytes 1474568 | tf_op jit(solution)/shard_map/ppermute | solution.py:68
  170.8 58.0 %collective-permute-start.23 = (f32[480,256]{1,0:T(8,128)}, f32[480,256]{1,0:T(8,128)}, u32[]{:S(2)}, u32[]{:S(2)}) collective-permute-start(f32[480,256]{1,0:T(8,128)} %get-tuple-element.552), channel_id=1, source_target_pairs={{0,24},{8,0},{16,8},{24,16},{1,25},{9,1},{17,9},{25,17},{2,26},{10... | collective-permute-start | bytes 1474568 | tf_op jit(solution)/shard_map/ppermute | solution.py:68
  184.9 63.2 %collective-permute-start.19 = (f32[640,256]{1,0:T(8,128)}, f32[640,256]{1,0:T(8,128)S(1)}, u32[]{:S(2)}, u32[]{:S(2)}) collective-permute-start(f32[640,256]{1,0:T(8,128)} %fusion.23), channel_id=1, source_target_pairs={{0,2},{2,0},{1,3},{3,1},{4,6},{6,4},{5,7},{7,5},{8,10},{10,8},{9,1... | collective-permute-start | bytes 1966088 | tf_op jit(solution)/shard_map/ppermute | solution.py:68
  185.5 65.2 %collective-permute-start.20 = (f32[640,256]{1,0:T(8,128)}, f32[640,256]{1,0:T(8,128)S(1)}, u32[]{:S(2)}, u32[]{:S(2)}) collective-permute-start(f32[640,256]{1,0:T(8,128)} %collective-permute-done.16), channel_id=1, source_target_pairs={{0,2},{2,0},{1,3},{3,1},{4,6},{6,4},{5,7},{7,5},{8,10},{10,8},{9,1... | collective-permute-start | bytes 1966088 | tf_op jit(solution)/shard_map/ppermute | solution.py:68
  195.9 54.8 %collective-permute-start.17 = (f32[640,256]{1,0:T(8,128)}, f32[640,256]{1,0:T(8,128)S(1)}, u32[]{:S(2)}, u32[]{:S(2)}) collective-permute-start(f32[640,256]{1,0:T(8,128)} %fusion.19), channel_id=1, source_target_pairs={{0,4},{4,0},{1,5},{5,1},{2,6},{6,2},{3,7},{7,3},{8,12},{12,8},{9,1... | collective-permute-start | bytes 1966088 | tf_op jit(solution)/shard_map/ppermute | solution.py:68
  248.2 48.7 %collective-permute-start.28 = (f32[704,256]{1,0:T(8,128)}, f32[704,256]{1,0:T(8,128)S(1)}, u32[]{:S(2)}, u32[]{:S(2)}) collective-permute-start(f32[704,256]{1,0:T(8,128)} %get-tuple-element.521), channel_id=1, source_target_pairs={{0,16},{8,24},{16,0},{24,8},{1,17},{9,25},{17,1},{25,9},{2,18},{10... | collective-permute-start | bytes 2162696 | tf_op jit(solution)/shard_map/ppermute | solution.py:68
  250.7 46.2 %collective-permute-start.29 = (f32[704,256]{1,0:T(8,128)}, f32[704,256]{1,0:T(8,128)}, u32[]{:S(2)}, u32[]{:S(2)}) collective-permute-start(f32[704,256]{1,0:T(8,128)} %get-tuple-element.520), channel_id=1, source_target_pairs={{0,24},{8,0},{16,8},{24,16},{1,25},{9,1},{17,9},{25,17},{2,26},{10... | collective-permute-start | bytes 2162696 | tf_op jit(solution)/shard_map/ppermute | solution.py:68
  250.7 47.0 %collective-permute-start.24 = (f32[256,512]{1,0:T(8,128)S(1)}, f32[256,512]{1,0:T(8,128)S(1)}, u32[]{:S(2)}, u32[]{:S(2)}) collective-permute-start(f32[256,512]{1,0:T(8,128)S(1)} %pad_maximum_fusion.18), channel_id=1, source_target_pairs={{0,2},{2,0},{4,6},{6,4},{1,3},{3,1},{5,7},{7,5},{8,10},{10,8},{12,... | collective-permute-start | bytes 1572872 | tf_op jit(solution)/shard_map/ppermute | solution.py:118
  252.2 45.5 %collective-permute-start.25 = (f32[256,512]{1,0:T(8,128)S(1)}, f32[256,512]{1,0:T(8,128)}, u32[]{:S(2)}, u32[]{:S(2)}) collective-permute-start(f32[256,512]{1,0:T(8,128)S(1)} %pad_maximum_fusion.18), channel_id=1, source_target_pairs={{0,4},{2,6},{4,0},{6,2},{1,5},{3,7},{5,1},{7,3},{8,12},{10,14},{12... | collective-permute-start | bytes 1572872 | tf_op jit(solution)/shard_map/ppermute | solution.py:118
  306.6 143.1 %all-gather.9.cloned.1.call-start = ((), (), s32[]{:S(2)}) async-start(), calls=%async_computation.7 | async-start | bytes 5898240 | tf_op jit(solution)/shard_map/all_gather | solution.py:636
  307.3 39.0 %collective-permute-start.32 = (f32[352,1024]{1,0:T(8,128)}, f32[352,1024]{1,0:T(8,128)S(1)}, u32[]{:S(2)}, u32[]{:S(2)}) collective-permute-start(f32[352,1024]{1,0:T(8,128)} %pad_maximum_fusion.7), channel_id=1, source_target_pairs={{0,2},{2,0},{1,3},{3,1},{4,6},{6,4},{5,7},{7,5},{8,10},{10,8},{9,1... | collective-permute-start | bytes 4325384 | tf_op jit(solution)/shard_map/ppermute | solution.py:68
  383.2 257.5 %reduce-scatter.7.cloned.1.call-start = ((), (), s32[]{:S(2)}) async-start(), calls=%async_computation.8 | async-start | bytes 5898240 | tf_op jit(solution)/shard_map/reduce_scatter | solution.py:639
  419.2 59.6 %collective-permute-start.38 = (f32[352,1024]{1,0:T(8,128)}, f32[352,1024]{1,0:T(8,128)}, u32[]{:S(2)}, u32[]{:S(2)}) collective-permute-start(f32[352,1024]{1,0:T(8,128)} %collective-permute-done.35), channel_id=1, source_target_pairs={{0,2},{2,0},{1,3},{3,1},{4,6},{6,4},{5,7},{7,5},{8,10},{10,8},{9,1... | collective-permute-start | bytes 4325384 | tf_op jit(solution)/shard_map/ppermute | solution.py:68
  569.5 132.9 %all-gather.11.cloned.1.call-start = ((), (), s32[]{:S(2)}) async-start(), calls=%async_computation.9 | async-start | bytes 5898240 | tf_op jit(solution)/shard_map/all_gather | solution.py:636
  644.5 295.0 %reduce-scatter.9.cloned.1.call-start = ((), (), s32[]{:S(2)}) async-start(), calls=%async_computation.10 | async-start | bytes 5898240 | tf_op jit(solution)/shard_map/reduce_scatter | solution.py:639
  658.5 55.0 %collective-permute-start.43 = (f32[352,1024]{1,0:T(8,128)}, f32[352,1024]{1,0:T(8,128)}, u32[]{:S(2)}, u32[]{:S(2)}) collective-permute-start(f32[352,1024]{1,0:T(8,128)} %slice_add_fusion.2), channel_id=1, source_target_pairs={{0,4},{4,0},{1,5},{5,1},{2,6},{6,2},{3,7},{7,3},{8,12},{12,8},{9,1... | collective-permute-start | bytes 4325384 | tf_op jit(solution)/shard_map/ppermute | solution.py:68
  659.3 52.2 %collective-permute-start.44 = (f32[352,1024]{1,0:T(8,128)}, f32[352,1024]{1,0:T(8,128)}, u32[]{:S(2)}, u32[]{:S(2)}) collective-permute-start(f32[352,1024]{1,0:T(8,128)} %slice_add_fusion.3), channel_id=1, source_target_pairs={{0,2},{2,0},{1,3},{3,1},{4,6},{6,4},{5,7},{7,5},{8,10},{10,8},{9,1... | collective-permute-start | bytes 4325384 | tf_op jit(solution)/shard_map/ppermute | solution.py:68
  702.5 282.9 %reduce-scatter.11.cloned.1.call-start = ((), (), s32[]{:S(2)}) async-start(), calls=%async_computation.11 | async-start | bytes 5898240 | tf_op jit(solution)/shard_map/reduce_scatter | solution.py:639
  716.2 59.1 %collective-permute-start.53 = (f32[176,1024]{1,0:T(8,128)}, f32[176,1024]{1,0:T(8,128)}, u32[]{:S(2)}, u32[]{:S(2)}) collective-permute-start(f32[176,1024]{1,0:T(8,128)} %get-tuple-element.341), channel_id=1, source_target_pairs={{0,2},{2,0},{1,3},{3,1},{4,6},{6,4},{5,7},{7,5},{8,10},{10,8},{9,1... | collective-permute-start | bytes 2162696 | tf_op jit(solution)/shard_map/ppermute | solution.py:68
  717.7 59.2 %collective-permute-start.54 = (f32[176,1024]{1,0:T(8,128)}, f32[176,1024]{1,0:T(8,128)}, u32[]{:S(2)}, u32[]{:S(2)}) collective-permute-start(f32[176,1024]{1,0:T(8,128)} %get-tuple-element.342), channel_id=1, source_target_pairs={{0,2},{2,0},{1,3},{3,1},{4,6},{6,4},{5,7},{7,5},{8,10},{10,8},{9,1... | collective-permute-start | bytes 2162696 | tf_op jit(solution)/shard_map/ppermute | solution.py:68
  718.2 53.6 %collective-permute-start.51 = (f32[176,1024]{1,0:T(8,128)}, f32[176,1024]{1,0:T(8,128)}, u32[]{:S(2)}, u32[]{:S(2)}) collective-permute-start(f32[176,1024]{1,0:T(8,128)} %get-tuple-element.335), channel_id=1, source_target_pairs={{0,4},{4,0},{1,5},{5,1},{2,6},{6,2},{3,7},{7,3},{8,12},{12,8},{9,1... | collective-permute-start | bytes 2162696 | tf_op jit(solution)/shard_map/ppermute | solution.py:68
  719.7 55.5 %collective-permute-start.52 = (f32[176,1024]{1,0:T(8,128)}, f32[176,1024]{1,0:T(8,128)}, u32[]{:S(2)}, u32[]{:S(2)}) collective-permute-start(f32[176,1024]{1,0:T(8,128)} %get-tuple-element.336), channel_id=1, source_target_pairs={{0,4},{4,0},{1,5},{5,1},{2,6},{6,2},{3,7},{7,3},{8,12},{12,8},{9,1... | collective-permute-start | bytes 2162696 | tf_op jit(solution)/shard_map/ppermute | solution.py:68
  846.6 40.0 %collective-permute-start.69 = (f32[256,512]{1,0:T(8,128)}, f32[256,512]{1,0:T(8,128)S(1)}, u32[]{:S(2)}, u32[]{:S(2)}) collective-permute-start(f32[256,512]{1,0:T(8,128)} %get-tuple-element.545), channel_id=1, source_target_pairs={{0,4},{4,0},{1,5},{5,1},{2,6},{6,2},{3,7},{7,3},{8,12},{12,8},{9,1... | collective-permute-start | bytes 1572872 | tf_op jit(solution)/shard_map/ppermute | solution.py:68
  848.1 40.0 %collective-permute-start.70 = (f32[256,512]{1,0:T(8,128)}, f32[256,512]{1,0:T(8,128)S(1)}, u32[]{:S(2)}, u32[]{:S(2)}) collective-permute-start(f32[256,512]{1,0:T(8,128)} %get-tuple-element.544), channel_id=1, source_target_pairs={{0,4},{4,0},{1,5},{5,1},{2,6},{6,2},{3,7},{7,3},{8,12},{12,8},{9,1... | collective-permute-start | bytes 1572872 | tf_op jit(solution)/shard_map/ppermute | solution.py:68
  976.5 38.0 %collective-permute-start.91 = (f32[512,128]{1,0:T(8,128)}, f32[512,128]{1,0:T(8,128)}, u32[]{:S(2)}, u32[]{:S(2)}) collective-permute-start(f32[512,128]{1,0:T(8,128)} %get-tuple-element.628), channel_id=1, source_target_pairs={{0,8},{8,16},{16,24},{24,0},{1,9},{9,17},{17,25},{25,1},{2,10},{10... | collective-permute-start | bytes 786440 | tf_op jit(solution)/shard_map/ppermute | solution.py:68
  (192 other events, 2721.9 us)
Sparse Core Ops, SparseCore 0:
  70.9 71.4 all-gather.4
  144.1 87.8 all-gather.6
  306.7 73.7 reduce-scatter.4
  383.3 66.3 all-gather.8
  569.6 70.9 reduce-scatter.6
  644.6 57.7 all-gather.10
  704.7 58.6 reduce-scatter.8
  835.9 67.0 reduce-scatter.10
